TPU v7x, 128 devices: a whole 4x4x4 slice. The times are simulated.
128 devices in a mesh: row: 8 (over x, core), col: 16 (over y, z).
Axes of the slice: x: 4, y: 4, z: 4, core: 2. Of those that a mesh axis runs over, the one named last changes fastest.
Arguments:
- state: float32 [180, 131072], P(None, ('row', 'col')), may hold values from -6 to 6
- neighbours: int32 [4, 131072], P(None, ('row', 'col')), may hold values from 0 to 6143
- send_faces: int32 [4, 65536], P(None, ('row', 'col')), may hold values from 0 to 4095
- jacobian: float32 [131072], P(('row', 'col')), may hold values from 0.5 to 2
- face_extract: float32 [4, 90, 180], replicated, may hold values from -0.4375 to 0.4375
- volume_op: float32 [180, 180], replicated, may hold values from -0.4375 to 0.4375
- flux_matrix: float32 [90, 90], replicated, may hold values from -0.625 to 0.625
- lift_op: float32 [180, 4, 90], replicated, may hold values from -0.3125 to 0.3125
- sf_face: int32 [32768], P(('row', 'col')), may hold values from 0 to 4095
- sf_dest: int32 [32768, 1], P(('row', 'col')), may hold values from 0 to 127, as said below
- sf_row: int32 [32768], P(('row', 'col')), may hold values from 0 to 508
- sf_col: int32 [32768], P(('row', 'col')), may hold values from 0 to 508
- sf_weights: float32 [16, 10, 32768], P(None, None, ('row', 'col')), may hold values from 0 to 0.3
- ocean: float32 [3, 4096, 8192], P(None, 'row', 'col'), may hold values from -6 to 6
- depth: float32 [4096, 8192], P('row', 'col'), may hold values from 0.5 to 2
- wet: int32 [4096, 8192], P('row', 'col'), may hold values 0 or 1
Outputs:
- state_out: float32 [180, 131072], P(None, ('row', 'col'))
- ocean_out: float32 [3, 4096, 8192], P(None, 'row', 'col')
Inputs may be any that keep to these rules, and one draw needn't show every extreme that they name: `neighbours`: entries below 4096 name a face of the same partition; entry 4096 + j * 512 + k names the k-th trace received from neighbour j. `send_faces`: local face indices of the partition that holds the column. `sf_face`: local face index on the partition that holds the seafloor face. `sf_dest`: tile index r * 16 + c; each names the partition's own tile or one of the up to eight tiles beside it, diagonals included; among the seafloor faces of one partition the own tile is named exactly 64 times and no tile more than 64 times.
All inputs are finite; a program needn't handle non-finite values. No bound on the sum of `wet` on one device may be relied on, other than what follows from the above.
Results may differ from a plain program's by a relative error of at most 0.0001.
Values sent between devices are 32-bit elements; how exact they have to be, the bound alone decides.
No kernel may reach another device: no remote copies, remote signals or barrier semaphores. Data moves between devices by JAX's collectives and lax.ppermute only.
A program may use at most 128 MiB of HBM per device.

v0:
```python
import jax
import jax.numpy as jnp
from jax import lax
from jax.sharding import PartitionSpec as P

FNODES = 10
PATCH = 4
CAP = 64


HI = lax.Precision.HIGHEST


def extended(value, sides, width):
    for axis, dim in sides:
        count, length = (lax.axis_size(axis), value.shape[dim])
        up = [(i, (i + 1) % count) for i in range(count - 1)]
        down = [(j, i) for i, j in up]
        last = lax.slice_in_dim(value, length - width, length, axis=dim)
        initial = lax.slice_in_dim(value, 0, width, axis=dim)
        before = lax.ppermute(last, axis, up)
        after = lax.ppermute(initial, axis, down)
        value = jnp.concatenate([before, value, after], axis=dim)
    return value


def traces_of(face_extract, state):
    traces = jnp.einsum("fpk,ke->pfe", face_extract, state, precision=HI)
    return traces.reshape(traces.shape[0], -1)


def elastic_step(
    state, neighbours, send_faces, jacobian, face_extract, volume_op, flux_matrix, lift_op
):
    elems = state.shape[1]
    width = face_extract.shape[1]
    sending = send_faces.shape[1]
    pool = traces_of(face_extract, state)
    parts = jnp.take(pool, send_faces.reshape(-1), axis=1).reshape(width, 4, sending)
    padded = extended(parts[None, None], (("row", 0), ("col", 1)), 1)
    received = jnp.concatenate(
        [padded[0, 1][:, 1], padded[2, 1][:, 0], padded[1, 0][:, 3], padded[1, 2][:, 2]], axis=1
    )
    whole = jnp.concatenate([pool, received], axis=1)
    near = jnp.take(whole, neighbours.reshape(-1), axis=1)
    flux = jnp.dot(flux_matrix, pool - near, precision=HI).reshape(width, 4, elems)
    lifted = jnp.einsum("kfq,qfe->ke", lift_op, flux, precision=HI)
    inner = jnp.dot(volume_op, state, precision=HI)
    return state + 0.25 * jacobian * (inner + lifted)


def slot_positions(target_index, count):
    owners = (target_index[:, None] == jnp.arange(count, dtype=jnp.int32)[None, :]).astype(
        jnp.int32
    )
    ranks = jnp.cumsum(owners, axis=0) - owners
    slot = jnp.sum(ranks * owners, axis=1)
    return target_index * CAP + slot


def body(
    state,
    neighbours,
    send_faces,
    jacobian,
    face_extract,
    volume_op,
    flux_matrix,
    lift_op,
    sf_face,
    sf_dest,
    sf_row,
    sf_col,
    sf_weights,
    ocean,
    depth,
    wet,
):
    for step in range(2):
        state = elastic_step(
            state, neighbours, send_faces, jacobian, face_extract, volume_op, flux_matrix, lift_op
        )
    elems = state.shape[1]
    rows_tile = ocean.shape[1]
    cols_tile = ocean.shape[2]
    n_col = lax.axis_size("col")
    chosen = jnp.take(state, sf_face % elems, axis=1)
    face = sf_face // elems
    vz_ops = face_extract[:, 2 * FNODES : 3 * FNODES, :]
    all_faces = jnp.einsum("fpk,ks->fps", vz_ops, chosen, precision=HI)
    onehot = (face[None, :] == jnp.arange(4, dtype=jnp.int32)[:, None]).astype(jnp.float32)
    vz = jnp.sum(all_faces * onehot[:, None, :], axis=0)
    values = jnp.sum(sf_weights * vz[None], axis=1)
    dest = sf_dest[:, 0]
    patch_cells = values.shape[0]
    starts = sf_row * cols_tile + sf_col
    my_row = lax.axis_index("row")
    my_col = lax.axis_index("col")
    near_index = (dest // n_col - my_row + 1) * 3 + (dest % n_col - my_col + 1)
    position = slot_positions(near_index, 9)
    packed = jnp.concatenate([values.T, starts.astype(jnp.float32)[:, None]], axis=1)
    box = jnp.zeros((9 * CAP, patch_cells + 1), jnp.float32).at[position].set(packed)
    box = box.reshape(3, 3, CAP * (patch_cells + 1))
    framed = extended(box, (("row", 0), ("col", 1)), 1)
    pieces = [framed[i, j] for i in (0, 2, 4) for j in (0, 2, 4)]
    arrived = jnp.stack(pieces).reshape(9 * CAP, patch_cells + 1)
    got_values = arrived[:, :patch_cells]
    got_anchors = arrived[:, patch_cells].astype(jnp.int32)
    cell = jnp.arange(patch_cells, dtype=jnp.int32)
    offsets = cell // PATCH * cols_tile + cell % PATCH
    target = got_anchors[:, None] + offsets[None, :]
    uplift = (
        jnp.zeros((rows_tile * cols_tile,), jnp.float32)
        .at[target.reshape(-1)]
        .add(got_values.reshape(-1))
    )
    uplift = uplift.reshape(rows_tile, cols_tile)
    wet_f = wet.astype(jnp.float32)
    fields = ocean * wet_f[None]
    padded = extended(fields, (("row", 1), ("col", 2)), 1)
    north = padded[:, :-2, 1:-1]
    south = padded[:, 2:, 1:-1]
    west = padded[:, 1:-1, :-2]
    east = padded[:, 1:-1, 2:]
    avg = 0.25 * (north + south + west + east)
    height = avg[0] - 0.2 * (east[1] - west[1] + (south[2] - north[2])) + uplift
    speed_u = avg[1] - 0.2 * depth * (east[0] - west[0])
    speed_v = avg[2] - 0.2 * depth * (south[0] - north[0])
    ocean_out = jnp.stack([height, speed_u, speed_v]) * wet_f[None]
    return (state, ocean_out)


def solution(mesh):
    return jax.shard_map(
        body,
        mesh=mesh,
        in_specs=(
            P(None, ("row", "col")),
            P(None, ("row", "col")),
            P(None, ("row", "col")),
            P(("row", "col")),
            P(),
            P(),
            P(),
            P(),
            P(("row", "col")),
            P(("row", "col"), None),
            P(("row", "col")),
            P(("row", "col")),
            P(None, None, ("row", "col")),
            P(None, "row", "col"),
            P("row", "col"),
            P("row", "col"),
        ),
        out_specs=(P(None, ("row", "col")), P(None, "row", "col")),
        check_vma=False,
    )
```

profile of v0, /device:TPU:24, one launch (start us, length us, event | category | flops | bytes accessed | tf_op | source)
XLA Modules:
  0.0 399.9 jit_solution(8887862669945086240)
XLA Ops:
  3.4 3.8 convolution_bitcast_fusion.3
  7.2 1.9 copy.123
  9.0 7.7 %gather_fusion.1 = f32[2048,90]{1,0:T(8,128)} fusion(f32[90,4096]{0,1:T(8,128)S(1)} %bitcast.167, s32[2048]{0:T(1024)S(1)} %fusion.71), kind=kCustom, calls=%fused_computation.clone | custom fusion | bytes 1482752 | tf_op jit(solution)/shard_map/jit(_take)/gather | solution.py:39
  19.5 2.6 collective-permute-start
  24.8 2.8 broadcast_multiply_fusion
  29.5 4.0 %collective-permute-start.8 = (f32[3,1,512]{2,1,0:T(1,128)}, f32[3,1,512]{2,1,0:T(1,128)S(1)}, u32[]{:S(2)}, u32[]{:S(2)}) collective-permute-start(f32[3,1,512]{2,1,0:T(1,128)} %get-tuple-element.15), channel_id=1, source_target_pairs={{0,16},{16,32},{32,48},{48,64},{64,80},{80,96},{96,112},{1,17},{17... | collective-permute-start | bytes 18440 | tf_op jit(solution)/shard_map/ppermute | solution.py:21
  38.9 3.5 pad_maximum_fusion.1
  42.4 3.8 collective-permute-start.2
  46.2 4.4 %collective-permute-start.3 = (f32[3,1,90,4,512]{4,3,2,1,0:T(4,128)}, f32[3,1,90,4,512]{4,3,2,1,0:T(4,128)}, u32[]{:S(2)}, u32[]{:S(2)}) collective-permute-start(f32[3,1,90,4,512]{4,3,2,1,0:T(4,128)} %pad_maximum_fusion.1), channel_id=1, source_target_pairs={{1,0},{2,1},{3,2},{4,3},{5,4},{6,5},{7,6},{8,7},{9,8},{10,9},{11,1... | collective-permute-start | bytes 6635528 | tf_op jit(solution)/shard_map/ppermute | solution.py:22
  57.7 2.4 copy.88
  60.2 2.4 copy.90
  66.0 30.7 %collective-permute-done.2 = f32[3,1,90,4,512]{4,3,2,1,0:T(4,128)} collective-permute-done((f32[3,1,90,4,512]{4,3,2,1,0:T(4,128)}, f32[3,1,90,4,512]{4,3,2,1,0:T(4,128)}, u32[]{:S(2)}, u32[]{:S(2)}) %collective-permute-start.2) | collective-permute-done | bytes 2211872 | tf_op jit(solution)/shard_map/ppermute | solution.py:21
  96.7 2.0 slice.228
  98.7 2.5 copy.127
  101.2 2.0 slice.230
  103.2 2.5 copy.128
  109.0 16.1 %gather_fusion.2 = f32[4096,90]{1,0:T(8,128)} fusion(f32[90,6144]{0,1:T(8,128)} %fusion.56, s32[4096]{0:T(1024)S(1)} %fusion.70), kind=kCustom, calls=%fused_computation.1.clone | custom fusion | bytes 2965504 | tf_op jit(solution)/shard_map/jit(_take)/gather | solution.py:45
  125.1 5.8 %convolution_bitcast_fusion.1 = f32[90,4096]{1,0:T(8,128)} fusion(f32[90,90]{1,0:T(8,128)} %param.26, f32[90,4096]{0,1:T(8,128)} %bitcast.168, f32[4096,90]{1,0:T(8,128)} %gather_fusion.2, pred[4096]{0:T(1024)(128)(4,1)} %compare_and_fusion), kind=kOutput, calls=%fused_computation.8 | convolution fusion | flops 398868480 | bytes 4460176 | tf_op jit(solution)/shard_map/dot_general | solution.py:46
  130.9 3.1 reshape.149
  133.9 3.8 fusion.17
  137.8 1.8 fusion.13
  140.4 2.7 convolution_bitcast_fusion.2
  143.1 2.8 copy.125
  145.9 9.2 %gather_fusion.3 = f32[2048,90]{1,0:T(8,128)} fusion(f32[90,4096]{0,1:T(8,128)} %bitcast.170, s32[2048]{0:T(1024)S(1)} %fusion.71), kind=kCustom, calls=%fused_computation.2.clone | custom fusion | bytes 1482752 | tf_op jit(solution)/shard_map/jit(_take)/gather | solution.py:39
  155.1 2.5 broadcast_select_fusion
  157.6 2.5 copy.101
  160.2 3.7 collective-permute-start.4
  169.3 1.9 collective-permute-start.10
  171.2 2.1 copy.114
  173.3 6.0 %collective-permute-start.11 = (f32[3,514,1]{1,0,2:T(4,128)}, f32[3,514,1]{1,0,2:T(4,128)}, u32[]{:S(2)}, u32[]{:S(2)}) collective-permute-start(f32[3,514,1]{1,0,2:T(4,128)} %copy.114), channel_id=1, source_target_pairs={{1,0},{2,1},{3,2},{4,3},{5,4},{6,5},{7,6},{8,7},{9,8},{10,9},{11,1... | collective-permute-start | bytes 18512 | tf_op jit(solution)/shard_map/ppermute | solution.py:22
  179.9 1.9 copy.113
  181.8 1.9 copy.115
  183.7 3.6 pad_maximum_fusion.2
  187.3 1.9 collective-permute-start.6
  189.2 6.3 %collective-permute-start.7 = (f32[3,1,90,4,512]{4,3,2,1,0:T(4,128)}, f32[3,1,90,4,512]{4,3,2,1,0:T(4,128)}, u32[]{:S(2)}, u32[]{:S(2)}) collective-permute-start(f32[3,1,90,4,512]{4,3,2,1,0:T(4,128)} %pad_maximum_fusion.2), channel_id=1, source_target_pairs={{1,0},{2,1},{3,2},{4,3},{5,4},{6,5},{7,6},{8,7},{9,8},{10,9},{11,1... | collective-permute-start | bytes 6635528 | tf_op jit(solution)/shard_map/ppermute | solution.py:22
  195.5 3.2 maximum_maximum_fusion
  198.7 2.5 fusion.4
  201.3 2.2 fusion.40
  205.9 2.5 copy.102
  208.4 2.5 copy.104
  214.2 28.1 %collective-permute-done.6 = f32[3,1,90,4,512]{4,3,2,1,0:T(4,128)} collective-permute-done((f32[3,1,90,4,512]{4,3,2,1,0:T(4,128)}, f32[3,1,90,4,512]{4,3,2,1,0:T(4,128)}, u32[]{:S(2)}, u32[]{:S(2)}) %collective-permute-start.6) | collective-permute-done | bytes 2211872 | tf_op jit(solution)/shard_map/ppermute | solution.py:21
  242.3 2.0 slice.234
  244.3 2.5 copy.129
  246.8 2.0 slice.236
  248.9 2.5 copy.130
  254.7 16.1 %gather_fusion.4 = f32[4096,90]{1,0:T(8,128)} fusion(f32[90,6144]{0,1:T(8,128)} %fusion.52, s32[4096]{0:T(1024)S(1)} %fusion.70), kind=kCustom, calls=%fused_computation.3.clone | custom fusion | bytes 2965504 | tf_op jit(solution)/shard_map/jit(_take)/gather | solution.py:45
  270.8 5.2 %convolution_bitcast_fusion = f32[90,4096]{1,0:T(8,128)} fusion(f32[90,90]{1,0:T(8,128)} %param.26, f32[90,4096]{0,1:T(8,128)} %bitcast.171, f32[4096,90]{1,0:T(8,128)} %gather_fusion.4, pred[4096]{0:T(1024)(128)(4,1)S(1)} %copy-done.22), kind=kOutput, calls=%fused_computation.7 | convolution fusion | flops 398868480 | bytes 4460176 | tf_op jit(solution)/shard_map/dot_general | solution.py:46
  276.0 3.1 reshape.151
  279.1 3.8 fusion.20
  282.9 2.7 fusion.16
  285.6 2.4 copy.117
  288.0 3.0 gather_fusion
  294.7 2.2 scatter_custom_fusion
  298.6 1.8 reshape.153
  302.1 2.0 collective-permute-start.12
  310.9 1.9 collective-permute-start.14
  312.8 6.0 %collective-permute-start.15 = (f32[5,1,1088]{2,1,0:T(1,128)S(1)}, f32[5,1,1088]{2,1,0:T(1,128)S(1)}, u32[]{:S(2)}, u32[]{:S(2)}) collective-permute-start(f32[5,1,1088]{2,1,0:T(1,128)S(1)} %get-tuple-element.18), channel_id=1, source_target_pairs={{1,0},{2,1},{3,2},{4,3},{5,4},{6,5},{7,6},{8,7},{9,8},{10,9},{11,1... | collective-permute-start | bytes 65288 | tf_op jit(solution)/shard_map/ppermute | solution.py:22
  320.9 2.7 stack.13
  323.6 1.9 reshape.154
  328.2 1.7 add.180
  333.1 59.5 %scatter_custom_fusion.1 = f32[262144]{0:T(1024)} fusion(s32[9216]{0:T(1024)} %bitcast.191, f32[9216]{0:T(1024)} %reshape.209, f32[]{:T(128)} %constant.124.clone.1), kind=kCustom, calls=%fused_computation.82 | custom fusion | flops 9216 | bytes 1049088 | tf_op jit(solution)/shard_map/scatter-add | solution.py:115
  392.6 2.3 reshape.156
  395.0 2.6 fusion.30
  397.6 2.3 maximum_multiply_fusion
  (139 shorter events, 66.8 us)
Async XLA Ops:
  0.6 133.3 %copy-start = (f32[180,4,90]{2,1,0:T(4,128)S(1)}, f32[180,4,90]{2,1,0:T(4,128)}, u32[]{:S(2)}) copy-start(f32[180,4,90]{2,1,0:T(4,128)} %param.27) | copy-start | bytes 777604
  1.4 15.3 %copy-start.23 = (pred[2048]{0:T(1024)(128)(4,1)}, pred[2048]{0:T(1024)(128)(4,1)S(1)}, u32[]{:S(2)}) copy-start(pred[2048]{0:T(1024)(128)(4,1)S(1)} %compare_and_fusion.1) | copy-start | bytes 6148
  2.6 0.8 copy-start.13
  9.0 7.7 %copy-start.1 = (f32[90,4,1024]{0,2,1:T(8,128)}, f32[90,4,1024]{0,2,1:T(8,128)S(1)}, u32[]{:S(2)}) copy-start(f32[90,4,1024]{0,2,1:T(8,128)S(1)} %copy.123) | copy-start | bytes 4423684
  19.5 19.4 %collective-permute-start = (f32[1,1,90,4,512]{4,3,2,1,0:T(4,128)}, f32[1,1,90,4,512]{4,3,2,1,0:T(4,128)}, u32[]{:S(2)}, u32[]{:S(2)}) collective-permute-start(f32[1,1,90,4,512]{4,3,2,1,0:T(4,128)} %copy.87), channel_id=1, source_target_pairs={{0,16},{16,32},{32,48},{48,64},{64,80},{80,96},{96,112},{1,17},{17... | collective-permute-start | bytes 2211848 | tf_op jit(solution)/shard_map/ppermute | solution.py:21
  22.2 16.7 %collective-permute-start.1 = (f32[1,1,90,4,512]{4,3,2,1,0:T(4,128)}, f32[1,1,90,4,512]{4,3,2,1,0:T(4,128)}, u32[]{:S(2)}, u32[]{:S(2)}) collective-permute-start(f32[1,1,90,4,512]{4,3,2,1,0:T(4,128)} %copy.87), channel_id=1, source_target_pairs={{16,0},{32,16},{48,32},{64,48},{80,64},{96,80},{112,96},{17,1},{33... | collective-permute-start | bytes 2211848 | tf_op jit(solution)/shard_map/ppermute | solution.py:22
  24.8 2.8 copy-start.7
  24.8 8.7 %copy-start.27 = (s32[256,1]{0,1:T(1,128)S(1)}, s32[256,1]{0,1:T(1,128)}, u32[]{:S(2)}) copy-start(s32[256,1]{0,1:T(1,128)} %param.29) | copy-start | bytes 3076
  28.2 138.2 %collective-permute-start.9 = (f32[3,1,512]{2,1,0:T(1,128)}, f32[3,1,512]{2,1,0:T(1,128)S(1)}, u32[]{:S(2)}, u32[]{:S(2)}) collective-permute-start(f32[3,1,512]{2,1,0:T(1,128)} %get-tuple-element.14), channel_id=1, source_target_pairs={{16,0},{32,16},{48,32},{64,48},{80,64},{96,80},{112,96},{17,1},{33... | collective-permute-start | bytes 18440 | tf_op jit(solution)/shard_map/ppermute | solution.py:22
  29.5 136.9 %collective-permute-start.8 = (f32[3,1,512]{2,1,0:T(1,128)}, f32[3,1,512]{2,1,0:T(1,128)S(1)}, u32[]{:S(2)}, u32[]{:S(2)}) collective-permute-start(f32[3,1,512]{2,1,0:T(1,128)} %get-tuple-element.15), channel_id=1, source_target_pairs={{0,16},{16,32},{32,48},{48,64},{64,80},{80,96},{96,112},{1,17},{17... | collective-permute-start | bytes 18440 | tf_op jit(solution)/shard_map/ppermute | solution.py:21
  33.6 0.5 copy-start.24
  38.0 13.9 %copy-start.25 = (s32[256,1]{0,1:T(1,128)S(1)}, s32[256,1]{0,1:T(1,128)}, u32[]{:S(2)}) copy-start(s32[256,1]{0,1:T(1,128)} %copy-done.24) | copy-start | bytes 3076
  38.0 17.7 %copy-start.21 = (s32[4,1024]{1,0:T(4,128)S(1)}, s32[4,1024]{1,0:T(4,128)}, u32[]{:S(2)}) copy-start(s32[4,1024]{1,0:T(4,128)} %param.21) | copy-start | bytes 49156
  38.0 18.3 %copy-start.2 = (f32[90,4,1024]{0,2,1:T(8,128)S(1)}, f32[90,4,1024]{0,2,1:T(8,128)}, u32[]{:S(2)}) copy-start(f32[90,4,1024]{0,2,1:T(8,128)} %copy-done.1) | copy-start | bytes 4423684
  42.4 54.3 %collective-permute-start.2 = (f32[3,1,90,4,512]{4,3,2,1,0:T(4,128)}, f32[3,1,90,4,512]{4,3,2,1,0:T(4,128)}, u32[]{:S(2)}, u32[]{:S(2)}) collective-permute-start(f32[3,1,90,4,512]{4,3,2,1,0:T(4,128)} %pad_maximum_fusion.1), channel_id=1, source_target_pairs={{0,1},{1,2},{2,3},{3,4},{4,5},{5,6},{6,7},{7,8},{8,9},{9,10},{10,1... | collective-permute-start | bytes 6635528 | tf_op jit(solution)/shard_map/ppermute | solution.py:21
  46.2 55.0 %collective-permute-start.3 = (f32[3,1,90,4,512]{4,3,2,1,0:T(4,128)}, f32[3,1,90,4,512]{4,3,2,1,0:T(4,128)}, u32[]{:S(2)}, u32[]{:S(2)}) collective-permute-start(f32[3,1,90,4,512]{4,3,2,1,0:T(4,128)} %pad_maximum_fusion.1), channel_id=1, source_target_pairs={{1,0},{2,1},{3,2},{4,3},{5,4},{6,5},{7,6},{8,7},{9,8},{10,9},{11,1... | collective-permute-start | bytes 6635528 | tf_op jit(solution)/shard_map/ppermute | solution.py:22
  133.9 3.8 copy-start.15
  133.9 6.5 %copy-start.14 = (f32[4,90,180]{1,2,0:T(8,128)S(1)}, f32[4,90,180]{1,2,0:T(8,128)}, u32[]{:S(2)}) copy-start(f32[4,90,180]{1,2,0:T(8,128)} %copy-done.13) | copy-start | bytes 777604
  139.5 0.9 copy-start.9
  155.1 10.0 %copy-start.28 = (s32[256]{0:T(256)S(1)}, s32[256]{0:T(256)}, u32[]{:S(2)}) copy-start(s32[256]{0:T(256)} %param.28) | copy-start | bytes 3076
  155.1 10.7 %copy-start.26 = (s32[256]{0:T(256)S(1)}, s32[256]{0:T(256)}, u32[]{:S(2)}) copy-start(s32[256]{0:T(256)} %get-tuple-element.7) | copy-start | bytes 3076
  160.2 23.5 %collective-permute-start.4 = (f32[1,1,90,4,512]{4,3,2,1,0:T(4,128)}, f32[1,1,90,4,512]{4,3,2,1,0:T(4,128)}, u32[]{:S(2)}, u32[]{:S(2)}) collective-permute-start(f32[1,1,90,4,512]{4,3,2,1,0:T(4,128)} %copy.101), channel_id=1, source_target_pairs={{0,16},{16,32},{32,48},{48,64},{64,80},{80,96},{96,112},{1,17},{17... | collective-permute-start | bytes 2211848 | tf_op jit(solution)/shard_map/ppermute | solution.py:21
  163.8 19.9 %collective-permute-start.5 = (f32[1,1,90,4,512]{4,3,2,1,0:T(4,128)}, f32[1,1,90,4,512]{4,3,2,1,0:T(4,128)}, u32[]{:S(2)}, u32[]{:S(2)}) collective-permute-start(f32[1,1,90,4,512]{4,3,2,1,0:T(4,128)} %copy.101), channel_id=1, source_target_pairs={{16,0},{32,16},{48,32},{64,48},{80,64},{96,80},{112,96},{17,1},{33... | collective-permute-start | bytes 2211848 | tf_op jit(solution)/shard_map/ppermute | solution.py:22
  166.4 34.9 %copy-start.17 = (f32[3,1,512]{2,1,0:T(1,128)}, f32[3,1,512]{2,1,0:T(1,128)S(1)}, u32[]{:S(2)}) copy-start(f32[3,1,512]{2,1,0:T(1,128)S(1)} %collective-permute-done.9) | copy-start | bytes 18436
  166.4 34.9 %copy-start.19 = (f32[3,1,512]{2,1,0:T(1,128)}, f32[3,1,512]{2,1,0:T(1,128)S(1)}, u32[]{:S(2)}) copy-start(f32[3,1,512]{2,1,0:T(1,128)S(1)} %collective-permute-done.8) | copy-start | bytes 18436
  169.3 10.7 %collective-permute-start.10 = (f32[3,514,1]{1,2,0:T(1,128)S(1)}, f32[3,514,1]{1,2,0:T(1,128)}, u32[]{:S(2)}, u32[]{:S(2)}) collective-permute-start(f32[3,514,1]{1,2,0:T(1,128)S(1)} %copy.112), channel_id=1, source_target_pairs={{0,1},{1,2},{2,3},{3,4},{4,5},{5,6},{6,7},{7,8},{8,9},{9,10},{10,1... | collective-permute-start | bytes 18512 | tf_op jit(solution)/shard_map/ppermute | solution.py:21
  173.3 8.5 %collective-permute-start.11 = (f32[3,514,1]{1,0,2:T(4,128)}, f32[3,514,1]{1,0,2:T(4,128)}, u32[]{:S(2)}, u32[]{:S(2)}) collective-permute-start(f32[3,514,1]{1,0,2:T(4,128)} %copy.114), channel_id=1, source_target_pairs={{1,0},{2,1},{3,2},{4,3},{5,4},{6,5},{7,6},{8,7},{9,8},{10,9},{11,1... | collective-permute-start | bytes 18512 | tf_op jit(solution)/shard_map/ppermute | solution.py:22
  183.7 11.8 %copy-start.4 = (f32[3,514,1]{2,1,0:T(8,128)S(1)}, f32[3,514,1]{2,1,0:T(8,128)}, u32[]{:S(2)}) copy-start(f32[3,514,1]{2,1,0:T(8,128)} %copy.113) | copy-start | bytes 18508
  183.7 11.8 %copy-start.5 = (f32[3,514,1]{2,1,0:T(8,128)S(1)}, f32[3,514,1]{2,1,0:T(8,128)}, u32[]{:S(2)}) copy-start(f32[3,514,1]{2,1,0:T(8,128)} %copy.115) | copy-start | bytes 18508
  187.3 55.0 %collective-permute-start.6 = (f32[3,1,90,4,512]{4,3,2,1,0:T(4,128)}, f32[3,1,90,4,512]{4,3,2,1,0:T(4,128)}, u32[]{:S(2)}, u32[]{:S(2)}) collective-permute-start(f32[3,1,90,4,512]{4,3,2,1,0:T(4,128)} %pad_maximum_fusion.2), channel_id=1, source_target_pairs={{0,1},{1,2},{2,3},{3,4},{4,5},{5,6},{6,7},{7,8},{8,9},{9,10},{10,1... | collective-permute-start | bytes 6635528 | tf_op jit(solution)/shard_map/ppermute | solution.py:21
  189.2 57.6 %collective-permute-start.7 = (f32[3,1,90,4,512]{4,3,2,1,0:T(4,128)}, f32[3,1,90,4,512]{4,3,2,1,0:T(4,128)}, u32[]{:S(2)}, u32[]{:S(2)}) collective-permute-start(f32[3,1,90,4,512]{4,3,2,1,0:T(4,128)} %pad_maximum_fusion.2), channel_id=1, source_target_pairs={{1,0},{2,1},{3,2},{4,3},{5,4},{6,5},{7,6},{8,7},{9,8},{10,9},{11,1... | collective-permute-start | bytes 6635528 | tf_op jit(solution)/shard_map/ppermute | solution.py:22
  198.7 2.6 copy-start.16
  201.3 2.5 copy-start.6
  201.3 3.1 copy-start.3
  254.7 16.1 %copy-start.22 = (pred[4096]{0:T(1024)(128)(4,1)S(1)}, pred[4096]{0:T(1024)(128)(4,1)}, u32[]{:S(2)}) copy-start(pred[4096]{0:T(1024)(128)(4,1)} %compare_and_fusion) | copy-start | bytes 12292
  279.1 3.8 copy-start.10
  282.9 8.1 %slice-start = ((f32[4,90,180]{2,0,1:T(4,128)}), f32[4,10,180]{2,0,1:T(4,128)S(1)}, s32[]{:S(2)}) async-start(f32[4,90,180]{2,0,1:T(4,128)} %param.24), calls=%async_computation | async-start | bytes 81920 | tf_op jit(solution)/shard_map/slice | solution.py:89
  296.9 98.0 %copy-start.18 = (f32[3,1,512]{2,1,0:T(1,128)S(1)}, f32[3,1,512]{2,1,0:T(1,128)}, u32[]{:S(2)}) copy-start(f32[3,1,512]{2,1,0:T(1,128)} %copy-done.17) | copy-start | bytes 18436
  296.9 98.0 %copy-start.20 = (f32[3,1,512]{2,1,0:T(1,128)S(1)}, f32[3,1,512]{2,1,0:T(1,128)}, u32[]{:S(2)}) copy-start(f32[3,1,512]{2,1,0:T(1,128)} %copy-done.19) | copy-start | bytes 18436
  302.1 6.3 %collective-permute-start.12 = (f32[1,3,1088]{2,1,0:T(4,128)}, f32[1,3,1088]{2,1,0:T(4,128)S(1)}, u32[]{:S(2)}, u32[]{:S(2)}) collective-permute-start(f32[1,3,1088]{2,1,0:T(4,128)} %slice.194), channel_id=1, source_target_pairs={{0,16},{16,32},{32,48},{48,64},{64,80},{80,96},{96,112},{1,17},{17... | collective-permute-start | bytes 39176 | tf_op jit(solution)/shard_map/ppermute | solution.py:21
  305.7 5.1 %collective-permute-start.13 = (f32[1,3,1088]{2,1,0:T(4,128)}, f32[1,3,1088]{2,1,0:T(4,128)S(1)}, u32[]{:S(2)}, u32[]{:S(2)}) collective-permute-start(f32[1,3,1088]{2,1,0:T(4,128)} %slice.196), channel_id=1, source_target_pairs={{16,0},{32,16},{48,32},{64,48},{80,64},{96,80},{112,96},{17,1},{33... | collective-permute-start | bytes 39176 | tf_op jit(solution)/shard_map/ppermute | solution.py:22
  310.9 9.2 %collective-permute-start.14 = (f32[5,1,1088]{2,1,0:T(1,128)S(1)}, f32[5,1,1088]{2,1,0:T(1,128)S(1)}, u32[]{:S(2)}, u32[]{:S(2)}) collective-permute-start(f32[5,1,1088]{2,1,0:T(1,128)S(1)} %get-tuple-element.19), channel_id=1, source_target_pairs={{0,1},{1,2},{2,3},{3,4},{4,5},{5,6},{6,7},{7,8},{8,9},{9,10},{10,1... | collective-permute-start | bytes 65288 | tf_op jit(solution)/shard_map/ppermute | solution.py:21
  312.8 7.5 %collective-permute-start.15 = (f32[5,1,1088]{2,1,0:T(1,128)S(1)}, f32[5,1,1088]{2,1,0:T(1,128)S(1)}, u32[]{:S(2)}, u32[]{:S(2)}) collective-permute-start(f32[5,1,1088]{2,1,0:T(1,128)S(1)} %get-tuple-element.18), channel_id=1, source_target_pairs={{1,0},{2,1},{3,2},{4,3},{5,4},{6,5},{7,6},{8,7},{9,8},{10,9},{11,1... | collective-permute-start | bytes 65288 | tf_op jit(solution)/shard_map/ppermute | solution.py:22
  394.9 2.7 copy-start.8
  394.9 2.7 copy-start.11
  394.9 2.7 copy-start.12
where the time goes:
time: 405 us; the launch traced here: 400 us
  local copies, waits for them, and re-layouts  152 us (38%)
  other arithmetic  105 us (26%)
  waiting for transfers between devices  60.8 us (15%)
  starting transfers between devices  49.8 us (12%)
  matrix products  30.8 us (8%)
    scatter-add x1, other arithmetic, body(): uplift = jnp.zeros((rows_tile * cols_tile,), jnp.float32).at[target.resha...  59.5 us
    ppermute x8, waiting for transfers between devices, extended(): before = lax.ppermute(last, axis, up)  58.9 us
    gather x2, local copies, waits for them, and re-layouts, elastic_step(): near = jnp.take(whole, neighbours.reshape(-1), axis=1)  32.2 us
    unnamed x76, local copies, waits for them, and re-layouts  28.8 us
    ppermute x8, starting transfers between devices, extended(): after = lax.ppermute(initial, axis, down)  27.8 us
    ppermute x8, starting transfers between devices, extended(): before = lax.ppermute(last, axis, up)  22 us
    gather x2, local copies, waits for them, and re-layouts, elastic_step(): jnp.take(pool, send_faces.reshape(-1), axis=1).reshape(width, 4, sending)  16.9 us
    dot_general x2, matrix products, elastic_step(): jnp.dot(flux_matrix, pool - near, precision=HI).reshape(width, 4, elems)  11 us
  transfers between devices with their start and end apart: 16, of which 4 were waited for; matrix products, arithmetic and copies ran while one was open for 32% of the time, Pallas kernels for 0%

commit v1 on v0

v1 whole, which is shorter than its diff:
```python
import functools

import jax
import jax.numpy as jnp
from jax import lax
from jax.experimental import pallas as pl
from jax.experimental.pallas import tpu as pltpu
from jax.sharding import PartitionSpec as P

N_ROW = 8
N_COL = 16
ELEMS = 1024
NQ = 180
NF = 90
SEND = 512
LANES = 128
POOL = 4 * ELEMS
WHOLE = POOL + 4 * SEND
TILE = 512
EDGE = 16
BLOCK = SEND + EDGE
SF = 256
CAP = 64
GROUP = 256

F32 = jnp.float32
BF16 = jnp.bfloat16
VMEM = pl.BlockSpec(memory_space=pltpu.VMEM)
SMEM = pl.BlockSpec(memory_space=pltpu.SMEM)
NN = (((1,), (0,)), ((), ()))
NT = (((1,), (1,)), ((), ()))
TT = (((0,), (1,)), ((), ()))

PAIR_A = [(i, i ^ 1) for i in range(N_ROW)]
PAIR_B = [(i, (((i + 1) ^ 1) - 1) % N_ROW) for i in range(N_ROW)]
PAIR_C = [(i, i ^ 1) for i in range(N_COL)]
PAIR_D = [(i, (((i + 1) ^ 1) - 1) % N_COL) for i in range(N_COL)]


def call(kernel, outs, name, n_in, smem=(), scratch=(), aliases=None, flops=0):
    return pl.pallas_call(
        kernel,
        out_shape=[jax.ShapeDtypeStruct(s, d) for s, d in outs],
        in_specs=[SMEM if i in smem else VMEM for i in range(n_in)],
        out_specs=[VMEM] * len(outs),
        scratch_shapes=list(scratch),
        input_output_aliases=aliases or {},
        compiler_params=pltpu.CompilerParams(vmem_limit_bytes=40 * 2**20),
        cost_estimate=pl.CostEstimate(flops=flops, bytes_accessed=2**21, transcendentals=0),
        name=name,
    )


def split(x):
    hi = x.astype(BF16)
    return hi, (x - hi.astype(F32)).astype(BF16)


def dot(a, b, dims=NN):
    return lax.dot_general(a, b, dims, preferred_element_type=F32)


def dot3(a, b, dims=NN):
    ah, al = a
    bh, bl = b
    return dot(ah, bh, dims) + (dot(ah, bl, dims) + dot(al, bh, dims))


def parities():
    row = lax.axis_index("row")
    col = lax.axis_index("col")
    return row, col, row % 2, col % 2


def slots():
    _, _, odd_row, odd_col = parities()
    return 1 - odd_row, odd_row, 3 - odd_col, 2 + odd_col


def fill_trace_ops(extract, eh, el):
    eh[...] = jnp.zeros(eh.shape, BF16)
    el[...] = jnp.zeros(el.shape, BF16)
    for f in range(4):
        h, l = split(extract[f])
        eh[pl.ds(f * LANES, NF), :] = h
        el[pl.ds(f * LANES, NF), :] = l


def write_traces(q, eh, el, table):
    traces = dot3(split(q), (eh[...], el[...]), TT)
    for f in range(4):
        table[pl.ds(f * ELEMS, ELEMS), :] = traces[:, f * LANES : (f + 1) * LANES]


def gather_rows(index, table, out, rows):
    unroll = 16

    def step(j, carry):
        for u in range(unroll):
            at = pl.multiple_of((j * unroll + u) * 8, 8)
            got = [table[pl.ds(index(at + t), 1), :] for t in range(8)]
            out[pl.ds(at, 8), :] = jnp.concatenate(got, axis=0)
        return carry

    lax.fori_loop(0, rows // 8 // unroll, step, 0)


def gather_sends(send, table, outs):
    for slot, out in zip(slots(), outs):
        gather_rows(lambda i, slot=slot: send[slot, i], table, out, SEND)


def first_kernel(state, extract, send, table, out_a, out_b, out_c, out_d, eh, el):
    fill_trace_ops(extract, eh, el)
    write_traces(state[...], eh, el, table)
    gather_sends(send, table, (out_a, out_b, out_c, out_d))


def operators_kernel(extract, volume, flux, lift, v2, l2):
    total = volume[...]
    fl = split(flux[...])
    l2[...] = jnp.zeros(l2.shape, F32)
    for f in range(4):
        folded = dot3(split(lift[:, f, :]), fl)
        l2[:, pl.ds(f * LANES, NF)] = folded
        total = total + dot3(split(folded), split(extract[f]))
    v2[...] = total


def place_received(table, recv):
    row, col, _, _ = parities()
    gone_b = (row == 0) | (row == N_ROW - 1)
    gone_d = (col == 0) | (col == N_COL - 1)
    for slot, got, gone in zip(slots(), recv, (None, gone_b, None, gone_d)):
        value = got[pl.ds(0, SEND), :]
        if gone is not None:
            value = jnp.where(gone, 0.0, value)
        table[pl.ds(pl.multiple_of(POOL + slot * SEND, SEND), SEND), :] = value


def advance(q, near, jac, v2, l2):
    inner = dot3(split(v2), split(q))
    gathered = jnp.concatenate([near[pl.ds(f * ELEMS, ELEMS), :] for f in range(4)], axis=1)
    gathered = jnp.where(lax.broadcasted_iota(jnp.int32, gathered.shape, 1) % LANES < NF, gathered, 0.0)
    lifted = dot3(split(l2), split(gathered), NT)
    return q + 0.25 * jac * (inner - lifted)


def middle_kernel(
    state, jac, extract, v2, l2, nbr, send, table_in, in_a, in_b, in_c, in_d,
    new_state, table, out_a, out_b, out_c, out_d, eh, el, near,
):
    place_received(table, (in_a, in_b, in_c, in_d))
    gather_rows(lambda i: nbr[i], table, near, POOL)
    new = advance(state[...], near, jac[...], v2[...], l2[...])
    new_state[...] = new
    fill_trace_ops(extract, eh, el)
    write_traces(new, eh, el, table)
    gather_sends(send, table, (out_a, out_b, out_c, out_d))


def last_kernel(
    state, jac, extract, v2, l2, nbr, sf_face, sf_dest, sf_row, sf_col, weights, table_in, in_a, in_b, in_c, in_d,
    new_state, table, stay, box_a, box_b, near,
):
    place_received(table, (in_a, in_b, in_c, in_d))
    gather_rows(lambda i: nbr[i], table, near, POOL)
    new = advance(state[...], near, jac[...], v2[...], l2[...])
    new_state[...] = new
    ops = jnp.concatenate([extract[f][20:30, :] for f in range(4)], axis=0)
    on_faces = dot3(split(ops), split(new))
    elem = sf_face[...] % ELEMS
    face = sf_face[...] // ELEMS
    pick = (lax.broadcasted_iota(jnp.int32, (ELEMS, SF), 0) == elem).astype(BF16)
    fh, fl = split(on_faces)
    chosen = dot(fh, pick) + dot(fl, pick)
    vz = jnp.zeros((10, SF), F32)
    for f in range(4):
        vz = vz + jnp.where(face == f, chosen[f * 10 : (f + 1) * 10, :], 0.0)
    values = jnp.concatenate(
        [jnp.sum(weights[c] * vz, axis=0, keepdims=True) for c in range(16)]
        + [sf_row[...].astype(F32), sf_col[...].astype(F32), jnp.zeros((6, SF), F32)],
        axis=0,
    )
    row, col, odd_row, odd_col = parities()
    dest = sf_dest[...]
    dr = dest // N_COL - row
    dc = dest % N_COL - col
    to_a = 1 - 2 * odd_row
    to_c = 1 - 2 * odd_col
    group_r = jnp.where(dr == 0, 0, jnp.where(dr == to_a, 1, 2))
    group_c = jnp.where(dc == 0, 0, jnp.where(dc == to_c, 1, 2))
    group = group_r * 3 + group_c
    groups = lax.broadcasted_iota(jnp.int32, (16, SF), 0)
    owners = (groups == group).astype(F32)
    before = (
        lax.broadcasted_iota(jnp.int32, (SF, SF), 0) < lax.broadcasted_iota(jnp.int32, (SF, SF), 1)
    ).astype(BF16)
    ranks = dot(owners.astype(BF16), before)
    rank = jnp.sum(ranks * owners, axis=0, keepdims=True).astype(jnp.int32)
    place = group_r * GROUP + group_c * CAP + rank
    into = (lax.broadcasted_iota(jnp.int32, (3 * GROUP, SF), 0) == place).astype(BF16)
    vh, vl = split(values)
    box = dot(vh, into, NT) + dot(vl, into, NT)
    stay[...] = box[:, :GROUP]
    box_a[...] = box[:, GROUP : 2 * GROUP]
    box_b[...] = box[:, 2 * GROUP :]


def uplift_kernel(mine, got_c, got_d, height, wet, out, cols_h, cols_l, rows):
    lane = lax.broadcasted_iota(jnp.int32, (72, LANES), 1)
    first = jnp.where(lane < CAP, mine[:, :LANES], got_c[...])
    patches = [first[24 * g : 24 * (g + 1)] for g in range(3)]
    patches += [got_d[24 * g : 24 * (g + 1), :] for g in range(3)]
    half = lax.broadcasted_iota(jnp.int32, (24, LANES), 1) < CAP
    patches = [jnp.where(half, p, 0.0) if g >= 3 else p for g, p in enumerate(patches)]
    data = jnp.concatenate(patches, axis=1)
    total = data.shape[1]
    anchor_row = data[16:17, :].astype(jnp.int32)
    anchor_col = data[17:18, :].astype(jnp.int32)
    at = lax.broadcasted_iota(jnp.int32, (TILE, total), 0)
    d_col = at - anchor_col
    d_row = at - anchor_row
    acc = jnp.zeros((TILE, TILE), F32)
    masks = [d_col == b for b in range(4)]
    for a in range(4):
        spread = jnp.zeros((TILE, total), F32)
        for b in range(4):
            spread = jnp.where(masks[b], data[4 * a + b : 4 * a + b + 1, :], spread)
        sh, sl = split(spread)
        pick = (d_row == a).astype(BF16)
        acc = acc + (dot(pick, sh, NT) + dot(pick, sl, NT))
    out[...] = height[...] + acc * wet[...].astype(F32)


def body(
    state, neighbours, send_faces, jacobian, face_extract, volume_op, flux_matrix, lift_op,
    sf_face, sf_dest, sf_row, sf_col, sf_weights, ocean, depth, wet,
):
    nbr = neighbours.reshape(POOL)
    jac = jacobian.reshape(1, ELEMS)
    block = ((SEND, LANES), F32)
    table_t = ((WHOLE, LANES), F32)
    state_t = ((NQ, ELEMS), F32)
    trace_ops = [pltpu.VMEM((4 * LANES, NQ), BF16)] * 2
    near = pltpu.VMEM((POOL, LANES), F32)

    def exchange(a, b, c, d):
        d = lax.ppermute(d, "col", PAIR_D)
        c = lax.ppermute(c, "col", PAIR_C)
        b = lax.ppermute(b, "row", PAIR_B)
        a = lax.ppermute(a, "row", PAIR_A)
        return a, b, c, d

    table, *sends = call(
        first_kernel, [table_t] + [block] * 4, "traces_first", 3, smem=(2,), scratch=trace_ops
    )(state, face_extract, send_faces)
    recv = exchange(*sends)
    v2, l2 = call(
        operators_kernel, [((NQ, NQ), F32), ((NQ, 4 * LANES), F32)], "operators", 4
    )(face_extract, volume_op, flux_matrix, lift_op)
    state, table, *sends = call(
        middle_kernel, [state_t, table_t] + [block] * 4, "step_first", 12, smem=(5, 6),
        scratch=trace_ops + [near], aliases={7: 1},
    )(state, jac, face_extract, v2, l2, nbr, send_faces, table, *recv)
    recv = exchange(*sends)
    box_t = ((24, GROUP), F32)
    state, _, stay, box_a, box_b = call(
        last_kernel, [state_t, table_t, box_t, box_t, box_t], "step_last", 16, smem=(5,),
        scratch=[near], aliases={11: 1},
    )(
        state, jac, face_extract, v2, l2, nbr, sf_face.reshape(1, SF), sf_dest.reshape(1, SF),
        sf_row.reshape(1, SF), sf_col.reshape(1, SF), sf_weights, table, *recv,
    )
    got_b = lax.ppermute(box_b, "row", PAIR_B)
    got_a = lax.ppermute(box_a, "row", PAIR_A)
    mine = jnp.concatenate([stay, got_a, got_b], axis=0)
    got_d = lax.ppermute(mine[:, LANES:], "col", PAIR_D)
    got_c = lax.ppermute(mine[:, :LANES], "col", PAIR_C)

    wet_f = wet.astype(F32)
    fields = ocean * wet_f[None]
    row, col = lax.axis_index("row"), lax.axis_index("col")
    odd_row, odd_col = row % 2 == 1, col % 2 == 1

    def edges(first, last, axis, odd, at, count, even_pairs, odd_pairs):
        near_even = lax.ppermute(jnp.where(odd, first, last), axis, even_pairs)
        near_odd = lax.ppermute(jnp.where(odd, last, first), axis, odd_pairs)
        near_odd = jnp.where((at == 0) | (at == count - 1), 0.0, near_odd)
        return jnp.where(odd, near_even, near_odd), jnp.where(odd, near_odd, near_even)

    up, down = edges(fields[:, 0, :], fields[:, -1, :], "row", odd_row, row, N_ROW, PAIR_A, PAIR_B)
    left, right = edges(fields[:, :, 0], fields[:, :, -1], "col", odd_col, col, N_COL, PAIR_C, PAIR_D)
    north = jnp.concatenate([up[:, None, :], fields[:, :-1, :]], axis=1)
    south = jnp.concatenate([fields[:, 1:, :], down[:, None, :]], axis=1)
    west = jnp.concatenate([left[:, :, None], fields[:, :, :-1]], axis=2)
    east = jnp.concatenate([fields[:, :, 1:], right[:, :, None]], axis=2)
    avg = 0.25 * (north + south + west + east)
    height = avg[0] - 0.2 * (east[1] - west[1] + (south[2] - north[2]))
    speed_u = avg[1] - 0.2 * depth * (east[0] - west[0])
    speed_v = avg[2] - 0.2 * depth * (south[0] - north[0])
    plane = call(
        uplift_kernel, [((TILE, TILE), F32)], "uplift", 5,
        scratch=[],
    ) if False else None
    (height,) = pl.pallas_call(
        functools.partial(uplift_plain),
        out_shape=[jax.ShapeDtypeStruct((TILE, TILE), F32)],
        in_specs=[VMEM] * 5,
        out_specs=[VMEM],
        compiler_params=pltpu.CompilerParams(vmem_limit_bytes=40 * 2**20),
        name="uplift",
    )(mine, got_c, got_d, height * wet_f, wet)
    ocean_out = jnp.stack([height, speed_u * wet_f, speed_v * wet_f])
    return state, ocean_out


def uplift_plain(mine, got_c, got_d, height, wet, out):
    uplift_kernel(mine, got_c, got_d, height, wet, out, None, None, None)


def solution(mesh):
    both = ("row", "col")
    return jax.shard_map(
        body,
        mesh=mesh,
        in_specs=(
            P(None, both), P(None, both), P(None, both), P(both), P(), P(), P(), P(),
            P(both), P(both, None), P(both), P(both), P(None, None, both),
            P(None, "row", "col"), P("row", "col"), P("row", "col"),
        ),
        out_specs=(P(None, both), P(None, "row", "col")),
        check_vma=False,
    )
```

time: 405 us -> 115 us (0.28)
  the two profiles are of different devices: /device:TPU:24 before, /device:TPU:0 now
where the time goes in v1:
time: 115 us; the launch traced here: 114 us
  Pallas kernels  33.5 us (29%)
  starting transfers between devices  26.5 us (23%)
  local copies, waits for them, and re-layouts  24.7 us (21%)
  other arithmetic  20.2 us (18%)
  waiting for transfers between devices  8.34 us (7%)
    pallas_call x1, Pallas kernels, body(): call(middle_kernel, [state_t, table_t] + [block] * 4, 'step_first', 12, s...  13 us
    ppermute x2, starting transfers between devices, edges(): near_odd = lax.ppermute(jnp.where(odd, last, first), axis, odd_pairs)  9.44 us
    unnamed x71, local copies, waits for them, and re-layouts  9.06 us
    pallas_call x1, Pallas kernels, body(): call(first_kernel, [table_t] + [block] * 4, 'traces_first', 3, smem=(2,),...  7.44 us
    pallas_call x1, Pallas kernels, body(): call(last_kernel, [state_t, table_t, box_t, box_t, box_t], 'step_last', 1...  6.88 us
    slice x1, local copies, waits for them, and re-layouts, body(): north = jnp.concatenate([up[:, None, :], fields[:, :-1, :]], axis=1)  6.86 us
    mul x1, other arithmetic, body(): avg = 0.25 * (north + south + west + east)  6.41 us
    ppermute x1, starting transfers between devices, body(): got_d = lax.ppermute(mine[:, LANES:], 'col', PAIR_D)  5.14 us
  transfers between devices with their start and end apart: 16, of which 4 were waited for; matrix products, arithmetic and copies ran while one was open for 28% of the time, Pallas kernels for 8%

profile of v1, /device:TPU:0, one launch (start us, length us, event | category | flops | bytes accessed | tf_op | source)
XLA Modules:
  0.0 114.3 jit_solution(12651677429512513619)
XLA Ops:
  0.6 1.3 %convert_element_type.3 = f32[512,512]{1,0:T(8,128)S(1)} convert(s32[512,512]{1,0:T(8,128)} %wet.1) | non-fusion elementwise | flops 262144 | bytes 2097152 | tf_op jit(solution)/shard_map/convert_element_type | solution.py:281
  2.0 0.0 copy-start.29
  2.0 0.0 copy-start.11
  2.0 2.4 %broadcast_multiply_fusion = f32[3,512,512]{2,1,0:T(8,128)S(1)} fusion(f32[3,512,512]{2,1,0:T(8,128)} %param.29, f32[512,512]{1,0:T(8,128)S(1)} %convert_element_type.3), kind=kLoop, calls=%fused_computation.25 | loop fusion | flops 786432 | bytes 7340032 | tf_op jit(solution)/shard_map/mul | solution.py:282
  4.4 0.0 copy-start.21
  4.4 1.6 %select_reduce_fusion = (f32[3,512]{1,0:T(4,128)}, f32[3,512]{1,0:T(4,128)}) fusion(f32[3,512,512]{2,1,0:T(8,128)S(1)} %broadcast_multiply_fusion, pred[]{:T(512)S(6)} %eq.24), kind=kLoop, calls=%fused_computation.55 | loop fusion | flops 3072 | bytes 24577 | tf_op jit(solution)/shard_map/jit(_where)/select_n | solution.py:288
  6.1 6.6 %collective-permute-start.15 = (f32[3,512]{1,0:T(4,128)}, f32[3,512]{1,0:T(4,128)}, u32[]{:S(2)}, u32[]{:S(2)}) collective-permute-start(f32[3,512]{1,0:T(4,128)} %get-tuple-element.36), channel_id=1, source_target_pairs={{0,15},{1,2},{2,1},{3,4},{4,3},{5,6},{6,5},{7,8},{8,7},{9,10},{10,... | collective-permute-start | bytes 18440 | tf_op jit(solution)/shard_map/ppermute | solution.py:288
  12.6 0.0 collective-permute-start.14
  12.7 0.6 copy.82
  13.3 0.0 collective-permute-start.12
  13.3 0.6 copy.81
  13.9 2.9 %collective-permute-start.13 = (f32[3,512]{1,0:T(4,128)}, f32[3,512]{1,0:T(4,128)}, u32[]{:S(2)}, u32[]{:S(2)}) collective-permute-start(f32[3,512]{1,0:T(4,128)} %bitcast.58), channel_id=1, source_target_pairs={{0,112},{16,32},{32,16},{48,64},{64,48},{80,96},{96,80},{112,0},{1... | collective-permute-start | bytes 18440 | tf_op jit(solution)/shard_map/ppermute | solution.py:288
  16.7 0.1 copy.67.extract
  16.8 0.0 copy-start.1
  16.8 1.1 copy-done.1
  17.9 7.4 %traces_first.1 = (f32[6144,128]{1,0:T(8,128)S(1)}, f32[512,128]{1,0:T(8,128)}, f32[512,128]{1,0:T(8,128)S(1)}, f32[512,128]{1,0:T(8,128)S(1)}, f32[512,128]{1,0:T(8,128)S(1)}) custom-call(f32[180,1024]{1,0:T(8,128)S(1)} %copy-done.1, f32[4,90,180]{2,1,0:T(8,128)S(1)} %copy.67.extract, s32[4,512]{1,0:T(4,128)S(1)} %copy-done.11), custom_call_target="tpu_custom_call" | custom-call | bytes 2097152 | tf_op jit(solution)/shard_map/traces_first/pallas_call | solution.py:255
  25.4 0.0 collective-permute-start
  25.4 0.0 copy-start.22
  25.4 6.9 %fusion.32 = (f32[3,511,512]{2,1,0:T(8,128)}, f32[3,511,512]{2,1,0:T(8,128)}) fusion(f32[3,512,512]{2,1,0:T(8,128)} %copy-done.21), kind=kLoop, calls=%fused_computation.70 | loop fusion | bytes 12558336 | tf_op jit(solution)/shard_map/slice | solution.py:294
  32.3 3.8 %fusion.31 = (f32[3,512,511]{2,1,0:T(8,128)}, f32[3,512,511]{2,1,0:T(8,128)}) fusion(f32[3,512,512]{2,1,0:T(8,128)S(1)} %copy-done.22), kind=kLoop, calls=%fused_computation.69 | loop fusion | bytes 12558336 | tf_op jit(solution)/shard_map/slice | solution.py:297
  36.1 0.7 copy.80
  36.8 1.7 %copy.69.weights = f32[16,10,256]{2,1,0:T(8,128)} copy(f32[16,10,256]{2,0,1:T(8,128)} %param.28) | data formatting | bytes 327680 | tf_op args[12]
  38.5 1.0 copy-done.8
  39.5 0.9 copy-done.9
  40.4 0.8 copy-done.10
  41.2 1.6 %operators.1 = (f32[180,180]{1,0:T(8,128)S(1)}, f32[180,512]{1,0:T(8,128)S(1)}) custom-call(f32[4,90,180]{2,1,0:T(8,128)S(1)} %copy.67.extract, f32[180,180]{1,0:T(8,128)S(1)} %copy-done.9, f32[90,90]{1,0:T(8,128)S(1)} %copy-done.10, f32[180,4,90]{2,1,0:T(4,128)S(1)} %copy-done.8), custom_call_target="tpu_custom_call" | custom-call | bytes 2097152 | tf_op jit(solution)/shard_map/operators/pallas_call | solution.py:259
  42.8 0.0 copy-start.3
  42.9 0.7 copy-done.3
  43.6 0.7 copy-done.6
  44.3 0.8 collective-permute-start.1
  45.0 2.0 %collective-permute-start.2 = (f32[512,128]{1,0:T(8,128)}, f32[512,128]{1,0:T(8,128)}, u32[]{:S(2)}, u32[]{:S(2)}) collective-permute-start(f32[512,128]{1,0:T(8,128)} %copy-done.19), channel_id=1, source_target_pairs={{0,1},{1,0},{2,3},{3,2},{4,5},{5,4},{6,7},{7,6},{8,9},{9,8},{10,11... | collective-permute-start | bytes 786440 | tf_op jit(solution)/shard_map/ppermute | solution.py:250
  47.0 0.7 select_bitcast_fusion.3
  47.8 0.6 copy.70
  48.4 0.6 copy.71
  49.0 0.0 collective-permute-done.15
  49.0 0.0 collective-permute-start.3
  49.0 1.3 %select_bitcast_fusion.1 = (f32[3,512,1]{1,0,2:T(4,128)}, f32[3,512,1]{1,0,2:T(4,128)}) fusion(f32[3,512]{1,0:T(4,128)} %collective-permute-done.14, f32[3,512]{1,0:T(4,128)} %collective-permute-done.15, pred[]{:T(512)S(6)} %or.7, pred[]{:T(512)S(6)} %eq.24), kind=kLoop, calls=%fused_computation.66 | loop fusion | flops 4608 | bytes 24578 | tf_op jit(solution)/shard_map/broadcast_in_dim | solution.py:296
  50.3 1.9 %copy.72 = f32[3,512,1]{2,1,0:T(8,128)} copy(f32[3,512,1]{1,0,2:T(4,128)} %get-tuple-element.48) | data formatting | bytes 12288 | tf_op jit(solution)/shard_map/broadcast_in_dim | solution.py:296
  52.2 1.9 %copy.73 = f32[3,512,1]{2,1,0:T(8,128)} copy(f32[3,512,1]{1,0,2:T(4,128)} %get-tuple-element.49) | data formatting | bytes 12288 | tf_op jit(solution)/shard_map/broadcast_in_dim | solution.py:297
  54.1 0.0 copy-start.13
  54.1 0.0 copy-start.25
  54.1 6.4 %fusion.1 = f32[3,512,512]{2,1,0:T(8,128)S(1)} fusion(f32[3,512,1]{2,1,0:T(8,128)} %copy.73, f32[3,512,1]{2,1,0:T(8,128)} %copy.72, f32[3,1,512]{2,1,0:T(1,128)} %copy.71, f32[3,1,512]{2,1,0:T(1,128)} %copy.70, f32[3,511,512]{2,1,0:T(8,128)} %get-tuple-element.44, f32[3,511,512]{2,1,0:T(8,128)} %get-tuple-element.45, f32[3,512,511]{2,1,0:T(8,128)} %get-tuple-element.41, ...), kind=kLoop, calls=%fused_computation.13 | loop fusion | flops 6291456 | bytes 15728640 | tf_op jit(solution)/shard_map/mul | solution.py:298
  60.5 0.0 copy-start
  60.7 13.0 %step_first.1 = (f32[180,1024]{1,0:T(8,128)S(1)}, f32[6144,128]{1,0:T(8,128)S(1)}, f32[512,128]{1,0:T(8,128)S(1)}, f32[512,128]{1,0:T(8,128)S(1)}, f32[512,128]{1,0:T(8,128)S(1)}, /*index=5*/f32[512,128]{1,0:T(8,128)S(1)}) custom-call(f32[180,1024]{1,0:T(8,128)S(1)} %copy-done.2, f32[1,1024]{1,0:T(1,128)S(1)} %bitcast.63, ...), custom_call_target="tpu_custom_call", output_to_operand_aliasing={{1}: (7, {})} | custom-call | bytes 2097152 | tf_op jit(solution)/shard_map/step_first/pallas_call | solution.py:262
  73.7 0.1 collective-permute-start.4
  73.8 2.0 %collective-permute-start.5 = (f32[512,128]{1,0:T(8,128)S(1)}, f32[512,128]{1,0:T(8,128)S(1)}, u32[]{:S(2)}, u32[]{:S(2)}) collective-permute-start(f32[512,128]{1,0:T(8,128)S(1)} %get-tuple-element.29), channel_id=1, source_target_pairs={{0,112},{16,32},{32,16},{48,64},{64,48},{80,96},{96,80},{112,0},{1... | collective-permute-start | bytes 786440 | tf_op jit(solution)/shard_map/ppermute | solution.py:251
  75.8 0.3 collective-permute-start.6
  76.1 0.0 copy-start.17
  76.1 4.9 %collective-permute-start.7 = (f32[512,128]{1,0:T(8,128)S(1)}, f32[512,128]{1,0:T(8,128)S(1)}, u32[]{:S(2)}, u32[]{:S(2)}) collective-permute-start(f32[512,128]{1,0:T(8,128)S(1)} %get-tuple-element.31), channel_id=1, source_target_pairs={{0,15},{1,2},{2,1},{3,4},{4,3},{5,6},{6,5},{7,8},{8,7},{9,10},{10,... | collective-permute-start | bytes 786440 | tf_op jit(solution)/shard_map/ppermute | solution.py:249
  81.0 3.8 %fusion.10 = (f32[512,512]{1,0:T(8,128)S(1)}, f32[1,512,512]{2,1,0:T(8,128)}) fusion(f32[3,512,511]{2,1,0:T(8,128)S(1)} %copy-done.25, f32[3,512,511]{2,1,0:T(8,128)S(1)} %copy-done.26, f32[3,511,512]{2,1,0:T(8,128)S(1)} %copy-done.24, f32[3,511,512]{2,1,0:T(8,128)S(1)} %copy-done.23, f32[3,512,1]{2,1,0:T(8,128)} %copy.73, f32[3,512,1]{2,1,0:T(8,128)} %copy.72, ...), kind=kLoop, calls=%fused_computation.32 | loop fusion | flops 4718592 | bytes 18874368 | tf_op jit(solution)/shard_map/mul | solution.py:313
  84.8 2.3 %collective-permute-done.7.in_d = f32[512,128]{1,0:T(8,128)S(1)} collective-permute-done((f32[512,128]{1,0:T(8,128)S(1)}, f32[512,128]{1,0:T(8,128)S(1)}, u32[]{:S(2)}, u32[]{:S(2)}) %collective-permute-start.7) | collective-permute-done | bytes 262176 | tf_op jit(solution)/shard_map/ppermute | solution.py:249
  87.1 0.0 copy-start.28
  87.1 6.9 %step_last.1 = (f32[180,1024]{1,0:T(8,128)}, f32[6144,128]{1,0:T(8,128)S(1)}, f32[24,256]{1,0:T(8,128)S(1)}, f32[24,256]{1,0:T(8,128)S(1)}, f32[24,256]{1,0:T(8,128)S(1)}) custom-call(f32[180,1024]{1,0:T(8,128)S(1)} %get-tuple-element.26.state, f32[1,1024]{1,0:T(1,128)S(1)} %bitcast.64, ...), custom_call_target="tpu_custom_call", output_to_operand_aliasing={{1}: (11, {})} | custom-call | bytes 2097152 | tf_op jit(solution)/shard_map/step_last/pallas_call | solution.py:268
  94.0 0.0 collective-permute-start.8
  94.1 1.8 %collective-permute-start.9 = (f32[24,256]{1,0:T(8,128)S(1)}, f32[24,256]{1,0:T(8,128)S(1)}, u32[]{:S(2)}, u32[]{:S(2)}) collective-permute-start(f32[24,256]{1,0:T(8,128)S(1)} %get-tuple-element.35), channel_id=1, source_target_pairs={{0,112},{16,32},{32,16},{48,64},{64,48},{80,96},{96,80},{112,0},{1... | collective-permute-start | bytes 73736 | tf_op jit(solution)/shard_map/ppermute | solution.py:275
  95.9 2.7 %collective-permute-done.9 = f32[24,256]{1,0:T(8,128)S(1)} collective-permute-done((f32[24,256]{1,0:T(8,128)S(1)}, f32[24,256]{1,0:T(8,128)S(1)}, u32[]{:S(2)}, u32[]{:S(2)}) %collective-permute-start.9) | collective-permute-done | bytes 24608 | tf_op jit(solution)/shard_map/ppermute | solution.py:275
  98.6 5.1 %collective-permute-start.11 = (f32[72,128]{1,0:T(8,128)S(1)}, f32[72,128]{1,0:T(8,128)S(1)}, u32[]{:S(2)}, u32[]{:S(2)}) collective-permute-start(f32[72,128]{1,0:T(8,128)S(1)} %get-tuple-element.46), channel_id=1, source_target_pairs={{0,15},{1,2},{2,1},{3,4},{4,3},{5,6},{6,5},{7,8},{8,7},{9,10},{10,... | collective-permute-start | bytes 110600 | tf_op jit(solution)/shard_map/ppermute | solution.py:278
  103.8 0.0 collective-permute-start.10
  103.8 0.7 fusion.28
  104.4 0.0 copy-start.27
  104.4 1.6 %collective-permute-done.11.got_d = f32[72,128]{1,0:T(8,128)S(1)} collective-permute-done((f32[72,128]{1,0:T(8,128)S(1)}, f32[72,128]{1,0:T(8,128)S(1)}, u32[]{:S(2)}, u32[]{:S(2)}) %collective-permute-start.11) | collective-permute-done | bytes 36896 | tf_op jit(solution)/shard_map/ppermute | solution.py:278
  106.0 1.7 %collective-permute-done.10.got_c = f32[72,128]{1,0:T(8,128)S(1)} collective-permute-done((f32[72,128]{1,0:T(8,128)S(1)}, f32[72,128]{1,0:T(8,128)S(1)}, u32[]{:S(2)}, u32[]{:S(2)}) %collective-permute-start.10) | collective-permute-done | bytes 36896 | tf_op jit(solution)/shard_map/ppermute | solution.py:279
  107.7 4.6 %uplift.1 = f32[512,512]{1,0:T(8,128)S(1)} custom-call(f32[72,256]{1,0:T(8,128)S(1)} %constant_dynamic-update-slice_fusion.mine, f32[72,128]{1,0:T(8,128)S(1)} %collective-permute-done.10.got_c, f32[72,128]{1,0:T(8,128)S(1)} %collective-permute-done.11.got_d, f32[512,512]{1,0:T(8,128)S(1)} %get-tuple-element.38.height, s32[512,512]{1,0:T(8,128)S(1)} %copy-done), custom_call_target="tpu_custom_call" | custom-call | tf_op jit(solution)/shard_map/uplift/pallas_call | solution.py:306
  112.4 2.0 %pad_maximum_fusion.4 = f32[3,512,512]{2,1,0:T(8,128)} fusion(f32[1,512,512]{2,1,0:T(8,128)S(1)} %fusion.28, f32[1,512,512]{2,1,0:T(8,128)S(1)} %copy-done.27, f32[1,512,512]{2,1,0:T(8,128)S(1)} %bitcast.60), kind=kLoop, calls=%fused_computation.16 | loop fusion | flops 1572864 | bytes 6291456 | tf_op jit(solution)/shard_map/stack | solution.py:314
  (62 shorter events, 0.1 us)
Async XLA Ops:
  2.0 14.8 %copy-start.29 = (f32[4,90,180]{2,0,1:T(4,128)S(1)}, f32[4,90,180]{2,0,1:T(4,128)}, u32[]{:S(2)}) copy-start(f32[4,90,180]{2,0,1:T(4,128)} %param.20) | copy-start | bytes 777604
  2.0 14.8 %copy-start.11 = (s32[4,512]{1,0:T(4,128)S(1)}, s32[4,512]{1,0:T(4,128)}, u32[]{:S(2)}) copy-start(s32[4,512]{1,0:T(4,128)} %send.3) | copy-start | bytes 24580
  4.4 9.4 %copy-start.21 = (f32[3,512,512]{2,1,0:T(8,128)}, f32[3,512,512]{2,1,0:T(8,128)S(1)}, u32[]{:S(2)}) copy-start(f32[3,512,512]{2,1,0:T(8,128)S(1)} %broadcast_multiply_fusion) | copy-start | bytes 9437188
  6.1 42.9 %collective-permute-start.15 = (f32[3,512]{1,0:T(4,128)}, f32[3,512]{1,0:T(4,128)}, u32[]{:S(2)}, u32[]{:S(2)}) collective-permute-start(f32[3,512]{1,0:T(4,128)} %get-tuple-element.36), channel_id=1, source_target_pairs={{0,15},{1,2},{2,1},{3,4},{4,3},{5,6},{6,5},{7,8},{8,7},{9,10},{10,... | collective-permute-start | bytes 18440 | tf_op jit(solution)/shard_map/ppermute | solution.py:288
  12.6 36.3 %collective-permute-start.14 = (f32[3,512]{1,0:T(4,128)}, f32[3,512]{1,0:T(4,128)}, u32[]{:S(2)}, u32[]{:S(2)}) collective-permute-start(f32[3,512]{1,0:T(4,128)} %get-tuple-element.37), channel_id=1, source_target_pairs={{0,1},{1,0},{2,3},{3,2},{4,5},{5,4},{6,7},{7,6},{8,9},{9,8},{10,11... | collective-permute-start | bytes 18440 | tf_op jit(solution)/shard_map/ppermute | solution.py:287
  13.3 31.0 %collective-permute-start.12 = (f32[3,512]{1,0:T(4,128)}, f32[3,512]{1,0:T(4,128)}, u32[]{:S(2)}, u32[]{:S(2)}) collective-permute-start(f32[3,512]{1,0:T(4,128)} %bitcast.59), channel_id=1, source_target_pairs={{0,16},{16,0},{32,48},{48,32},{64,80},{80,64},{96,112},{112,96},{1... | collective-permute-start | bytes 18440 | tf_op jit(solution)/shard_map/ppermute | solution.py:287
  13.9 31.2 %collective-permute-start.13 = (f32[3,512]{1,0:T(4,128)}, f32[3,512]{1,0:T(4,128)}, u32[]{:S(2)}, u32[]{:S(2)}) collective-permute-start(f32[3,512]{1,0:T(4,128)} %bitcast.58), channel_id=1, source_target_pairs={{0,112},{16,32},{32,16},{48,64},{64,48},{80,96},{96,80},{112,0},{1... | collective-permute-start | bytes 18440 | tf_op jit(solution)/shard_map/ppermute | solution.py:288
  16.8 1.1 copy-start.1
  25.4 6.9 %copy-start.18 = (f32[512,128]{1,0:T(8,128)}, f32[512,128]{1,0:T(8,128)S(1)}, u32[]{:S(2)}) copy-start(f32[512,128]{1,0:T(8,128)S(1)} %get-tuple-element.25) | copy-start | bytes 786436
  25.4 6.9 %copy-start.19 = (f32[512,128]{1,0:T(8,128)}, f32[512,128]{1,0:T(8,128)S(1)}, u32[]{:S(2)}) copy-start(f32[512,128]{1,0:T(8,128)S(1)} %get-tuple-element.24) | copy-start | bytes 786436
  25.4 6.9 %copy-start.20 = (f32[512,128]{1,0:T(8,128)}, f32[512,128]{1,0:T(8,128)S(1)}, u32[]{:S(2)}) copy-start(f32[512,128]{1,0:T(8,128)S(1)} %get-tuple-element.23) | copy-start | bytes 786436
  25.4 35.2 %collective-permute-start = (f32[512,128]{1,0:T(8,128)}, f32[512,128]{1,0:T(8,128)}, u32[]{:S(2)}, u32[]{:S(2)}) collective-permute-start(f32[512,128]{1,0:T(8,128)} %get-tuple-element.22), channel_id=1, source_target_pairs={{0,16},{16,0},{32,48},{48,32},{64,80},{80,64},{96,112},{112,96},{1... | collective-permute-start | bytes 786440 | tf_op jit(solution)/shard_map/ppermute | solution.py:252
  25.4 6.9 %copy-start.22 = (f32[3,512,512]{2,1,0:T(8,128)S(1)}, f32[3,512,512]{2,1,0:T(8,128)}, u32[]{:S(2)}) copy-start(f32[3,512,512]{2,1,0:T(8,128)} %copy-done.21) | copy-start | bytes 9437188
  38.5 1.0 copy-start.8
  39.5 0.9 copy-start.9
  40.4 0.8 copy-start.10
  42.8 0.7 copy-start.3
  43.6 0.7 copy-start.6
  44.3 16.3 %collective-permute-start.1 = (f32[512,128]{1,0:T(8,128)}, f32[512,128]{1,0:T(8,128)}, u32[]{:S(2)}, u32[]{:S(2)}) collective-permute-start(f32[512,128]{1,0:T(8,128)} %copy-done.20), channel_id=1, source_target_pairs={{0,112},{16,32},{32,16},{48,64},{64,48},{80,96},{96,80},{112,0},{1... | collective-permute-start | bytes 786440 | tf_op jit(solution)/shard_map/ppermute | solution.py:251
  45.0 15.6 %collective-permute-start.2 = (f32[512,128]{1,0:T(8,128)}, f32[512,128]{1,0:T(8,128)}, u32[]{:S(2)}, u32[]{:S(2)}) collective-permute-start(f32[512,128]{1,0:T(8,128)} %copy-done.19), channel_id=1, source_target_pairs={{0,1},{1,0},{2,3},{3,2},{4,5},{5,4},{6,7},{7,6},{8,9},{9,8},{10,11... | collective-permute-start | bytes 786440 | tf_op jit(solution)/shard_map/ppermute | solution.py:250
  49.0 11.7 %collective-permute-start.3 = (f32[512,128]{1,0:T(8,128)}, f32[512,128]{1,0:T(8,128)}, u32[]{:S(2)}, u32[]{:S(2)}) collective-permute-start(f32[512,128]{1,0:T(8,128)} %copy-done.18), channel_id=1, source_target_pairs={{0,15},{1,2},{2,1},{3,4},{4,3},{5,6},{6,5},{7,8},{8,7},{9,10},{10,... | collective-permute-start | bytes 786440 | tf_op jit(solution)/shard_map/ppermute | solution.py:249
  54.1 6.6 %copy-start.2 = (f32[180,1024]{1,0:T(8,128)S(1)}, f32[180,1024]{1,0:T(8,128)}, u32[]{:S(2)}) copy-start(f32[180,1024]{1,0:T(8,128)} %state.3) | copy-start | bytes 2211844
  54.1 6.6 %copy-start.4 = (f32[180,512]{1,0:T(8,128)S(1)}, f32[180,512]{1,0:T(8,128)}, u32[]{:S(2)}) copy-start(f32[180,512]{1,0:T(8,128)} %copy-done.3) | copy-start | bytes 1105924
  54.1 6.6 %copy-start.7 = (f32[180,180]{1,0:T(8,128)S(1)}, f32[180,180]{1,0:T(8,128)}, u32[]{:S(2)}) copy-start(f32[180,180]{1,0:T(8,128)} %copy-done.6) | copy-start | bytes 388804
  54.1 6.6 %copy-start.12 = (s32[4,512]{1,0:T(4,128)S(1)}, s32[4,512]{1,0:T(4,128)}, u32[]{:S(2)}) copy-start(s32[4,512]{1,0:T(4,128)} %send.3) | copy-start | bytes 24580
  54.1 6.6 %copy-start.13 = (f32[1024]{0:T(1024)S(1)}, f32[1024]{0:T(1024)}, u32[]{:S(2)}) copy-start(f32[1024]{0:T(1024)} %param.19) | copy-start | bytes 12292
  54.1 26.9 %copy-start.24 = (f32[3,511,512]{2,1,0:T(8,128)S(1)}, f32[3,511,512]{2,1,0:T(8,128)}, u32[]{:S(2)}) copy-start(f32[3,511,512]{2,1,0:T(8,128)} %get-tuple-element.45) | copy-start | bytes 9418756
  54.1 26.8 %copy-start.25 = (f32[3,512,511]{2,1,0:T(8,128)S(1)}, f32[3,512,511]{2,1,0:T(8,128)}, u32[]{:S(2)}) copy-start(f32[3,512,511]{2,1,0:T(8,128)} %get-tuple-element.40) | copy-start | bytes 9418756
  54.1 26.8 %copy-start.26 = (f32[3,512,511]{2,1,0:T(8,128)S(1)}, f32[3,512,511]{2,1,0:T(8,128)}, u32[]{:S(2)}) copy-start(f32[3,512,511]{2,1,0:T(8,128)} %get-tuple-element.41) | copy-start | bytes 9418756
  60.5 20.4 %copy-start = (s32[512,512]{1,0:T(8,128)S(1)}, s32[512,512]{1,0:T(8,128)}, u32[]{:S(2)}) copy-start(s32[512,512]{1,0:T(8,128)} %wet.1) | copy-start | bytes 3145732
  60.5 20.4 %copy-start.23 = (f32[3,511,512]{2,1,0:T(8,128)S(1)}, f32[3,511,512]{2,1,0:T(8,128)}, u32[]{:S(2)}) copy-start(f32[3,511,512]{2,1,0:T(8,128)} %get-tuple-element.44) | copy-start | bytes 9418756
  60.6 20.4 %copy-start.30 = (f32[3,1,512]{2,1,0:T(1,128)S(1)}, f32[3,1,512]{2,1,0:T(1,128)}, u32[]{:S(2)}) copy-start(f32[3,1,512]{2,1,0:T(1,128)} %copy.70) | copy-start | bytes 18436
  60.6 20.4 %copy-start.31 = (f32[3,1,512]{2,1,0:T(1,128)S(1)}, f32[3,1,512]{2,1,0:T(1,128)}, u32[]{:S(2)}) copy-start(f32[3,1,512]{2,1,0:T(1,128)} %copy.71) | copy-start | bytes 18436
  73.7 11.1 %collective-permute-start.4 = (f32[512,128]{1,0:T(8,128)S(1)}, f32[512,128]{1,0:T(8,128)S(1)}, u32[]{:S(2)}, u32[]{:S(2)}) collective-permute-start(f32[512,128]{1,0:T(8,128)S(1)} %get-tuple-element.28), channel_id=1, source_target_pairs={{0,16},{16,0},{32,48},{48,32},{64,80},{80,64},{96,112},{112,96},{1... | collective-permute-start | bytes 786440 | tf_op jit(solution)/shard_map/ppermute | solution.py:252
  73.8 11.0 %collective-permute-start.5 = (f32[512,128]{1,0:T(8,128)S(1)}, f32[512,128]{1,0:T(8,128)S(1)}, u32[]{:S(2)}, u32[]{:S(2)}) collective-permute-start(f32[512,128]{1,0:T(8,128)S(1)} %get-tuple-element.29), channel_id=1, source_target_pairs={{0,112},{16,32},{32,16},{48,64},{64,48},{80,96},{96,80},{112,0},{1... | collective-permute-start | bytes 786440 | tf_op jit(solution)/shard_map/ppermute | solution.py:251
  75.8 9.0 %collective-permute-start.6 = (f32[512,128]{1,0:T(8,128)S(1)}, f32[512,128]{1,0:T(8,128)S(1)}, u32[]{:S(2)}, u32[]{:S(2)}) collective-permute-start(f32[512,128]{1,0:T(8,128)S(1)} %get-tuple-element.30), channel_id=1, source_target_pairs={{0,1},{1,0},{2,3},{3,2},{4,5},{5,4},{6,7},{7,6},{8,9},{9,8},{10,11... | collective-permute-start | bytes 786440 | tf_op jit(solution)/shard_map/ppermute | solution.py:250
  76.1 11.0 %copy-start.5 = (f32[16,10,256]{2,1,0:T(8,128)S(1)}, f32[16,10,256]{2,1,0:T(8,128)}, u32[]{:S(2)}) copy-start(f32[16,10,256]{2,1,0:T(8,128)} %copy.69.weights) | copy-start | bytes 491524
  76.1 11.0 %copy-start.14 = (s32[256]{0:T(256)S(1)}, s32[256]{0:T(256)}, u32[]{:S(2)}) copy-start(s32[256]{0:T(256)} %param.24) | copy-start | bytes 3076
  76.1 11.0 %copy-start.15 = (s32[256,1]{0,1:T(1,128)S(1)}, s32[256,1]{0,1:T(1,128)}, u32[]{:S(2)}) copy-start(s32[256,1]{0,1:T(1,128)} %param.25) | copy-start | bytes 3076
  76.1 11.0 %copy-start.16 = (s32[256]{0:T(256)S(1)}, s32[256]{0:T(256)}, u32[]{:S(2)}) copy-start(s32[256]{0:T(256)} %param.26) | copy-start | bytes 3076
  76.1 11.0 %copy-start.17 = (s32[256]{0:T(256)S(1)}, s32[256]{0:T(256)}, u32[]{:S(2)}) copy-start(s32[256]{0:T(256)} %param.27) | copy-start | bytes 3076
  76.1 11.0 %collective-permute-start.7 = (f32[512,128]{1,0:T(8,128)S(1)}, f32[512,128]{1,0:T(8,128)S(1)}, u32[]{:S(2)}, u32[]{:S(2)}) collective-permute-start(f32[512,128]{1,0:T(8,128)S(1)} %get-tuple-element.31), channel_id=1, source_target_pairs={{0,15},{1,2},{2,1},{3,4},{4,3},{5,6},{6,5},{7,8},{8,7},{9,10},{10,... | collective-permute-start | bytes 786440 | tf_op jit(solution)/shard_map/ppermute | solution.py:249
  87.1 16.6 %copy-start.28 = (f32[512,512]{1,0:T(8,128)S(1)}, f32[512,512]{1,0:T(8,128)}, u32[]{:S(2)}) copy-start(f32[512,512]{1,0:T(8,128)} %param.30) | copy-start | bytes 3145732
  94.0 1.9 %collective-permute-start.8 = (f32[24,256]{1,0:T(8,128)S(1)}, f32[24,256]{1,0:T(8,128)S(1)}, u32[]{:S(2)}, u32[]{:S(2)}) collective-permute-start(f32[24,256]{1,0:T(8,128)S(1)} %get-tuple-element.34), channel_id=1, source_target_pairs={{0,16},{16,0},{32,48},{48,32},{64,80},{80,64},{96,112},{112,96},{1... | collective-permute-start | bytes 73736 | tf_op jit(solution)/shard_map/ppermute | solution.py:276
  94.1 4.5 %collective-permute-start.9 = (f32[24,256]{1,0:T(8,128)S(1)}, f32[24,256]{1,0:T(8,128)S(1)}, u32[]{:S(2)}, u32[]{:S(2)}) collective-permute-start(f32[24,256]{1,0:T(8,128)S(1)} %get-tuple-element.35), channel_id=1, source_target_pairs={{0,112},{16,32},{32,16},{48,64},{64,48},{80,96},{96,80},{112,0},{1... | collective-permute-start | bytes 73736 | tf_op jit(solution)/shard_map/ppermute | solution.py:275
  98.6 7.4 %collective-permute-start.11 = (f32[72,128]{1,0:T(8,128)S(1)}, f32[72,128]{1,0:T(8,128)S(1)}, u32[]{:S(2)}, u32[]{:S(2)}) collective-permute-start(f32[72,128]{1,0:T(8,128)S(1)} %get-tuple-element.46), channel_id=1, source_target_pairs={{0,15},{1,2},{2,1},{3,4},{4,3},{5,6},{6,5},{7,8},{8,7},{9,10},{10,... | collective-permute-start | bytes 110600 | tf_op jit(solution)/shard_map/ppermute | solution.py:278
  103.8 4.0 %collective-permute-start.10 = (f32[72,128]{1,0:T(8,128)S(1)}, f32[72,128]{1,0:T(8,128)S(1)}, u32[]{:S(2)}, u32[]{:S(2)}) collective-permute-start(f32[72,128]{1,0:T(8,128)S(1)} %get-tuple-element.47), channel_id=1, source_target_pairs={{0,1},{1,0},{2,3},{3,2},{4,5},{5,4},{6,7},{7,6},{8,9},{9,8},{10,11... | collective-permute-start | bytes 110600 | tf_op jit(solution)/shard_map/ppermute | solution.py:279
  104.4 7.9 %copy-start.27 = (f32[1,512,512]{2,1,0:T(8,128)S(1)}, f32[1,512,512]{2,1,0:T(8,128)}, u32[]{:S(2)}) copy-start(f32[1,512,512]{2,1,0:T(8,128)} %get-tuple-element.39) | copy-start | bytes 3145732

commit v2 on v1

v2 whole, which is shorter than its diff:
```python
import jax
import jax.numpy as jnp
from jax import lax
from jax.experimental import pallas as pl
from jax.experimental.pallas import tpu as pltpu
from jax.sharding import PartitionSpec as P

N_ROW = 8
N_COL = 16
ELEMS = 1024
NQ = 180
KP = 256
NF = 90
SEND = 512
LANES = 128
POOL = 4 * ELEMS
WHOLE = POOL + 4 * SEND
TILE = 512
EDGE = 16
EDGE_LANE = 96
SF = 256
CAP = 64
GROUP = 256
CHUNK = 256

F32 = jnp.float32
BF16 = jnp.bfloat16
VMEM = pl.BlockSpec(memory_space=pltpu.VMEM)
SMEM = pl.BlockSpec(memory_space=pltpu.SMEM)
ANY = pl.BlockSpec(memory_space=pl.ANY)
NN = (((1,), (0,)), ((), ()))
NT = (((1,), (1,)), ((), ()))

PAIR_A = [(i, i ^ 1) for i in range(N_ROW)]
PAIR_B = [(i, (((i + 1) ^ 1) - 1) % N_ROW) for i in range(N_ROW)]
PAIR_C = [(i, i ^ 1) for i in range(N_COL)]
PAIR_D = [(i, (((i + 1) ^ 1) - 1) % N_COL) for i in range(N_COL)]


def call(kernel, name, ins, outs, scratch=(), aliases=None, flops=0):
    return pl.pallas_call(
        kernel,
        out_shape=[jax.ShapeDtypeStruct(s, d) for s, d, _ in outs],
        in_specs=list(ins),
        out_specs=[spec for _, _, spec in outs],
        scratch_shapes=list(scratch),
        input_output_aliases=aliases or {},
        compiler_params=pltpu.CompilerParams(vmem_limit_bytes=32 * 2**20),
        cost_estimate=pl.CostEstimate(flops=flops, bytes_accessed=2**21, transcendentals=0),
        name=name,
    )


def split(x):
    hi = x.astype(BF16)
    return hi, (x - hi.astype(F32)).astype(BF16)


def dot(a, b, dims=NN):
    return lax.dot_general(a, b, dims, preferred_element_type=F32)


def dot3(a, b, dims=NN):
    ah, al = a
    bh, bl = b
    return dot(ah, bh, dims) + (dot(ah, bl, dims) + dot(al, bh, dims))


def left_parts(x, axis):
    hi, lo = split(x)
    return jnp.concatenate([hi, hi, lo], axis=axis)


def right_parts(x, axis):
    hi, lo = split(x)
    return jnp.concatenate([hi, lo, hi], axis=axis)


def parities():
    row = lax.axis_index("row")
    col = lax.axis_index("col")
    return row, col, row % 2, col % 2


def slots():
    _, _, odd_row, odd_col = parities()
    return 1 - odd_row, odd_row, 3 - odd_col, 2 + odd_col


def gather_rows(index, base, table, out, rows):
    unroll = 16

    def step(j, carry):
        to = j * (unroll * 8)
        for u in range(unroll):
            at = pl.multiple_of(to + u * 8, 8)
            got = [table[pl.ds(index[base + at + t], 1), :] for t in range(8)]
            out[pl.ds(at, 8), :] = jnp.concatenate(got, axis=0)
        return carry

    lax.fori_loop(0, rows // 8 // unroll, step, 0)


def gather_sends(send, table, blocks, extras, outs, sems):
    where = slots()
    copies = []
    for i in (3, 2, 1, 0):
        gather_rows(send, where[i] * SEND, table, blocks[i], SEND)
        if extras is not None:
            if i >= 2:
                blocks[i][...] = blocks[i][...] + extras[i][...]
            else:
                blocks[i][pl.ds(SEND, EDGE), :] = extras[i][...]
        copy = pltpu.make_async_copy(blocks[i], outs[i], sems.at[i])
        copy.start()
        copies.append(copy)
    return copies


def pad_state(q, padded):
    padded[pl.ds(176, KP - 176), :] = jnp.zeros((KP - 176, ELEMS), F32)
    padded[pl.ds(0, NQ), :] = q


def traces_of_chunk(padded, ek, table, c):
    at = c * CHUNK
    mine = jnp.transpose(padded[:, at : at + CHUNK])
    traces = dot(left_parts(mine, 1), ek[...], NT)
    for f in range(4):
        table[pl.ds(f * ELEMS + at, CHUNK), :] = traces[:, f * LANES : (f + 1) * LANES]


def first_kernel(state, extract, send, table, ek, out_d, out_c, out_b, out_a, full, padded, ba, bb, bc, bd, sems):
    full[...] = jnp.zeros(full.shape, F32)
    for f in range(4):
        full[pl.ds(f * LANES, NF), pl.ds(0, NQ)] = extract[:, f, :]
    ek[...] = right_parts(full[...], 1)
    pad_state(state[...], padded)
    for c in range(ELEMS // CHUNK):
        traces_of_chunk(padded, ek, table, c)
    copies = gather_sends(send, table, (ba, bb, bc, bd), None, (out_a, out_b, out_c, out_d), sems)
    for copy in copies:
        copy.wait()


def prepare_kernel(
    extract, volume_h, flux_h, lift_h, ocean_h, wet_h, v2k, l2k, ea, eb, ec, ed,
    v2, l2, volume, flux, lift, sides, ends, wet_sides, wet_ends, sems,
):
    wide = TILE - LANES
    pairs = [(flux_h, flux), (lift_h, lift), (volume_h, volume)]
    for i, at in enumerate((0, TILE - 8)):
        pairs.append((ocean_h.at[:, pl.ds(at, 8), :], ends.at[i]))
        pairs.append((wet_h.at[pl.ds(at, 8), :], wet_ends.at[i]))
    for i, at in enumerate((0, wide)):
        pairs.append((ocean_h.at[:, :, pl.ds(at, LANES)], sides.at[i]))
        pairs.append((wet_h.at[:, pl.ds(at, LANES)], wet_sides.at[i]))
    copies = [pltpu.make_async_copy(src, dst, sems.at[i]) for i, (src, dst) in enumerate(pairs)]
    for copy in copies:
        copy.start()
    for copy in copies[:3]:
        copy.wait()
    total = volume[...]
    fl = split(flux[...])
    l2[...] = jnp.zeros(l2.shape, F32)
    v2[...] = jnp.zeros(v2.shape, F32)
    for f in range(4):
        folded = dot3(split(lift[:, f, :]), fl)
        l2[:, pl.ds(f * LANES, NF)] = folded
        total = total + dot3(split(folded), split(extract[:, f, :]))
    v2[:, pl.ds(0, NQ)] = total
    v2k[...] = left_parts(v2[...], 1)
    l2k[...] = left_parts(l2[...], 1)
    for copy in copies[3:]:
        copy.wait()
    _, _, odd_row, odd_col = parities()
    lane = lax.broadcasted_iota(jnp.int32, (TILE, LANES), 1)
    last = LANES - 1
    west = wet_sides[0, :, 0:1].astype(F32)
    east = wet_sides[1, :, last : last + 1].astype(F32)
    north = wet_ends[0, 0:1, :].astype(F32)
    south = wet_ends[1, 7:8, :].astype(F32)
    to_c = jnp.zeros((TILE, LANES), F32)
    to_d = jnp.zeros((TILE, LANES), F32)
    rows_a = []
    rows_b = []
    for f in range(3):
        left = sides[0, f, :, 0:1] * west
        right = sides[1, f, :, last : last + 1] * east
        to_c = jnp.where(lane == EDGE_LANE + f, jnp.where(odd_col == 1, left, right), to_c)
        to_d = jnp.where(lane == EDGE_LANE + f, jnp.where(odd_col == 1, right, left), to_d)
        top = ends[0, f, 0:1, :] * north
        bottom = ends[1, f, 7:8, :] * south
        for rows, edge in (
            (rows_a, jnp.where(odd_row == 1, top, bottom)),
            (rows_b, jnp.where(odd_row == 1, bottom, top)),
        ):
            rows += [edge[:, t * LANES : (t + 1) * LANES] for t in range(4)]
    spare = [jnp.zeros((EDGE - 12, LANES), F32)]
    ea[...] = jnp.concatenate(rows_a + spare, axis=0)
    eb[...] = jnp.concatenate(rows_b + spare, axis=0)
    ec[...] = to_c
    ed[...] = to_d


def receive(table, recv, sems):
    copies = []
    for i, slot in enumerate(slots()):
        at = pl.multiple_of(POOL + slot * SEND, SEND)
        copy = pltpu.make_async_copy(recv[i].at[pl.ds(0, SEND), :], table.at[pl.ds(at, SEND), :], sems.at[i])
        copy.start()
        copies.append(copy)
    return copies


def zero_absent(table):
    row, col, _, _ = parities()
    for gone, slot in (
        (row == 0, 0), (row == N_ROW - 1, 1), (col == 0, 2), (col == N_COL - 1, 3),
    ):
        @pl.when(gone)
        def _():
            table[pl.ds(POOL + slot * SEND, SEND), :] = jnp.zeros((SEND, LANES), F32)


def advance(q, near, jac, v2k, l2k, new):
    size = 512
    for at in range(0, ELEMS, size):
        mine = q[:, at : at + size]
        inner = dot(v2k[...], right_parts(mine, 0))
        gathered = jnp.concatenate([near[pl.ds(f * ELEMS + at, size), :] for f in range(4)], axis=1)
        lifted = dot(l2k[...], right_parts(gathered, 1), NT)
        new[:, at : at + size] = mine[:NQ] + 0.25 * jac[:, at : at + size] * (inner - lifted)


def middle_kernel(
    state, jac, ek, v2k, l2k, ea, eb, ec, ed, nbr, send, table_in, in_a, in_b, in_c, in_d,
    new_state, table, out_d, out_c, out_b, out_a,
    padded, near, ba, bb, bc, bd, sems, out_sems,
):
    arriving = receive(table, (in_a, in_b, in_c, in_d), sems)
    pad_state(state[...], padded)
    for copy in arriving:
        copy.wait()
    zero_absent(table)
    gather_rows(nbr, 0, table, near, POOL)
    advance(padded, near, jac, v2k, l2k, new_state)
    padded[pl.ds(0, NQ), :] = new_state[...]
    for c in range(ELEMS // CHUNK):
        traces_of_chunk(padded, ek, table, c)
    copies = gather_sends(
        send, table, (ba, bb, bc, bd), (ea, eb, ec, ed), (out_a, out_b, out_c, out_d), out_sems
    )
    for copy in copies:
        copy.wait()


def last_kernel(
    state, jac, extract, v2k, l2k, nbr, sf_face, sf_dest, sf_row, sf_col, weights, table_in, in_a, in_b, in_c, in_d,
    new_state, table, stay, box_a, box_b,
    padded, near, new_local, sems, out_sem,
):
    arriving = receive(table, (in_a, in_b, in_c, in_d), sems)
    pad_state(state[...], padded)
    for copy in arriving:
        copy.wait()
    zero_absent(table)
    gather_rows(nbr, 0, table, near, POOL)
    advance(padded, near, jac, v2k, l2k, new_local)
    leaving = pltpu.make_async_copy(new_local, new_state, out_sem)
    leaving.start()
    ops = jnp.concatenate([extract[20:30, f, :] for f in range(4)], axis=0)
    on_faces = dot3(split(ops), split(new_local[...]))
    elem = sf_face[...] % ELEMS
    face = sf_face[...] // ELEMS
    pick = (lax.broadcasted_iota(jnp.int32, (ELEMS, SF), 0) == elem).astype(BF16)
    fh, fl = split(on_faces)
    chosen = dot(fh, pick) + dot(fl, pick)
    vz = jnp.zeros((10, SF), F32)
    for f in range(4):
        vz = vz + jnp.where(face == f, chosen[f * 10 : (f + 1) * 10, :], 0.0)
    values = weights[0] * vz[0:1]
    for k in range(1, 10):
        values = values + weights[k] * vz[k : k + 1]
    values = jnp.concatenate(
        [values, sf_row[...].astype(F32), sf_col[...].astype(F32), jnp.zeros((6, SF), F32)], axis=0
    )
    row, col, odd_row, odd_col = parities()
    dest = sf_dest[...]
    dr = dest // N_COL - row
    dc = dest % N_COL - col
    to_a = 1 - 2 * odd_row
    to_c = 1 - 2 * odd_col
    group_r = jnp.where(dr == 0, 0, jnp.where(dr == to_a, 1, 2))
    group_c = jnp.where(dc == 0, 0, jnp.where(dc == to_c, 1, 2))
    group = group_r * 3 + group_c
    groups = lax.broadcasted_iota(jnp.int32, (16, SF), 0)
    owners = (groups == group).astype(F32)
    before = (
        lax.broadcasted_iota(jnp.int32, (SF, SF), 0) < lax.broadcasted_iota(jnp.int32, (SF, SF), 1)
    ).astype(BF16)
    ranks = dot(owners.astype(BF16), before)
    rank = jnp.sum(ranks * owners, axis=0, keepdims=True).astype(jnp.int32)
    place = group_r * GROUP + group_c * CAP + rank
    into = (lax.broadcasted_iota(jnp.int32, (3 * GROUP, SF), 0) == place).astype(BF16)
    vh, vl = split(values)
    box = dot(vh, into, NT) + dot(vl, into, NT)
    stay[...] = box[:, :GROUP]
    box_a[...] = box[:, GROUP : 2 * GROUP]
    box_b[...] = box[:, 2 * GROUP :]
    leaving.wait()


def stencil_kernel(ocean, wet, depth, after, height, speeds, fields):
    wet_f = wet[...].astype(F32)
    for f in range(3):
        fields[f, pl.ds(0, 8), :] = jnp.zeros((8, TILE), F32)
        fields[f, pl.ds(TILE + 8, 8), :] = jnp.zeros((8, TILE), F32)
        fields[f, pl.ds(8, TILE), :] = ocean[f] * wet_f
    rows = 32
    lane = lax.broadcasted_iota(jnp.int32, (rows, TILE), 1)

    def step(i, carry):
        at = pl.multiple_of(i * rows, rows)
        mask = wet[pl.ds(at, rows), :].astype(F32)
        sums, across, along = [], [], []
        for f in range(3):
            big = fields[f, pl.ds(at, rows + 16), :]
            mine = big[8 : 8 + rows]
            up = big[7 : 7 + rows]
            down = big[9 : 9 + rows]
            west = jnp.where(lane == 0, 0.0, pltpu.roll(mine, 1, 1))
            east = jnp.where(lane == TILE - 1, 0.0, pltpu.roll(mine, TILE - 1, 1))
            sums.append(0.25 * ((up + down) + (west + east)))
            across.append(east - west)
            along.append(down - up)
        d = 0.2 * depth[pl.ds(at, rows), :]
        height[pl.ds(at, rows), :] = (sums[0] - 0.2 * (across[1] + along[2])) * mask
        speeds[0, pl.ds(at, rows), :] = (sums[1] - d * across[0]) * mask
        speeds[1, pl.ds(at, rows), :] = (sums[2] - d * along[0]) * mask
        return carry

    lax.fori_loop(0, TILE // rows, step, 0)


def add_edges(height, speeds, wet, depth, ga, gb, gc, gd):
    row, col, odd_row, odd_col = parities()
    gone_b = (row == 0) | (row == N_ROW - 1)
    gone_d = (col == 0) | (col == N_COL - 1)

    def edge_row(got, f):
        return jnp.concatenate([got[pl.ds(4 * f + t, 1), :] for t in range(4)], axis=1)

    from_a = [edge_row(ga, f) for f in range(3)]
    from_b = [jnp.where(gone_b, 0.0, edge_row(gb, f)) for f in range(3)]
    for at, sign, odd in ((0, 1.0, 1), (TILE - 1, -1.0, 0)):
        h, u, v = [jnp.where(odd_row == odd, x, y) for x, y in zip(from_a, from_b)]
        here = pl.ds(at, 1)
        mask = wet[here, :].astype(F32)
        d = (sign * 0.2) * depth[here, :]
        height[here, :] = height[here, :] + mask * (0.25 * h + (sign * 0.2) * v)
        speeds[0, here, :] = speeds[0, here, :] + mask * (0.25 * u)
        speeds[1, here, :] = speeds[1, here, :] + mask * (0.25 * v + d * h)
    lane = lax.broadcasted_iota(jnp.int32, (TILE, LANES), 1)
    from_c = [gc[:, EDGE_LANE + f : EDGE_LANE + f + 1] for f in range(3)]
    from_d = [jnp.where(gone_d, 0.0, gd[:, EDGE_LANE + f : EDGE_LANE + f + 1]) for f in range(3)]
    for at, edge, sign, odd in ((0, 0, 1.0, 1), (TILE - LANES, LANES - 1, -1.0, 0)):
        h, u, v = [jnp.where(odd_col == odd, x, y) for x, y in zip(from_c, from_d)]
        here = pl.ds(at, LANES)
        mask = jnp.where(lane == edge, wet[:, here].astype(F32), 0.0)
        d = (sign * 0.2) * depth[:, here]
        height[:, here] = height[:, here] + mask * (0.25 * h + (sign * 0.2) * u)
        speeds[0, :, here] = speeds[0, :, here] + mask * (0.25 * u + d * h)
        speeds[1, :, here] = speeds[1, :, here] + mask * (0.25 * v)


def uplift_of(data):
    total = data.shape[1]
    at = lax.broadcasted_iota(jnp.int32, (TILE, total), 0)
    d_row = at - data[16:17, :].astype(jnp.int32)
    d_col = at - data[17:18, :].astype(jnp.int32)
    masks = [d_col == b for b in range(4)]
    added = None
    for a in range(4):
        spread = jnp.zeros((TILE, total), F32)
        for b in range(4):
            spread = jnp.where(masks[b], data[4 * a + b : 4 * a + b + 1, :], spread)
        pick = (d_row == a).astype(BF16)
        part = dot(jnp.concatenate([pick, pick], axis=1), jnp.concatenate(split(spread), axis=1), NT)
        added = part if added is None else added + part
    return added


def finish_own_kernel(
    mine, wet, depth, height_in, speeds_in, in_a, in_b, in_c, in_d, height, speeds, out,
    ga, gb, gc, gd, sems, out_sem,
):
    arriving = [
        pltpu.make_async_copy(in_a.at[pl.ds(SEND, EDGE), :], ga, sems.at[0]),
        pltpu.make_async_copy(in_b.at[pl.ds(SEND, EDGE), :], gb, sems.at[1]),
        pltpu.make_async_copy(in_c, gc, sems.at[2]),
        pltpu.make_async_copy(in_d, gd, sems.at[3]),
    ]
    for copy in arriving:
        copy.start()
    for copy in arriving:
        copy.wait()
    add_edges(height, speeds, wet, depth, ga, gb, gc, gd)
    leaving = pltpu.make_async_copy(speeds, out.at[pl.ds(1, 2)], out_sem)
    leaving.start()
    half = lax.broadcasted_iota(jnp.int32, (24, LANES), 1) < CAP
    first = jnp.where(half, mine[pl.ds(0, 24), :], pltpu.roll(mine[pl.ds(24, 24), :], CAP, 1))
    second = jnp.where(half, mine[pl.ds(48, 24), :], 0.0)
    added = uplift_of(jnp.concatenate([first, second], axis=1))
    height[...] = height[...] + added * wet[...].astype(F32)
    leaving.wait()


def uplift_kernel(got_c, got_d, height, wet, whole, out, plane, sems):
    half = lax.broadcasted_iota(jnp.int32, (24, LANES), 1) < CAP
    added = uplift_of(jnp.concatenate(
        [jnp.where(half, got_d[pl.ds(24 * g, 24), :], got_c[pl.ds(24 * g, 24), :]) for g in range(3)], axis=1
    ))
    size = 128
    copies = []
    for part in range(TILE // size):
        at = part * size
        plane[pl.ds(at, size), :] = (
            height[pl.ds(at, size), :] + added[at : at + size] * wet[pl.ds(at, size), :].astype(F32)
        )
        copy = pltpu.make_async_copy(plane.at[pl.ds(at, size), :], out.at[0, pl.ds(at, size), :], sems.at[part])
        copy.start()
        copies.append(copy)
    for copy in copies:
        copy.wait()


def exchange(a, b, c, d):
    d = lax.ppermute(d, "col", PAIR_D)
    c = lax.ppermute(c, "col", PAIR_C)
    b = lax.ppermute(b, "row", PAIR_B)
    a = lax.ppermute(a, "row", PAIR_A)
    return a, b, c, d


def body(
    state, neighbours, send_faces, jacobian, face_extract, volume_op, flux_matrix, lift_op,
    sf_face, sf_dest, sf_row, sf_col, sf_weights, ocean, depth, wet,
):
    nbr = neighbours.reshape(POOL)
    send = send_faces.reshape(4 * SEND)
    jac = jacobian.reshape(1, ELEMS)
    extract = face_extract.transpose(1, 0, 2)
    weights = sf_weights.transpose(1, 0, 2)
    dma = pltpu.SemaphoreType.DMA
    short = (SEND, LANES)
    tall = (SEND + EDGE, LANES)
    table_o = ((WHOLE, LANES), F32, VMEM)
    padded = pltpu.VMEM((KP, ELEMS), F32)
    near = pltpu.VMEM((POOL, LANES), F32)

    table, ek, sd, sc, sb, sa = call(
        first_kernel, "traces_first", [VMEM, VMEM, SMEM],
        [table_o, ((4 * LANES, 3 * KP), BF16, VMEM)] + [(short, F32, ANY)] * 4,
        [pltpu.VMEM((4 * LANES, KP), F32), padded] + [pltpu.VMEM(short, F32)] * 4 + [dma((4,))], flops=10**10,
    )(state, extract, send)
    recv = exchange(sa, sb, sc, sd)
    v2k, l2k, ea, eb, ec, ed = call(
        prepare_kernel, "prepare", [VMEM] + [pl.BlockSpec(memory_space=pltpu.HBM)] * 5,
        [((NQ, 3 * KP), BF16, VMEM), ((NQ, 12 * LANES), BF16, VMEM)]
        + [((EDGE, LANES), F32, VMEM)] * 2 + [(short, F32, VMEM)] * 2,
        [
            pltpu.VMEM((NQ, KP), F32), pltpu.VMEM((NQ, 4 * LANES), F32), pltpu.VMEM((NQ, NQ), F32),
            pltpu.VMEM((NF, NF), F32), pltpu.VMEM((NQ, 4, NF), F32), pltpu.VMEM((2, 3, TILE, LANES), F32),
            pltpu.VMEM((2, 3, 8, TILE), F32), pltpu.VMEM((2, TILE, LANES), jnp.int32),
            pltpu.VMEM((2, 8, TILE), jnp.int32), dma((11,)),
        ], flops=5*10**9,
    )(extract, volume_op, flux_matrix, lift_op, ocean, wet)
    state, table, sd, sc, sb, sa = call(
        middle_kernel, "step_first", [VMEM] * 9 + [SMEM] * 2 + [VMEM] + [ANY] * 4,
        [((NQ, ELEMS), F32, VMEM), table_o] + [(short, F32, ANY)] * 2 + [(tall, F32, ANY)] * 2,
        [padded, near] + [pltpu.VMEM(tall, F32)] * 2 + [pltpu.VMEM(short, F32)] * 2 + [dma((4,)), dma((4,))],
        aliases={11: 1},
    )(state, jac, ek, v2k, l2k, ea, eb, ec, ed, nbr, send, table, *recv)
    recv = exchange(sa, sb, sc, sd)
    height, speeds = call(
        stencil_kernel, "stencil", [VMEM] * 4,
        [((TILE, TILE), F32, VMEM), ((2, TILE, TILE), F32, VMEM)],
        [pltpu.VMEM((3, TILE + 16, TILE), F32)], flops=10**9,
    )(ocean, wet, depth, state[:8, :LANES])
    box_o = ((24, GROUP), F32, VMEM)
    state, _, stay, box_a, box_b = call(
        last_kernel, "step_last", [VMEM] * 5 + [SMEM] + [VMEM] * 6 + [ANY] * 4,
        [((NQ, ELEMS), F32, ANY), table_o, box_o, box_o, box_o],
        [padded, near, pltpu.VMEM((NQ, ELEMS), F32), dma((4,)), dma(())],
        aliases={11: 1},
    )(
        state, jac, extract, v2k, l2k, nbr, sf_face.reshape(1, SF), sf_dest.reshape(1, SF),
        sf_row.reshape(1, SF), sf_col.reshape(1, SF), weights, table, *recv,
    )
    got_b = lax.ppermute(box_b, "row", PAIR_B)
    got_a = lax.ppermute(box_a, "row", PAIR_A)
    mine = jnp.concatenate([stay, got_a, got_b], axis=0)
    own = mine[:, :LANES]
    height, _, ocean_out = call(
        finish_own_kernel, "finish_own", [VMEM] * 5 + [ANY] * 4,
        [((TILE, TILE), F32, VMEM), ((2, TILE, TILE), F32, VMEM), ((3, TILE, TILE), F32, ANY)],
        [pltpu.VMEM((EDGE, LANES), F32)] * 2 + [pltpu.VMEM(short, F32)] * 2 + [dma((4,)), dma(())],
        aliases={3: 0, 4: 1}, flops=10**9,
    )(own, wet, depth, height, speeds, *recv)
    got_d = lax.ppermute(mine[:, LANES:], "col", PAIR_D)
    got_c = lax.ppermute(own, "col", PAIR_C)
    (ocean_out,) = call(
        uplift_kernel, "uplift", [VMEM] * 4 + [ANY], [((3, TILE, TILE), F32, ANY)],
        [pltpu.VMEM((TILE, TILE), F32), dma((4,))],
        aliases={4: 0},
    )(got_c, got_d, height, wet, ocean_out)
    return state, ocean_out


def solution(mesh):
    both = ("row", "col")
    return jax.shard_map(
        body,
        mesh=mesh,
        in_specs=(
            P(None, both), P(None, both), P(None, both), P(both), P(), P(), P(), P(),
            P(both), P(both, None), P(both), P(both), P(None, None, both),
            P(None, "row", "col"), P("row", "col"), P("row", "col"),
        ),
        out_specs=(P(None, both), P(None, "row", "col")),
        check_vma=False,
    )
```

time: 115 us -> 68.7 us (0.60)
  local copies, waits for them, and re-layouts: 24.7 us -> 2.91 us
  other arithmetic: 20.2 us -> 0 us
  starting transfers between devices: 26.5 us -> 23.9 us
  waiting for transfers between devices: 8.34 us -> 5.75 us
  Pallas kernels: 33.5 us -> 34.8 us
    mul x3 -> x0, other arithmetic: 12.6 us -> none  [the longest x1 6.41 us: body(): avg = 0.25 * (north + south + west + east)]
    slice x2 -> x1, local copies, waits for them, and re-layouts: 10.7 us -> 0.01 us  [body(): state[:8, :LANES]]
    ppermute x5 -> x1, starting transfers between devices: 9.45 us -> 0.09 us  [body(): got_c = lax.ppermute(own, 'col', PAIR_C)]
    unnamed x71 -> x38, local copies, waits for them, and re-layouts: 9.06 us -> 2.9 us
    ppermute x2, starting transfers between devices: 4.86 us -> 9.94 us  [exchange(): d = lax.ppermute(d, 'col', PAIR_D)]
    broadcast_in_dim x4 -> x0, local copies, waits for them, and re-layouts: 4.99 us -> none  [the longest x1 1.91 us: body(): west = jnp.concatenate([left[:, :, None], fields[:, :, :-1]], axis=2)]
    another operation x2 -> x0, other arithmetic: 2.62 us -> none  [body(): ocean_out = jnp.stack([height, speed_u * wet_f, speed_v * wet_f])]
    ppermute x2, starting transfers between devices: 2.75 us -> 4.77 us  [exchange(): b = lax.ppermute(b, 'row', PAIR_B)]
  transfers between devices with their start and end apart: 16 -> 12, of which waited for: 4 -> 3; matrix products, arithmetic and copies ran while one was open for 28% -> 0% of each run, Pallas kernels for 8% -> 17%
where the time goes in v2:
time: 68.7 us; the launch traced here: 68.5 us
  Pallas kernels  34.8 us (51%)
  starting transfers between devices  23.9 us (35%)
  waiting for transfers between devices  5.75 us (8%)
  local copies, waits for them, and re-layouts  2.91 us (4%)
  between operations  1.1 us (2%)
    ppermute x2, starting transfers between devices, exchange(): d = lax.ppermute(d, 'col', PAIR_D)  9.94 us
    pallas_call x1, Pallas kernels, body(): call(middle_kernel, 'step_first', [VMEM] * 9 + [SMEM] * 2 + [VMEM] + [ANY...  9.08 us
    pallas_call x1, Pallas kernels, body(): call(last_kernel, 'step_last', [VMEM] * 5 + [SMEM] + [VMEM] * 6 + [ANY] *...  7.31 us
    ppermute x1, starting transfers between devices, body(): got_d = lax.ppermute(mine[:, LANES:], 'col', PAIR_D)  5.05 us
    ppermute x2, starting transfers between devices, exchange(): b = lax.ppermute(b, 'row', PAIR_B)  4.77 us
    pallas_call x1, Pallas kernels, body(): call(prepare_kernel, 'prepare', [VMEM] + [pl.BlockSpec(memory_space=pltpu...  4.46 us
    pallas_call x1, Pallas kernels, body(): call(stencil_kernel, 'stencil', [VMEM] * 4, [((TILE, TILE), F32, VMEM), (...  3.87 us
    pallas_call x1, Pallas kernels, body(): call(first_kernel, 'traces_first', [VMEM, VMEM, SMEM], [table_o, ((4 * LA...  3.76 us
  transfers between devices with their start and end apart: 12, of which 3 were waited for; matrix products, arithmetic and copies ran while one was open for 0% of the time, Pallas kernels for 17%

profile of v2, /device:TPU:0, one launch (start us, length us, event | category | flops | bytes accessed | tf_op | source)
XLA Modules:
  0.0 68.5 jit_solution(8027797806320418759)
XLA Ops:
  0.6 0.7 %copy.23 = s32[1,4,4,128]{3,1,2,0:T(4,128)S(1)} copy(s32[1,4,4,128]{3,2,1,0:T(4,128)} %bitcast.28) | data formatting | bytes 16384
  1.3 0.0 copy-start.3
  1.3 1.1 %copy-done.3 = f32[180,1024]{1,0:T(8,128)S(1)} copy-done((f32[180,1024]{1,0:T(8,128)S(1)}, f32[180,1024]{1,0:T(8,128)}, u32[]{:S(2)}) %copy-start.3) | copy-done | bytes 737304
  2.5 0.0 copy-start.5
  2.5 1.0 %copy-done.5 = f32[4,90,180]{2,0,1:T(4,128)S(1)} copy-done((f32[4,90,180]{2,0,1:T(4,128)S(1)}, f32[4,90,180]{2,0,1:T(4,128)}, u32[]{:S(2)}) %copy-start.5) | copy-done | bytes 259224
  3.4 0.0 copy-start.16
  3.4 0.0 copy-start
  3.4 0.0 copy-start.2
  3.5 0.0 copy-start.13
  3.5 0.0 copy-start.14
  3.5 0.0 copy-start.15
  3.5 3.8 %traces_first.1 = (f32[6144,128]{1,0:T(8,128)S(1)}, bf16[512,768]{1,0:T(8,128)(2,1)S(1)}, f32[512,128]{1,0:T(8,128)S(1)}, f32[512,128]{1,0:T(8,128)S(1)}, f32[51...) custom-call(f32[180,1024]{1,0:T(8,128)S(1)} %copy-done.3, f32[90,4,180]{2,1,0:T(4,128)S(1)} %bitcast.13, s32[2048]{0:T(1024)S(1)} %bitcast.19), custom_call_target="tpu_custom_call" | custom-call | flops 10000000000 | bytes 2097152 | tf_op jit(solution)/shard_map/traces_first/pallas_call | solution.py:462
  7.3 0.1 collective-permute-start
  7.3 2.9 %collective-permute-start.1 = (f32[512,128]{1,0:T(8,128)S(1)}, f32[512,128]{1,0:T(8,128)S(1)}, u32[]{:S(2)}, u32[]{:S(2)}) collective-permute-start(f32[512,128]{1,0:T(8,128)S(1)} %get-tuple-element.37), channel_id=1, source_target_pairs={{0,112},{16,32},{32,16},{48,64},{64,48},{80,96},{96,80},{112,0},{1... | collective-permute-start | bytes 786440 | tf_op jit(solution)/shard_map/ppermute | solution.py:441
  10.3 1.9 %collective-permute-start.2 = (f32[512,128]{1,0:T(8,128)S(1)}, f32[512,128]{1,0:T(8,128)S(1)}, u32[]{:S(2)}, u32[]{:S(2)}) collective-permute-start(f32[512,128]{1,0:T(8,128)S(1)} %get-tuple-element.38), channel_id=1, source_target_pairs={{0,1},{1,0},{2,3},{3,2},{4,5},{5,4},{6,7},{7,6},{8,9},{9,8},{10,11... | collective-permute-start | bytes 786440 | tf_op jit(solution)/shard_map/ppermute | solution.py:440
  12.2 5.0 %collective-permute-start.3 = (f32[512,128]{1,0:T(8,128)S(1)}, f32[512,128]{1,0:T(8,128)S(1)}, u32[]{:S(2)}, u32[]{:S(2)}) collective-permute-start(f32[512,128]{1,0:T(8,128)S(1)} %get-tuple-element.39), channel_id=1, source_target_pairs={{0,15},{1,2},{2,1},{3,4},{4,3},{5,6},{6,5},{7,8},{8,7},{9,10},{10,... | collective-permute-start | bytes 786440 | tf_op jit(solution)/shard_map/ppermute | solution.py:439
  17.2 0.0 copy-done.16
  17.2 0.0 copy-done
  17.2 0.0 copy-done.2
  17.2 0.0 copy-done.6
  17.2 0.0 copy-done.13
  17.2 0.0 copy-done.14
  17.2 0.0 copy-done.15
  17.2 0.0 copy-start.4
  17.2 0.0 copy-start.8
  17.3 4.5 %prepare.1 = (bf16[180,768]{1,0:T(8,128)(2,1)S(1)}, bf16[180,1536]{1,0:T(8,128)(2,1)S(1)}, f32[16,128]{1,0:T(8,128)S(1)}, f32[16,128]{1,0:T(8,128)S(1)}, f32[512,128]{1,0:T(8,128)S(1)}, /*index=5*/f32[512,128]{1,0:T(8,128)S(1)}) custom-call(f32[90,4,180]{2,1,0:T(4,128)S(1)} %bitcast.14, f32[180,180]{1,0:T(8,128)S(1)} %copy-done.14, f32[90,90]{1,0:T(8,128)S(1)} %copy-done.15, ...), custom_call_target="tpu_custom_call" | custom-call | flops 5000000000 | bytes 2097152 | tf_op jit(solution)/shard_map/prepare/pallas_call | solution.py:468
  21.7 0.0 collective-permute-done.in_a
  21.7 0.0 collective-permute-done.1.in_b
  21.7 0.0 collective-permute-done.2.in_c
  21.8 0.5 collective-permute-done.3.in_d
  22.3 0.0 copy-done.4
  22.3 0.0 copy-done.8
  22.3 9.1 %step_first.1 = (f32[180,1024]{1,0:T(8,128)S(1)}, f32[6144,128]{1,0:T(8,128)S(1)}, f32[512,128]{1,0:T(8,128)S(1)}, f32[512,128]{1,0:T(8,128)S(1)}, f32[528,128]{1,0:T(8,128)S(1)}, /*index=5*/f32[528,128]{1,0:T(8,128)S(1)}) custom-call(f32[180,1024]{1,0:T(8,128)S(1)} %copy-done.4, f32[1,1024]{1,0:T(1,128)S(1)} %bitcast.21, ...), custom_call_target="tpu_custom_call", output_to_operand_aliasing={{1}: (11, {})} | custom-call | bytes 2097152 | tf_op jit(solution)/shard_map/step_first/pallas_call | solution.py:479
  31.4 0.0 copy-start.7
  31.4 0.0 copy-start.9
  31.4 0.0 copy-start.10
  31.4 0.0 copy-start.11
  31.4 0.0 copy-start.12
  31.4 0.1 collective-permute-start.4
  31.5 1.8 %collective-permute-start.5 = (f32[528,128]{1,0:T(8,128)S(1)}, f32[528,128]{1,0:T(8,128)S(1)}, u32[]{:S(2)}, u32[]{:S(2)}) collective-permute-start(f32[528,128]{1,0:T(8,128)S(1)} %get-tuple-element.43), channel_id=1, source_target_pairs={{0,112},{16,32},{32,16},{48,64},{64,48},{80,96},{96,80},{112,0},{1... | collective-permute-start | bytes 811016 | tf_op jit(solution)/shard_map/ppermute | solution.py:441
  33.4 0.0 collective-permute-start.6
  33.4 5.0 %collective-permute-start.7 = (f32[512,128]{1,0:T(8,128)S(1)}, f32[512,128]{1,0:T(8,128)S(1)}, u32[]{:S(2)}, u32[]{:S(2)}) collective-permute-start(f32[512,128]{1,0:T(8,128)S(1)} %get-tuple-element.45), channel_id=1, source_target_pairs={{0,15},{1,2},{2,1},{3,4},{4,3},{5,6},{6,5},{7,8},{8,7},{9,10},{10,... | collective-permute-start | bytes 786440 | tf_op jit(solution)/shard_map/ppermute | solution.py:439
  38.3 0.0 copy-done.1
  38.3 3.9 %stencil.1 = (f32[512,512]{1,0:T(8,128)S(1)}, f32[2,512,512]{2,1,0:T(8,128)S(1)}) custom-call(f32[3,512,512]{2,1,0:T(8,128)S(1)} %copy-done.2, s32[512,512]{1,0:T(8,128)S(1)} %copy-done, f32[512,512]{1,0:T(8,128)S(1)} %copy-done.1, f32[8,128]{1,0:T(8,128)S(1)} %slice.11.after), custom_call_target="tpu_custom_call" | custom-call | flops 1000000000 | bytes 2097152 | tf_op jit(solution)/shard_map/stencil/pallas_call | solution.py:486
  42.2 0.0 collective-permute-done.6.in_c
  42.2 2.5 %collective-permute-done.7.in_d = f32[512,128]{1,0:T(8,128)S(1)} collective-permute-done((f32[512,128]{1,0:T(8,128)S(1)}, f32[512,128]{1,0:T(8,128)S(1)}, u32[]{:S(2)}, u32[]{:S(2)}) %collective-permute-start.7) | collective-permute-done | bytes 262176 | tf_op jit(solution)/shard_map/ppermute | solution.py:439
  44.7 0.0 collective-permute-done.4.in_a
  44.7 0.0 collective-permute-done.5.in_b
  44.7 0.0 copy-done.7
  44.7 0.0 copy-done.9
  44.8 0.0 copy-done.10
  44.8 0.0 copy-done.11
  44.8 0.0 copy-done.12
  44.8 7.3 %step_last.1 = (f32[180,1024]{1,0:T(8,128)}, f32[6144,128]{1,0:T(8,128)S(1)}, f32[24,256]{1,0:T(8,128)S(1)}, f32[24,256]{1,0:T(8,128)S(1)}, f32[24,256]{1,0:T(8,128)S(1)}) custom-call(f32[180,1024]{1,0:T(8,128)S(1)} %get-tuple-element.40.state, f32[1,1024]{1,0:T(1,128)S(1)} %bitcast.22, ...), custom_call_target="tpu_custom_call", output_to_operand_aliasing={{1}: (11, {})} | custom-call | bytes 2097152 | tf_op jit(solution)/shard_map/step_last/pallas_call | solution.py:492
  52.1 0.1 collective-permute-start.8
  52.2 1.8 %collective-permute-start.9 = (f32[24,256]{1,0:T(8,128)S(1)}, f32[24,256]{1,0:T(8,128)S(1)}, u32[]{:S(2)}, u32[]{:S(2)}) collective-permute-start(f32[24,256]{1,0:T(8,128)S(1)} %get-tuple-element.49), channel_id=1, source_target_pairs={{0,112},{16,32},{32,16},{48,64},{64,48},{80,96},{96,80},{112,0},{1... | collective-permute-start | bytes 73736 | tf_op jit(solution)/shard_map/ppermute | solution.py:501
  54.1 0.0 collective-permute-done.8
  54.1 2.7 %collective-permute-done.9 = f32[24,256]{1,0:T(8,128)S(1)} collective-permute-done((f32[24,256]{1,0:T(8,128)S(1)}, f32[24,256]{1,0:T(8,128)S(1)}, u32[]{:S(2)}, u32[]{:S(2)}) %collective-permute-start.9) | collective-permute-done | bytes 24608 | tf_op jit(solution)/shard_map/ppermute | solution.py:501
  56.8 0.1 collective-permute-start.10
  56.9 5.1 %collective-permute-start.11 = (f32[72,128]{1,0:T(8,128)S(1)}, f32[72,128]{1,0:T(8,128)S(1)}, u32[]{:S(2)}, u32[]{:S(2)}) collective-permute-start(f32[72,128]{1,0:T(8,128)S(1)} %get-tuple-element.54), channel_id=1, source_target_pairs={{0,15},{1,2},{2,1},{3,4},{4,3},{5,6},{6,5},{7,8},{8,7},{9,10},{10,... | collective-permute-start | bytes 110600 | tf_op jit(solution)/shard_map/ppermute | solution.py:511
  61.9 3.2 %finish_own.1 = (f32[512,512]{1,0:T(8,128)S(1)}, f32[2,512,512]{2,1,0:T(8,128)S(1)}, f32[3,512,512]{2,1,0:T(8,128)}) custom-call(f32[72,128]{1,0:T(8,128)S(1)} %get-tuple-element.55.mine, s32[512,512]{1,0:T(8,128)S(1)} %copy-done, f32[512,512]{1,0:T(8,128)S(1)} %copy-done.1, ...), custom_call_target="tpu_custom_call", output_to_operand_aliasing={{0}: (3, {}), {1}: (4, {})} | custom-call | flops 1000000000 | bytes 2097152 | tf_op jit(solution)/shard_map/finish_own/pallas_call | solution.py:505
  65.1 0.0 collective-permute-done.10.got_c
  65.1 0.0 collective-permute-done.11.got_d
  65.1 3.2 %uplift.1 = f32[3,512,512]{2,1,0:T(8,128)} custom-call(f32[72,128]{1,0:T(8,128)S(1)} %collective-permute-done.10.got_c, f32[72,128]{1,0:T(8,128)S(1)} %collective-permute-done.11.got_d, f32[512,512]{1,0:T(8,128)S(1)} %get-tuple-element.52.height, s32[512,512]{1,0:T(8,128)S(1)} %copy-done, ...), custom_call_target="tpu_custom_call", output_to_operand_aliasing={{}: (4, {})} | custom-call | bytes 2097152 | tf_op jit(solution)/shard_map/uplift/pallas_call | solution.py:513
  (8 shorter events, 0.0 us)
Async XLA Ops:
  1.3 1.1 %copy-start.3 = (f32[180,1024]{1,0:T(8,128)S(1)}, f32[180,1024]{1,0:T(8,128)}, u32[]{:S(2)}) copy-start(f32[180,1024]{1,0:T(8,128)} %state.3) | copy-start | bytes 2211844
  2.5 1.0 %copy-start.5 = (f32[4,90,180]{2,0,1:T(4,128)S(1)}, f32[4,90,180]{2,0,1:T(4,128)}, u32[]{:S(2)}) copy-start(f32[4,90,180]{2,0,1:T(4,128)} %param.20) | copy-start | bytes 777604
  3.4 13.7 %copy-start.16 = (s32[4,1024]{1,0:T(4,128)S(1)}, s32[4,1024]{1,0:T(4,128)}, u32[]{:S(2)}) copy-start(s32[4,1024]{1,0:T(4,128)} %param.17) | copy-start | bytes 49156
  3.4 13.7 %copy-start = (s32[512,512]{1,0:T(8,128)S(1)}, s32[512,512]{1,0:T(8,128)}, u32[]{:S(2)}) copy-start(s32[512,512]{1,0:T(8,128)} %wet.5) | copy-start | bytes 3145732
  3.4 13.7 %copy-start.2 = (f32[3,512,512]{2,1,0:T(8,128)S(1)}, f32[3,512,512]{2,1,0:T(8,128)}, u32[]{:S(2)}) copy-start(f32[3,512,512]{2,1,0:T(8,128)} %ocean.1) | copy-start | bytes 9437188
  3.4 13.7 %copy-start.6 = (f32[4,90,180]{2,0,1:T(4,128)S(1)}, f32[4,90,180]{2,0,1:T(4,128)}, u32[]{:S(2)}) copy-start(f32[4,90,180]{2,0,1:T(4,128)} %param.20) | copy-start | bytes 777604
  3.5 13.8 %copy-start.13 = (f32[180,4,90]{2,1,0:T(4,128)S(1)}, f32[180,4,90]{2,1,0:T(4,128)}, u32[]{:S(2)}) copy-start(f32[180,4,90]{2,1,0:T(4,128)} %lift_h.1) | copy-start | bytes 777604
  3.5 13.8 %copy-start.14 = (f32[180,180]{1,0:T(8,128)S(1)}, f32[180,180]{1,0:T(8,128)}, u32[]{:S(2)}) copy-start(f32[180,180]{1,0:T(8,128)} %volume_h.1) | copy-start | bytes 388804
  3.5 13.8 %copy-start.15 = (f32[90,90]{1,0:T(8,128)S(1)}, f32[90,90]{1,0:T(8,128)}, u32[]{:S(2)}) copy-start(f32[90,90]{1,0:T(8,128)} %flux_h.1) | copy-start | bytes 97204
  7.3 14.5 %collective-permute-start = (f32[512,128]{1,0:T(8,128)S(1)}, f32[512,128]{1,0:T(8,128)S(1)}, u32[]{:S(2)}, u32[]{:S(2)}) collective-permute-start(f32[512,128]{1,0:T(8,128)S(1)} %get-tuple-element.36), channel_id=1, source_target_pairs={{0,16},{16,0},{32,48},{48,32},{64,80},{80,64},{96,112},{112,96},{1... | collective-permute-start | bytes 786440 | tf_op jit(solution)/shard_map/ppermute | solution.py:442
  7.3 14.4 %collective-permute-start.1 = (f32[512,128]{1,0:T(8,128)S(1)}, f32[512,128]{1,0:T(8,128)S(1)}, u32[]{:S(2)}, u32[]{:S(2)}) collective-permute-start(f32[512,128]{1,0:T(8,128)S(1)} %get-tuple-element.37), channel_id=1, source_target_pairs={{0,112},{16,32},{32,16},{48,64},{64,48},{80,96},{96,80},{112,0},{1... | collective-permute-start | bytes 786440 | tf_op jit(solution)/shard_map/ppermute | solution.py:441
  10.3 11.5 %collective-permute-start.2 = (f32[512,128]{1,0:T(8,128)S(1)}, f32[512,128]{1,0:T(8,128)S(1)}, u32[]{:S(2)}, u32[]{:S(2)}) collective-permute-start(f32[512,128]{1,0:T(8,128)S(1)} %get-tuple-element.38), channel_id=1, source_target_pairs={{0,1},{1,0},{2,3},{3,2},{4,5},{5,4},{6,7},{7,6},{8,9},{9,8},{10,11... | collective-permute-start | bytes 786440 | tf_op jit(solution)/shard_map/ppermute | solution.py:440
  12.2 10.1 %collective-permute-start.3 = (f32[512,128]{1,0:T(8,128)S(1)}, f32[512,128]{1,0:T(8,128)S(1)}, u32[]{:S(2)}, u32[]{:S(2)}) collective-permute-start(f32[512,128]{1,0:T(8,128)S(1)} %get-tuple-element.39), channel_id=1, source_target_pairs={{0,15},{1,2},{2,1},{3,4},{4,3},{5,6},{6,5},{7,8},{8,7},{9,10},{10,... | collective-permute-start | bytes 786440 | tf_op jit(solution)/shard_map/ppermute | solution.py:439
  17.2 5.1 %copy-start.4 = (f32[180,1024]{1,0:T(8,128)S(1)}, f32[180,1024]{1,0:T(8,128)}, u32[]{:S(2)}) copy-start(f32[180,1024]{1,0:T(8,128)} %state.3) | copy-start | bytes 2211844
  17.2 5.0 %copy-start.8 = (f32[1024]{0:T(1024)S(1)}, f32[1024]{0:T(1024)}, u32[]{:S(2)}) copy-start(f32[1024]{0:T(1024)} %param.19) | copy-start | bytes 12292
  22.3 16.0 %copy-start.1 = (f32[512,512]{1,0:T(8,128)S(1)}, f32[512,512]{1,0:T(8,128)}, u32[]{:S(2)}) copy-start(f32[512,512]{1,0:T(8,128)} %depth.3) | copy-start | bytes 3145732
  31.4 13.4 %copy-start.7 = (f32[16,10,256]{2,0,1:T(8,128)S(1)}, f32[16,10,256]{2,0,1:T(8,128)}, u32[]{:S(2)}) copy-start(f32[16,10,256]{2,0,1:T(8,128)} %param.28) | copy-start | bytes 491524
  31.4 13.4 %copy-start.9 = (s32[256]{0:T(256)S(1)}, s32[256]{0:T(256)}, u32[]{:S(2)}) copy-start(s32[256]{0:T(256)} %param.24) | copy-start | bytes 3076
  31.4 13.4 %copy-start.10 = (s32[256,1]{0,1:T(1,128)S(1)}, s32[256,1]{0,1:T(1,128)}, u32[]{:S(2)}) copy-start(s32[256,1]{0,1:T(1,128)} %param.25) | copy-start | bytes 3076
  31.4 13.4 %copy-start.11 = (s32[256]{0:T(256)S(1)}, s32[256]{0:T(256)}, u32[]{:S(2)}) copy-start(s32[256]{0:T(256)} %param.26) | copy-start | bytes 3076
  31.4 13.4 %copy-start.12 = (s32[256]{0:T(256)S(1)}, s32[256]{0:T(256)}, u32[]{:S(2)}) copy-start(s32[256]{0:T(256)} %param.27) | copy-start | bytes 3076
  31.4 13.3 %collective-permute-start.4 = (f32[528,128]{1,0:T(8,128)S(1)}, f32[528,128]{1,0:T(8,128)S(1)}, u32[]{:S(2)}, u32[]{:S(2)}) collective-permute-start(f32[528,128]{1,0:T(8,128)S(1)} %get-tuple-element.42), channel_id=1, source_target_pairs={{0,16},{16,0},{32,48},{48,32},{64,80},{80,64},{96,112},{112,96},{1... | collective-permute-start | bytes 811016 | tf_op jit(solution)/shard_map/ppermute | solution.py:442
  31.5 13.2 %collective-permute-start.5 = (f32[528,128]{1,0:T(8,128)S(1)}, f32[528,128]{1,0:T(8,128)S(1)}, u32[]{:S(2)}, u32[]{:S(2)}) collective-permute-start(f32[528,128]{1,0:T(8,128)S(1)} %get-tuple-element.43), channel_id=1, source_target_pairs={{0,112},{16,32},{32,16},{48,64},{64,48},{80,96},{96,80},{112,0},{1... | collective-permute-start | bytes 811016 | tf_op jit(solution)/shard_map/ppermute | solution.py:441
  33.4 8.9 %collective-permute-start.6 = (f32[512,128]{1,0:T(8,128)S(1)}, f32[512,128]{1,0:T(8,128)S(1)}, u32[]{:S(2)}, u32[]{:S(2)}) collective-permute-start(f32[512,128]{1,0:T(8,128)S(1)} %get-tuple-element.44), channel_id=1, source_target_pairs={{0,1},{1,0},{2,3},{3,2},{4,5},{5,4},{6,7},{7,6},{8,9},{9,8},{10,11... | collective-permute-start | bytes 786440 | tf_op jit(solution)/shard_map/ppermute | solution.py:440
  33.4 11.4 %collective-permute-start.7 = (f32[512,128]{1,0:T(8,128)S(1)}, f32[512,128]{1,0:T(8,128)S(1)}, u32[]{:S(2)}, u32[]{:S(2)}) collective-permute-start(f32[512,128]{1,0:T(8,128)S(1)} %get-tuple-element.45), channel_id=1, source_target_pairs={{0,15},{1,2},{2,1},{3,4},{4,3},{5,6},{6,5},{7,8},{8,7},{9,10},{10,... | collective-permute-start | bytes 786440 | tf_op jit(solution)/shard_map/ppermute | solution.py:439
  52.1 2.0 %collective-permute-start.8 = (f32[24,256]{1,0:T(8,128)S(1)}, f32[24,256]{1,0:T(8,128)S(1)}, u32[]{:S(2)}, u32[]{:S(2)}) collective-permute-start(f32[24,256]{1,0:T(8,128)S(1)} %get-tuple-element.48), channel_id=1, source_target_pairs={{0,16},{16,0},{32,48},{48,32},{64,80},{80,64},{96,112},{112,96},{1... | collective-permute-start | bytes 73736 | tf_op jit(solution)/shard_map/ppermute | solution.py:502
  52.2 4.5 %collective-permute-start.9 = (f32[24,256]{1,0:T(8,128)S(1)}, f32[24,256]{1,0:T(8,128)S(1)}, u32[]{:S(2)}, u32[]{:S(2)}) collective-permute-start(f32[24,256]{1,0:T(8,128)S(1)} %get-tuple-element.49), channel_id=1, source_target_pairs={{0,112},{16,32},{32,16},{48,64},{64,48},{80,96},{96,80},{112,0},{1... | collective-permute-start | bytes 73736 | tf_op jit(solution)/shard_map/ppermute | solution.py:501
  56.8 8.3 %collective-permute-start.10 = (f32[72,128]{1,0:T(8,128)S(1)}, f32[72,128]{1,0:T(8,128)S(1)}, u32[]{:S(2)}, u32[]{:S(2)}) collective-permute-start(f32[72,128]{1,0:T(8,128)S(1)} %get-tuple-element.55.mine), channel_id=1, source_target_pairs={{0,1},{1,0},{2,3},{3,2},{4,5},{5,4},{6,7},{7,6},{8,9},{9,8},{10,11... | collective-permute-start | bytes 110600 | tf_op jit(solution)/shard_map/ppermute | solution.py:512
  56.9 8.2 %collective-permute-start.11 = (f32[72,128]{1,0:T(8,128)S(1)}, f32[72,128]{1,0:T(8,128)S(1)}, u32[]{:S(2)}, u32[]{:S(2)}) collective-permute-start(f32[72,128]{1,0:T(8,128)S(1)} %get-tuple-element.54), channel_id=1, source_target_pairs={{0,15},{1,2},{2,1},{3,4},{4,3},{5,6},{6,5},{7,8},{8,7},{9,10},{10,... | collective-permute-start | bytes 110600 | tf_op jit(solution)/shard_map/ppermute | solution.py:511

commit v3 on v2

--- a/solution.py
+++ b/solution.py
@@ -22,6 +22,7 @@
 CAP = 64
 GROUP = 256
 CHUNK = 256
+SIZE = 256
 
 F32 = jnp.float32
 BF16 = jnp.bfloat16
@@ -31,10 +32,25 @@
 NN = (((1,), (0,)), ((), ()))
 NT = (((1,), (1,)), ((), ()))
 
-PAIR_A = [(i, i ^ 1) for i in range(N_ROW)]
-PAIR_B = [(i, (((i + 1) ^ 1) - 1) % N_ROW) for i in range(N_ROW)]
-PAIR_C = [(i, i ^ 1) for i in range(N_COL)]
-PAIR_D = [(i, (((i + 1) ^ 1) - 1) % N_COL) for i in range(N_COL)]
+BOTH = ("row", "col")
+
+
+def at(r, c):
+    return r * N_COL + c
+
+
+def pairs_of(partner):
+    return [(at(r, c), at(*partner(r, c))) for r in range(N_ROW) for c in range(N_COL)]
+
+
+def step_out(i):
+    return i + 1 if i % 2 else i - 1
+
+
+PAIR_A = pairs_of(lambda r, c: (r ^ 1, c))
+PAIR_B = pairs_of(lambda r, c: (step_out(r), c) if 0 < r < N_ROW - 1 else ((r, c ^ 4) if c % 4 in (1, 2) else (N_ROW - 1 - r, c)))
+PAIR_C = pairs_of(lambda r, c: (r, c ^ 1))
+PAIR_D = pairs_of(lambda r, c: (r, step_out(c)) if 0 < c < N_COL - 1 else (r ^ 1, c))
 
 
 def call(kernel, name, ins, outs, scratch=(), aliases=None, flops=0):
@@ -108,7 +124,7 @@
         gather_rows(send, where[i] * SEND, table, blocks[i], SEND)
         if extras is not None:
             if i >= 2:
-                blocks[i][...] = blocks[i][...] + extras[i][...]
+                blocks[i][pl.ds(0, SEND), :] = blocks[i][pl.ds(0, SEND), :] + extras[i][...]
             else:
                 blocks[i][pl.ds(SEND, EDGE), :] = extras[i][...]
         copy = pltpu.make_async_copy(blocks[i], outs[i], sems.at[i])
@@ -143,23 +159,7 @@
         copy.wait()
 
 
-def prepare_kernel(
-    extract, volume_h, flux_h, lift_h, ocean_h, wet_h, v2k, l2k, ea, eb, ec, ed,
-    v2, l2, volume, flux, lift, sides, ends, wet_sides, wet_ends, sems,
-):
-    wide = TILE - LANES
-    pairs = [(flux_h, flux), (lift_h, lift), (volume_h, volume)]
-    for i, at in enumerate((0, TILE - 8)):
-        pairs.append((ocean_h.at[:, pl.ds(at, 8), :], ends.at[i]))
-        pairs.append((wet_h.at[pl.ds(at, 8), :], wet_ends.at[i]))
-    for i, at in enumerate((0, wide)):
-        pairs.append((ocean_h.at[:, :, pl.ds(at, LANES)], sides.at[i]))
-        pairs.append((wet_h.at[:, pl.ds(at, LANES)], wet_sides.at[i]))
-    copies = [pltpu.make_async_copy(src, dst, sems.at[i]) for i, (src, dst) in enumerate(pairs)]
-    for copy in copies:
-        copy.start()
-    for copy in copies[:3]:
-        copy.wait()
+def prepare_kernel(extract, volume, flux, lift, ocean, wet, v2k, l2k, ea, eb, ec, ed, v2, l2):
     total = volume[...]
     fl = split(flux[...])
     l2[...] = jnp.zeros(l2.shape, F32)
@@ -171,26 +171,23 @@
     v2[:, pl.ds(0, NQ)] = total
     v2k[...] = left_parts(v2[...], 1)
     l2k[...] = left_parts(l2[...], 1)
-    for copy in copies[3:]:
-        copy.wait()
     _, _, odd_row, odd_col = parities()
     lane = lax.broadcasted_iota(jnp.int32, (TILE, LANES), 1)
-    last = LANES - 1
-    west = wet_sides[0, :, 0:1].astype(F32)
-    east = wet_sides[1, :, last : last + 1].astype(F32)
-    north = wet_ends[0, 0:1, :].astype(F32)
-    south = wet_ends[1, 7:8, :].astype(F32)
+    west = wet[:, 0:1].astype(F32)
+    east = wet[:, TILE - 1 : TILE].astype(F32)
+    north = wet[0:1, :].astype(F32)
+    south = wet[TILE - 1 : TILE, :].astype(F32)
     to_c = jnp.zeros((TILE, LANES), F32)
     to_d = jnp.zeros((TILE, LANES), F32)
     rows_a = []
     rows_b = []
     for f in range(3):
-        left = sides[0, f, :, 0:1] * west
-        right = sides[1, f, :, last : last + 1] * east
+        left = ocean[f, :, 0:1] * west
+        right = ocean[f, :, TILE - 1 : TILE] * east
         to_c = jnp.where(lane == EDGE_LANE + f, jnp.where(odd_col == 1, left, right), to_c)
         to_d = jnp.where(lane == EDGE_LANE + f, jnp.where(odd_col == 1, right, left), to_d)
-        top = ends[0, f, 0:1, :] * north
-        bottom = ends[1, f, 7:8, :] * south
+        top = ocean[f, 0:1, :] * north
+        bottom = ocean[f, TILE - 1 : TILE, :] * south
         for rows, edge in (
             (rows_a, jnp.where(odd_row == 1, top, bottom)),
             (rows_b, jnp.where(odd_row == 1, bottom, top)),
@@ -223,28 +220,56 @@
             table[pl.ds(POOL + slot * SEND, SEND), :] = jnp.zeros((SEND, LANES), F32)
 
 
-def advance(q, near, jac, v2k, l2k, new):
-    size = 512
-    for at in range(0, ELEMS, size):
-        mine = q[:, at : at + size]
-        inner = dot(v2k[...], right_parts(mine, 0))
-        gathered = jnp.concatenate([near[pl.ds(f * ELEMS + at, size), :] for f in range(4)], axis=1)
-        lifted = dot(l2k[...], right_parts(gathered, 1), NT)
-        new[:, at : at + size] = mine[:NQ] + 0.25 * jac[:, at : at + size] * (inner - lifted)
+def gather_part(index, table, near, at):
+    for f in range(4):
+        for u in range(0, SIZE, 8):
+            got = [table[pl.ds(index[f * ELEMS + at + u + t], 1), :] for t in range(8)]
+            near[pl.ds(f * SIZE + u, 8), :] = jnp.concatenate(got, axis=0)
+
+
+def advance_part(q, near, jac, v2k, l2k, at):
+    here = pl.ds(at, SIZE)
+    mine = q[:, here]
+    inner = dot(v2k[...], right_parts(mine, 0))
+    gathered = jnp.concatenate([near[pl.ds(f * SIZE, SIZE), :] for f in range(4)], axis=1)
+    lifted = dot(l2k[...], right_parts(gathered, 1), NT)
+    return mine[:NQ] + 0.25 * jac[:, here] * (inner - lifted)
+
+
+def sweep(index, table, near0, near1, work):
+    pairs = ELEMS // SIZE // 2
+    gather_part(index, table, near0, 0)
+
+    def step(i, carry):
+        at = pl.multiple_of(i * (2 * SIZE), 2 * SIZE)
+        gather_part(index, table, near1, at + SIZE)
+        work(near0, at)
+        gather_part(index, table, near0, at + 2 * SIZE)
+        work(near1, at + SIZE)
+        return carry
+
+    lax.fori_loop(0, pairs - 1, step, 0)
+    at = ELEMS - 2 * SIZE
+    gather_part(index, table, near1, at + SIZE)
+    work(near0, at)
+    work(near1, at + SIZE)
 
 
 def middle_kernel(
-    state, jac, ek, v2k, l2k, ea, eb, ec, ed, nbr, send, table_in, in_a, in_b, in_c, in_d,
+    state, jac, ek, v2k, l2k, ea, eb, ec, ed, nbr, send, table_in, in_d, in_c, in_b, in_a,
     new_state, table, out_d, out_c, out_b, out_a,
-    padded, near, ba, bb, bc, bd, sems, out_sems,
+    padded, near0, near1, ba, bb, bc, bd, sems, out_sems,
 ):
     arriving = receive(table, (in_a, in_b, in_c, in_d), sems)
     pad_state(state[...], padded)
     for copy in arriving:
         copy.wait()
     zero_absent(table)
-    gather_rows(nbr, 0, table, near, POOL)
-    advance(padded, near, jac, v2k, l2k, new_state)
+
+    def work(near, at):
+        new_state[:, pl.ds(at, SIZE)] = advance_part(padded, near, jac, v2k, l2k, at)
+
+    sweep(nbr, table, near0, near1, work)
     padded[pl.ds(0, NQ), :] = new_state[...]
     for c in range(ELEMS // CHUNK):
         traces_of_chunk(padded, ek, table, c)
@@ -256,17 +281,20 @@
 
 
 def last_kernel(
-    state, jac, extract, v2k, l2k, nbr, sf_face, sf_dest, sf_row, sf_col, weights, table_in, in_a, in_b, in_c, in_d,
+    state, jac, extract, v2k, l2k, nbr, sf_face, sf_dest, sf_row, sf_col, weights, table_in, in_d, in_c, in_b, in_a,
     new_state, table, stay, box_a, box_b,
-    padded, near, new_local, sems, out_sem,
+    padded, near0, near1, new_local, sems, out_sem,
 ):
     arriving = receive(table, (in_a, in_b, in_c, in_d), sems)
     pad_state(state[...], padded)
     for copy in arriving:
         copy.wait()
     zero_absent(table)
-    gather_rows(nbr, 0, table, near, POOL)
-    advance(padded, near, jac, v2k, l2k, new_local)
+
+    def work(near, at):
+        new_local[:, pl.ds(at, SIZE)] = advance_part(padded, near, jac, v2k, l2k, at)
+
+    sweep(nbr, table, near0, near1, work)
     leaving = pltpu.make_async_copy(new_local, new_state, out_sem)
     leaving.start()
     ops = jnp.concatenate([extract[20:30, f, :] for f in range(4)], axis=0)
@@ -392,14 +420,14 @@
 
 
 def finish_own_kernel(
-    mine, wet, depth, height_in, speeds_in, in_a, in_b, in_c, in_d, height, speeds, out,
+    mine, wet, depth, height_in, speeds_in, in_d, in_c, in_b, in_a, height, speeds, out,
     ga, gb, gc, gd, sems, out_sem,
 ):
     arriving = [
         pltpu.make_async_copy(in_a.at[pl.ds(SEND, EDGE), :], ga, sems.at[0]),
         pltpu.make_async_copy(in_b.at[pl.ds(SEND, EDGE), :], gb, sems.at[1]),
-        pltpu.make_async_copy(in_c, gc, sems.at[2]),
-        pltpu.make_async_copy(in_d, gd, sems.at[3]),
+        pltpu.make_async_copy(in_c.at[pl.ds(0, SEND), :], gc, sems.at[2]),
+        pltpu.make_async_copy(in_d.at[pl.ds(0, SEND), :], gd, sems.at[3]),
     ]
     for copy in arriving:
         copy.start()
@@ -416,7 +444,7 @@
     leaving.wait()
 
 
-def uplift_kernel(got_c, got_d, height, wet, whole, out, plane, sems):
+def uplift_kernel(got_d, got_c, height, wet, whole, out, plane, sems):
     half = lax.broadcasted_iota(jnp.int32, (24, LANES), 1) < CAP
     added = uplift_of(jnp.concatenate(
         [jnp.where(half, got_d[pl.ds(24 * g, 24), :], got_c[pl.ds(24 * g, 24), :]) for g in range(3)], axis=1
@@ -436,11 +464,11 @@
 
 
 def exchange(a, b, c, d):
-    d = lax.ppermute(d, "col", PAIR_D)
-    c = lax.ppermute(c, "col", PAIR_C)
-    b = lax.ppermute(b, "row", PAIR_B)
-    a = lax.ppermute(a, "row", PAIR_A)
-    return a, b, c, d
+    d = lax.ppermute(d, BOTH, PAIR_D)
+    c = lax.ppermute(c, BOTH, PAIR_C)
+    b = lax.ppermute(b, BOTH, PAIR_B)
+    a = lax.ppermute(a, BOTH, PAIR_A)
+    return d, c, b, a
 
 
 def body(
@@ -457,7 +485,7 @@
     tall = (SEND + EDGE, LANES)
     table_o = ((WHOLE, LANES), F32, VMEM)
     padded = pltpu.VMEM((KP, ELEMS), F32)
-    near = pltpu.VMEM((POOL, LANES), F32)
+    near = [pltpu.VMEM((4 * SIZE, LANES), F32)] * 2
 
     table, ek, sd, sc, sb, sa = call(
         first_kernel, "traces_first", [VMEM, VMEM, SMEM],
@@ -466,20 +494,15 @@
     )(state, extract, send)
     recv = exchange(sa, sb, sc, sd)
     v2k, l2k, ea, eb, ec, ed = call(
-        prepare_kernel, "prepare", [VMEM] + [pl.BlockSpec(memory_space=pltpu.HBM)] * 5,
+        prepare_kernel, "prepare", [VMEM] * 6,
         [((NQ, 3 * KP), BF16, VMEM), ((NQ, 12 * LANES), BF16, VMEM)]
         + [((EDGE, LANES), F32, VMEM)] * 2 + [(short, F32, VMEM)] * 2,
-        [
-            pltpu.VMEM((NQ, KP), F32), pltpu.VMEM((NQ, 4 * LANES), F32), pltpu.VMEM((NQ, NQ), F32),
-            pltpu.VMEM((NF, NF), F32), pltpu.VMEM((NQ, 4, NF), F32), pltpu.VMEM((2, 3, TILE, LANES), F32),
-            pltpu.VMEM((2, 3, 8, TILE), F32), pltpu.VMEM((2, TILE, LANES), jnp.int32),
-            pltpu.VMEM((2, 8, TILE), jnp.int32), dma((11,)),
-        ], flops=5*10**9,
+        [pltpu.VMEM((NQ, KP), F32), pltpu.VMEM((NQ, 4 * LANES), F32)], flops=5 * 10**9,
     )(extract, volume_op, flux_matrix, lift_op, ocean, wet)
     state, table, sd, sc, sb, sa = call(
         middle_kernel, "step_first", [VMEM] * 9 + [SMEM] * 2 + [VMEM] + [ANY] * 4,
-        [((NQ, ELEMS), F32, VMEM), table_o] + [(short, F32, ANY)] * 2 + [(tall, F32, ANY)] * 2,
-        [padded, near] + [pltpu.VMEM(tall, F32)] * 2 + [pltpu.VMEM(short, F32)] * 2 + [dma((4,)), dma((4,))],
+        [((NQ, ELEMS), F32, VMEM), table_o] + [(tall, F32, ANY)] * 4,
+        [padded] + near + [pltpu.VMEM(tall, F32)] * 4 + [dma((4,)), dma((4,))],
         aliases={11: 1},
     )(state, jac, ek, v2k, l2k, ea, eb, ec, ed, nbr, send, table, *recv)
     recv = exchange(sa, sb, sc, sd)
@@ -492,15 +515,15 @@
     state, _, stay, box_a, box_b = call(
         last_kernel, "step_last", [VMEM] * 5 + [SMEM] + [VMEM] * 6 + [ANY] * 4,
         [((NQ, ELEMS), F32, ANY), table_o, box_o, box_o, box_o],
-        [padded, near, pltpu.VMEM((NQ, ELEMS), F32), dma((4,)), dma(())],
+        [padded] + near + [pltpu.VMEM((NQ, ELEMS), F32), dma((4,)), dma(())],
         aliases={11: 1},
     )(
         state, jac, extract, v2k, l2k, nbr, sf_face.reshape(1, SF), sf_dest.reshape(1, SF),
         sf_row.reshape(1, SF), sf_col.reshape(1, SF), weights, table, *recv,
     )
-    got_b = lax.ppermute(box_b, "row", PAIR_B)
-    got_a = lax.ppermute(box_a, "row", PAIR_A)
-    mine = jnp.concatenate([stay, got_a, got_b], axis=0)
+    got_b = lax.ppermute(box_b, BOTH, PAIR_B)
+    got_a = lax.ppermute(box_a, BOTH, PAIR_A)
+    mine = jnp.concatenate([stay, got_b, got_a], axis=0)
     own = mine[:, :LANES]
     height, _, ocean_out = call(
         finish_own_kernel, "finish_own", [VMEM] * 5 + [ANY] * 4,
@@ -508,13 +531,13 @@
         [pltpu.VMEM((EDGE, LANES), F32)] * 2 + [pltpu.VMEM(short, F32)] * 2 + [dma((4,)), dma(())],
         aliases={3: 0, 4: 1}, flops=10**9,
     )(own, wet, depth, height, speeds, *recv)
-    got_d = lax.ppermute(mine[:, LANES:], "col", PAIR_D)
-    got_c = lax.ppermute(own, "col", PAIR_C)
+    got_d = lax.ppermute(mine[:, LANES:], BOTH, PAIR_D)
+    got_c = lax.ppermute(own, BOTH, PAIR_C)
     (ocean_out,) = call(
         uplift_kernel, "uplift", [VMEM] * 4 + [ANY], [((3, TILE, TILE), F32, ANY)],
         [pltpu.VMEM((TILE, TILE), F32), dma((4,))],
-        aliases={4: 0},
-    )(got_c, got_d, height, wet, ocean_out)
+        aliases={4: 0}, flops=3 * 10**9,
+    )(got_d, got_c, height, wet, ocean_out)
     return state, ocean_out
 
 

time: 68.7 us -> 56.8 us (0.83)
  the two profiles are of different devices: /device:TPU:0 before, /device:TPU:24 now
where the time goes in v3:
time: 56.8 us; the launch traced here: 56.5 us
  Pallas kernels  30 us (53%)
  starting transfers between devices  14.4 us (25%)
  waiting for transfers between devices  8.24 us (15%)
  local copies, waits for them, and re-layouts  2.91 us (5%)
  between operations  1.04 us (2%)
    pallas_call x1, Pallas kernels, body(): call(middle_kernel, 'step_first', [VMEM] * 9 + [SMEM] * 2 + [VMEM] + [ANY...  7.2 us
    ppermute x2, starting transfers between devices, exchange(): d = lax.ppermute(d, BOTH, PAIR_D)  6.78 us
    pallas_call x1, Pallas kernels, body(): call(last_kernel, 'step_last', [VMEM] * 5 + [SMEM] + [VMEM] * 6 + [ANY] *...  5.99 us
    pallas_call x1, Pallas kernels, body(): call(stencil_kernel, 'stencil', [VMEM] * 4, [((TILE, TILE), F32, VMEM), (...  3.87 us
    pallas_call x1, Pallas kernels, body(): call(first_kernel, 'traces_first', [VMEM, VMEM, SMEM], [table_o, ((4 * LA...  3.75 us
    pallas_call x1, Pallas kernels, body(): call(uplift_kernel, 'uplift', [VMEM] * 4 + [ANY], [((3, TILE, TILE), F32,...  3.19 us
    pallas_call x1, Pallas kernels, body(): call(finish_own_kernel, 'finish_own', [VMEM] * 5 + [ANY] * 4, [((TILE, TI...  3.17 us
    ppermute x2, starting transfers between devices, exchange(): b = lax.ppermute(b, BOTH, PAIR_B)  2.96 us
  transfers between devices with their start and end apart: 12, of which 7 were waited for; matrix products, arithmetic and copies ran while one was open for 0% of the time, Pallas kernels for 17%

profile of v3, /device:TPU:24, one launch (start us, length us, event | category | flops | bytes accessed | tf_op | source)
XLA Modules:
  0.0 56.5 jit_solution(10753221608219897599)
XLA Ops:
  0.6 0.7 %copy.23 = s32[1,4,4,128]{3,1,2,0:T(4,128)S(1)} copy(s32[1,4,4,128]{3,2,1,0:T(4,128)} %bitcast.28) | data formatting | bytes 16384
  1.3 0.0 copy-start.3
  1.3 1.1 %copy-done.3 = f32[180,1024]{1,0:T(8,128)S(1)} copy-done((f32[180,1024]{1,0:T(8,128)S(1)}, f32[180,1024]{1,0:T(8,128)}, u32[]{:S(2)}) %copy-start.3) | copy-done | bytes 737304
  2.5 0.0 copy-start.5
  2.5 1.0 %copy-done.5 = f32[4,90,180]{2,0,1:T(4,128)S(1)} copy-done((f32[4,90,180]{2,0,1:T(4,128)S(1)}, f32[4,90,180]{2,0,1:T(4,128)}, u32[]{:S(2)}) %copy-start.5) | copy-done | bytes 259224
  3.4 0.0 copy-start.16
  3.4 0.0 copy-start.1
  3.5 0.0 copy-start.13
  3.5 0.0 copy-start.14
  3.5 0.0 copy-start.15
  3.5 3.8 %traces_first.1 = (f32[6144,128]{1,0:T(8,128)S(1)}, bf16[512,768]{1,0:T(8,128)(2,1)S(1)}, f32[512,128]{1,0:T(8,128)S(1)}, f32[512,128]{1,0:T(8,128)S(1)}, f32[51...) custom-call(f32[180,1024]{1,0:T(8,128)S(1)} %copy-done.3, f32[90,4,180]{2,1,0:T(4,128)S(1)} %bitcast.13, s32[2048]{0:T(1024)S(1)} %bitcast.19), custom_call_target="tpu_custom_call" | custom-call | flops 10000000000 | bytes 2097152 | tf_op jit(solution)/shard_map/traces_first/pallas_call | solution.py:490
  7.2 4.3 %collective-permute-start = (f32[512,128]{1,0:T(8,128)S(1)}, f32[512,128]{1,0:T(8,128)S(1)}, u32[]{:S(2)}, u32[]{:S(2)}) collective-permute-start(f32[512,128]{1,0:T(8,128)S(1)} %get-tuple-element.36), channel_id=1, source_target_pairs={{0,16},{1,2},{2,1},{3,4},{4,3},{5,6},{6,5},{7,8},{8,7},{9,10},{10,... | collective-permute-start | bytes 786440 | tf_op jit(solution)/shard_map/ppermute | solution.py:467
  11.5 0.0 collective-permute-start.1
  11.5 1.9 %collective-permute-start.2 = (f32[512,128]{1,0:T(8,128)S(1)}, f32[512,128]{1,0:T(8,128)S(1)}, u32[]{:S(2)}, u32[]{:S(2)}) collective-permute-start(f32[512,128]{1,0:T(8,128)S(1)} %get-tuple-element.38), channel_id=1, source_target_pairs={{0,112},{1,5},{2,6},{3,115},{4,116},{5,1},{6,2},{7,119},{8,120},{9... | collective-permute-start | bytes 786440 | tf_op jit(solution)/shard_map/ppermute | solution.py:469
  13.5 0.0 collective-permute-start.3
  13.5 0.0 copy-done.16
  13.5 0.0 copy-done.1
  13.5 0.0 copy-done.2
  13.5 0.0 copy-done.6
  13.5 0.0 copy-done.13
  13.5 0.0 copy-done.14
  13.5 0.0 copy-done.15
  13.5 0.0 copy-start.4
  13.5 0.0 copy-start.8
  13.6 2.8 %prepare.1 = (bf16[180,768]{1,0:T(8,128)(2,1)S(1)}, bf16[180,1536]{1,0:T(8,128)(2,1)S(1)}, f32[16,128]{1,0:T(8,128)S(1)}, f32[16,128]{1,0:T(8,128)S(1)}, f32[512,128]{1,0:T(8,128)S(1)}, /*index=5*/f32[512,128]{1,0:T(8,128)S(1)}) custom-call(f32[90,4,180]{2,1,0:T(4,128)S(1)} %bitcast.14, f32[180,180]{1,0:T(8,128)S(1)} %copy-done.14, f32[90,90]{1,0:T(8,128)S(1)} %copy-done.15, ...), custom_call_target="tpu_custom_call" | custom-call | flops 5000000000 | bytes 2097152 | tf_op jit(solution)/shard_map/prepare/pallas_call | solution.py:496
  16.4 1.5 %collective-permute-done.in_d = f32[512,128]{1,0:T(8,128)S(1)} collective-permute-done((f32[512,128]{1,0:T(8,128)S(1)}, f32[512,128]{1,0:T(8,128)S(1)}, u32[]{:S(2)}, u32[]{:S(2)}) %collective-permute-start) | collective-permute-done | bytes 262176 | tf_op jit(solution)/shard_map/ppermute | solution.py:467
  17.8 1.5 %collective-permute-done.1.in_c = f32[512,128]{1,0:T(8,128)S(1)} collective-permute-done((f32[512,128]{1,0:T(8,128)S(1)}, f32[512,128]{1,0:T(8,128)S(1)}, u32[]{:S(2)}, u32[]{:S(2)}) %collective-permute-start.1) | collective-permute-done | bytes 262176 | tf_op jit(solution)/shard_map/ppermute | solution.py:468
  19.3 0.0 collective-permute-done.2.in_b
  19.3 0.0 collective-permute-done.3.in_a
  19.3 0.0 copy-done.4
  19.3 0.0 copy-done.8
  19.3 0.0 copy-start
  19.3 7.2 %step_first.1 = (f32[180,1024]{1,0:T(8,128)S(1)}, f32[6144,128]{1,0:T(8,128)S(1)}, f32[528,128]{1,0:T(8,128)S(1)}, f32[528,128]{1,0:T(8,128)S(1)}, f32[528,128]{1,0:T(8,128)S(1)}, /*index=5*/f32[528,128]{1,0:T(8,128)S(1)}) custom-call(f32[180,1024]{1,0:T(8,128)S(1)} %copy-done.4, f32[1,1024]{1,0:T(1,128)S(1)} %bitcast.21, ...), custom_call_target="tpu_custom_call", output_to_operand_aliasing={{1}: (11, {})} | custom-call | bytes 2097152 | tf_op jit(solution)/shard_map/step_first/pallas_call | solution.py:502
  26.6 0.0 copy-start.7
  26.6 0.0 copy-start.9
  26.6 0.0 copy-start.10
  26.6 0.0 copy-start.11
  26.6 0.0 copy-start.12
  26.6 2.5 %collective-permute-start.4 = (f32[528,128]{1,0:T(8,128)S(1)}, f32[528,128]{1,0:T(8,128)S(1)}, u32[]{:S(2)}, u32[]{:S(2)}) collective-permute-start(f32[528,128]{1,0:T(8,128)S(1)} %get-tuple-element.42), channel_id=1, source_target_pairs={{0,16},{1,2},{2,1},{3,4},{4,3},{5,6},{6,5},{7,8},{8,7},{9,10},{10,... | collective-permute-start | bytes 811016 | tf_op jit(solution)/shard_map/ppermute | solution.py:467
  29.1 0.0 collective-permute-start.5
  29.1 1.0 %collective-permute-start.6 = (f32[528,128]{1,0:T(8,128)S(1)}, f32[528,128]{1,0:T(8,128)S(1)}, u32[]{:S(2)}, u32[]{:S(2)}) collective-permute-start(f32[528,128]{1,0:T(8,128)S(1)} %get-tuple-element.44), channel_id=1, source_target_pairs={{0,112},{1,5},{2,6},{3,115},{4,116},{5,1},{6,2},{7,119},{8,120},{9... | collective-permute-start | bytes 811016 | tf_op jit(solution)/shard_map/ppermute | solution.py:469
  30.1 0.5 collective-permute-start.7
  30.7 0.0 copy-done
  30.7 3.9 %stencil.1 = (f32[512,512]{1,0:T(8,128)S(1)}, f32[2,512,512]{2,1,0:T(8,128)S(1)}) custom-call(f32[3,512,512]{2,1,0:T(8,128)S(1)} %copy-done.2, s32[512,512]{1,0:T(8,128)S(1)} %copy-done.1, f32[512,512]{1,0:T(8,128)S(1)} %copy-done, f32[8,128]{1,0:T(8,128)S(1)} %slice.11.after), custom_call_target="tpu_custom_call" | custom-call | flops 1000000000 | bytes 2097152 | tf_op jit(solution)/shard_map/stencil/pallas_call | solution.py:509
  34.6 1.3 %collective-permute-done.4.in_d = f32[528,128]{1,0:T(8,128)S(1)} collective-permute-done((f32[528,128]{1,0:T(8,128)S(1)}, f32[528,128]{1,0:T(8,128)S(1)}, u32[]{:S(2)}, u32[]{:S(2)}) %collective-permute-start.4) | collective-permute-done | bytes 270368 | tf_op jit(solution)/shard_map/ppermute | solution.py:467
  35.8 0.3 collective-permute-done.5.in_c
  36.1 0.0 collective-permute-done.6.in_b
  36.2 0.0 collective-permute-done.7.in_a
  36.2 0.0 copy-done.7
  36.2 0.0 copy-done.9
  36.2 0.0 copy-done.10
  36.2 0.0 copy-done.11
  36.2 0.0 copy-done.12
  36.2 6.0 %step_last.1 = (f32[180,1024]{1,0:T(8,128)}, f32[6144,128]{1,0:T(8,128)S(1)}, f32[24,256]{1,0:T(8,128)S(1)}, f32[24,256]{1,0:T(8,128)S(1)}, f32[24,256]{1,0:T(8,128)S(1)}) custom-call(f32[180,1024]{1,0:T(8,128)S(1)} %get-tuple-element.40.state, f32[1,1024]{1,0:T(1,128)S(1)} %bitcast.22, ...), custom_call_target="tpu_custom_call", output_to_operand_aliasing={{1}: (11, {})} | custom-call | bytes 2097152 | tf_op jit(solution)/shard_map/step_last/pallas_call | solution.py:515
  42.2 1.4 %collective-permute-start.8 = (f32[24,256]{1,0:T(8,128)S(1)}, f32[24,256]{1,0:T(8,128)S(1)}, u32[]{:S(2)}, u32[]{:S(2)}) collective-permute-start(f32[24,256]{1,0:T(8,128)S(1)} %get-tuple-element.48), channel_id=1, source_target_pairs={{0,112},{1,5},{2,6},{3,115},{4,116},{5,1},{6,2},{7,119},{8,120},{9... | collective-permute-start | bytes 73736 | tf_op jit(solution)/shard_map/ppermute | solution.py:524
  43.6 0.2 collective-permute-start.9
  43.9 2.9 %collective-permute-done.8 = f32[24,256]{1,0:T(8,128)S(1)} collective-permute-done((f32[24,256]{1,0:T(8,128)S(1)}, f32[24,256]{1,0:T(8,128)S(1)}, u32[]{:S(2)}, u32[]{:S(2)}) %collective-permute-start.8) | collective-permute-done | bytes 24608 | tf_op jit(solution)/shard_map/ppermute | solution.py:524
  46.8 0.0 collective-permute-done.9
  46.8 2.4 %collective-permute-start.10 = (f32[72,128]{1,0:T(8,128)S(1)}, f32[72,128]{1,0:T(8,128)S(1)}, u32[]{:S(2)}, u32[]{:S(2)}) collective-permute-start(f32[72,128]{1,0:T(8,128)S(1)} %get-tuple-element.55), channel_id=1, source_target_pairs={{0,16},{1,2},{2,1},{3,4},{4,3},{5,6},{6,5},{7,8},{8,7},{9,10},{10,... | collective-permute-start | bytes 110600 | tf_op jit(solution)/shard_map/ppermute | solution.py:534
  49.2 0.0 collective-permute-start.11
  49.2 3.2 %finish_own.1 = (f32[512,512]{1,0:T(8,128)S(1)}, f32[2,512,512]{2,1,0:T(8,128)S(1)}, f32[3,512,512]{2,1,0:T(8,128)}) custom-call(f32[72,128]{1,0:T(8,128)S(1)} %get-tuple-element.54.mine, s32[512,512]{1,0:T(8,128)S(1)} %copy-done.1, f32[512,512]{1,0:T(8,128)S(1)} %copy-done, ...), custom_call_target="tpu_custom_call", output_to_operand_aliasing={{0}: (3, {}), {1}: (4, {})} | custom-call | flops 1000000000 | bytes 2097152 | tf_op jit(solution)/shard_map/finish_own/pallas_call | solution.py:528
  52.4 0.5 collective-permute-done.10.got_d
  53.0 0.2 collective-permute-done.11.got_c
  53.2 3.2 %uplift.1 = f32[3,512,512]{2,1,0:T(8,128)} custom-call(f32[72,128]{1,0:T(8,128)S(1)} %collective-permute-done.10.got_d, f32[72,128]{1,0:T(8,128)S(1)} %collective-permute-done.11.got_c, f32[512,512]{1,0:T(8,128)S(1)} %get-tuple-element.52.height, s32[512,512]{1,0:T(8,128)S(1)} %copy-done.1, ...), custom_call_target="tpu_custom_call", output_to_operand_aliasing={{}: (4, {})} | custom-call | flops 3000000000 | bytes 2097152 | tf_op jit(solution)/shard_map/uplift/pallas_call | solution.py:536
  (8 shorter events, 0.0 us)
Async XLA Ops:
  1.3 1.1 %copy-start.3 = (f32[180,1024]{1,0:T(8,128)S(1)}, f32[180,1024]{1,0:T(8,128)}, u32[]{:S(2)}) copy-start(f32[180,1024]{1,0:T(8,128)} %state.3) | copy-start | bytes 2211844
  2.5 1.0 %copy-start.5 = (f32[4,90,180]{2,0,1:T(4,128)S(1)}, f32[4,90,180]{2,0,1:T(4,128)}, u32[]{:S(2)}) copy-start(f32[4,90,180]{2,0,1:T(4,128)} %param.20) | copy-start | bytes 777604
  3.4 10.0 %copy-start.16 = (s32[4,1024]{1,0:T(4,128)S(1)}, s32[4,1024]{1,0:T(4,128)}, u32[]{:S(2)}) copy-start(s32[4,1024]{1,0:T(4,128)} %param.17) | copy-start | bytes 49156
  3.4 10.0 %copy-start.1 = (s32[512,512]{1,0:T(8,128)S(1)}, s32[512,512]{1,0:T(8,128)}, u32[]{:S(2)}) copy-start(s32[512,512]{1,0:T(8,128)} %wet.7) | copy-start | bytes 3145732
  3.4 10.0 %copy-start.2 = (f32[3,512,512]{2,1,0:T(8,128)S(1)}, f32[3,512,512]{2,1,0:T(8,128)}, u32[]{:S(2)}) copy-start(f32[3,512,512]{2,1,0:T(8,128)} %ocean.3) | copy-start | bytes 9437188
  3.4 10.1 %copy-start.6 = (f32[4,90,180]{2,0,1:T(4,128)S(1)}, f32[4,90,180]{2,0,1:T(4,128)}, u32[]{:S(2)}) copy-start(f32[4,90,180]{2,0,1:T(4,128)} %param.20) | copy-start | bytes 777604
  3.5 10.1 %copy-start.13 = (f32[180,4,90]{2,1,0:T(4,128)S(1)}, f32[180,4,90]{2,1,0:T(4,128)}, u32[]{:S(2)}) copy-start(f32[180,4,90]{2,1,0:T(4,128)} %lift.1) | copy-start | bytes 777604
  3.5 10.1 %copy-start.14 = (f32[180,180]{1,0:T(8,128)S(1)}, f32[180,180]{1,0:T(8,128)}, u32[]{:S(2)}) copy-start(f32[180,180]{1,0:T(8,128)} %volume.1) | copy-start | bytes 388804
  3.5 10.1 %copy-start.15 = (f32[90,90]{1,0:T(8,128)S(1)}, f32[90,90]{1,0:T(8,128)}, u32[]{:S(2)}) copy-start(f32[90,90]{1,0:T(8,128)} %flux.1) | copy-start | bytes 97204
  7.2 10.6 %collective-permute-start = (f32[512,128]{1,0:T(8,128)S(1)}, f32[512,128]{1,0:T(8,128)S(1)}, u32[]{:S(2)}, u32[]{:S(2)}) collective-permute-start(f32[512,128]{1,0:T(8,128)S(1)} %get-tuple-element.36), channel_id=1, source_target_pairs={{0,16},{1,2},{2,1},{3,4},{4,3},{5,6},{6,5},{7,8},{8,7},{9,10},{10,... | collective-permute-start | bytes 786440 | tf_op jit(solution)/shard_map/ppermute | solution.py:467
  11.5 7.8 %collective-permute-start.1 = (f32[512,128]{1,0:T(8,128)S(1)}, f32[512,128]{1,0:T(8,128)S(1)}, u32[]{:S(2)}, u32[]{:S(2)}) collective-permute-start(f32[512,128]{1,0:T(8,128)S(1)} %get-tuple-element.37), channel_id=1, source_target_pairs={{0,1},{1,0},{2,3},{3,2},{4,5},{5,4},{6,7},{7,6},{8,9},{9,8},{10,11... | collective-permute-start | bytes 786440 | tf_op jit(solution)/shard_map/ppermute | solution.py:468
  11.5 7.8 %collective-permute-start.2 = (f32[512,128]{1,0:T(8,128)S(1)}, f32[512,128]{1,0:T(8,128)S(1)}, u32[]{:S(2)}, u32[]{:S(2)}) collective-permute-start(f32[512,128]{1,0:T(8,128)S(1)} %get-tuple-element.38), channel_id=1, source_target_pairs={{0,112},{1,5},{2,6},{3,115},{4,116},{5,1},{6,2},{7,119},{8,120},{9... | collective-permute-start | bytes 786440 | tf_op jit(solution)/shard_map/ppermute | solution.py:469
  13.5 5.9 %collective-permute-start.3 = (f32[512,128]{1,0:T(8,128)S(1)}, f32[512,128]{1,0:T(8,128)S(1)}, u32[]{:S(2)}, u32[]{:S(2)}) collective-permute-start(f32[512,128]{1,0:T(8,128)S(1)} %get-tuple-element.39), channel_id=1, source_target_pairs={{0,16},{1,17},{2,18},{3,19},{4,20},{5,21},{6,22},{7,23},{8,24},{9,... | collective-permute-start | bytes 786440 | tf_op jit(solution)/shard_map/ppermute | solution.py:470
  13.5 5.8 %copy-start.4 = (f32[180,1024]{1,0:T(8,128)S(1)}, f32[180,1024]{1,0:T(8,128)}, u32[]{:S(2)}) copy-start(f32[180,1024]{1,0:T(8,128)} %state.3) | copy-start | bytes 2211844
  13.5 5.8 %copy-start.8 = (f32[1024]{0:T(1024)S(1)}, f32[1024]{0:T(1024)}, u32[]{:S(2)}) copy-start(f32[1024]{0:T(1024)} %param.19) | copy-start | bytes 12292
  19.3 11.4 %copy-start = (f32[512,512]{1,0:T(8,128)S(1)}, f32[512,512]{1,0:T(8,128)}, u32[]{:S(2)}) copy-start(f32[512,512]{1,0:T(8,128)} %depth.3) | copy-start | bytes 3145732
  26.6 9.6 %copy-start.7 = (f32[16,10,256]{2,0,1:T(8,128)S(1)}, f32[16,10,256]{2,0,1:T(8,128)}, u32[]{:S(2)}) copy-start(f32[16,10,256]{2,0,1:T(8,128)} %param.28) | copy-start | bytes 491524
  26.6 9.6 %copy-start.9 = (s32[256]{0:T(256)S(1)}, s32[256]{0:T(256)}, u32[]{:S(2)}) copy-start(s32[256]{0:T(256)} %param.24) | copy-start | bytes 3076
  26.6 9.6 %copy-start.10 = (s32[256,1]{0,1:T(1,128)S(1)}, s32[256,1]{0,1:T(1,128)}, u32[]{:S(2)}) copy-start(s32[256,1]{0,1:T(1,128)} %param.25) | copy-start | bytes 3076
  26.6 9.6 %copy-start.11 = (s32[256]{0:T(256)S(1)}, s32[256]{0:T(256)}, u32[]{:S(2)}) copy-start(s32[256]{0:T(256)} %param.26) | copy-start | bytes 3076
  26.6 9.6 %copy-start.12 = (s32[256]{0:T(256)S(1)}, s32[256]{0:T(256)}, u32[]{:S(2)}) copy-start(s32[256]{0:T(256)} %param.27) | copy-start | bytes 3076
  26.6 9.2 %collective-permute-start.4 = (f32[528,128]{1,0:T(8,128)S(1)}, f32[528,128]{1,0:T(8,128)S(1)}, u32[]{:S(2)}, u32[]{:S(2)}) collective-permute-start(f32[528,128]{1,0:T(8,128)S(1)} %get-tuple-element.42), channel_id=1, source_target_pairs={{0,16},{1,2},{2,1},{3,4},{4,3},{5,6},{6,5},{7,8},{8,7},{9,10},{10,... | collective-permute-start | bytes 811016 | tf_op jit(solution)/shard_map/ppermute | solution.py:467
  29.1 7.1 %collective-permute-start.5 = (f32[528,128]{1,0:T(8,128)S(1)}, f32[528,128]{1,0:T(8,128)S(1)}, u32[]{:S(2)}, u32[]{:S(2)}) collective-permute-start(f32[528,128]{1,0:T(8,128)S(1)} %get-tuple-element.43), channel_id=1, source_target_pairs={{0,1},{1,0},{2,3},{3,2},{4,5},{5,4},{6,7},{7,6},{8,9},{9,8},{10,11... | collective-permute-start | bytes 811016 | tf_op jit(solution)/shard_map/ppermute | solution.py:468
  29.1 7.1 %collective-permute-start.6 = (f32[528,128]{1,0:T(8,128)S(1)}, f32[528,128]{1,0:T(8,128)S(1)}, u32[]{:S(2)}, u32[]{:S(2)}) collective-permute-start(f32[528,128]{1,0:T(8,128)S(1)} %get-tuple-element.44), channel_id=1, source_target_pairs={{0,112},{1,5},{2,6},{3,115},{4,116},{5,1},{6,2},{7,119},{8,120},{9... | collective-permute-start | bytes 811016 | tf_op jit(solution)/shard_map/ppermute | solution.py:469
  30.1 6.1 %collective-permute-start.7 = (f32[528,128]{1,0:T(8,128)S(1)}, f32[528,128]{1,0:T(8,128)S(1)}, u32[]{:S(2)}, u32[]{:S(2)}) collective-permute-start(f32[528,128]{1,0:T(8,128)S(1)} %get-tuple-element.45), channel_id=1, source_target_pairs={{0,16},{1,17},{2,18},{3,19},{4,20},{5,21},{6,22},{7,23},{8,24},{9,... | collective-permute-start | bytes 811016 | tf_op jit(solution)/shard_map/ppermute | solution.py:470
  42.2 4.5 %collective-permute-start.8 = (f32[24,256]{1,0:T(8,128)S(1)}, f32[24,256]{1,0:T(8,128)S(1)}, u32[]{:S(2)}, u32[]{:S(2)}) collective-permute-start(f32[24,256]{1,0:T(8,128)S(1)} %get-tuple-element.48), channel_id=1, source_target_pairs={{0,112},{1,5},{2,6},{3,115},{4,116},{5,1},{6,2},{7,119},{8,120},{9... | collective-permute-start | bytes 73736 | tf_op jit(solution)/shard_map/ppermute | solution.py:524
  43.6 3.1 %collective-permute-start.9 = (f32[24,256]{1,0:T(8,128)S(1)}, f32[24,256]{1,0:T(8,128)S(1)}, u32[]{:S(2)}, u32[]{:S(2)}) collective-permute-start(f32[24,256]{1,0:T(8,128)S(1)} %get-tuple-element.49), channel_id=1, source_target_pairs={{0,16},{1,17},{2,18},{3,19},{4,20},{5,21},{6,22},{7,23},{8,24},{9,... | collective-permute-start | bytes 73736 | tf_op jit(solution)/shard_map/ppermute | solution.py:525
  46.8 6.1 %collective-permute-start.10 = (f32[72,128]{1,0:T(8,128)S(1)}, f32[72,128]{1,0:T(8,128)S(1)}, u32[]{:S(2)}, u32[]{:S(2)}) collective-permute-start(f32[72,128]{1,0:T(8,128)S(1)} %get-tuple-element.55), channel_id=1, source_target_pairs={{0,16},{1,2},{2,1},{3,4},{4,3},{5,6},{6,5},{7,8},{8,7},{9,10},{10,... | collective-permute-start | bytes 110600 | tf_op jit(solution)/shard_map/ppermute | solution.py:534
  49.2 4.0 %collective-permute-start.11 = (f32[72,128]{1,0:T(8,128)S(1)}, f32[72,128]{1,0:T(8,128)S(1)}, u32[]{:S(2)}, u32[]{:S(2)}) collective-permute-start(f32[72,128]{1,0:T(8,128)S(1)} %get-tuple-element.54.mine), channel_id=1, source_target_pairs={{0,1},{1,0},{2,3},{3,2},{4,5},{5,4},{6,7},{7,6},{8,9},{9,8},{10,11... | collective-permute-start | bytes 110600 | tf_op jit(solution)/shard_map/ppermute | solution.py:535

commit v4 on v3

--- a/solution.py
+++ b/solution.py
@@ -49,6 +49,7 @@
 
 PAIR_A = pairs_of(lambda r, c: (r ^ 1, c))
 PAIR_B = pairs_of(lambda r, c: (step_out(r), c) if 0 < r < N_ROW - 1 else ((r, c ^ 4) if c % 4 in (1, 2) else (N_ROW - 1 - r, c)))
+PAIR_B_SMALL = pairs_of(lambda r, c: (step_out(r), c) if 0 < r < N_ROW - 1 else (r, c ^ 1))
 PAIR_C = pairs_of(lambda r, c: (r, c ^ 1))
 PAIR_D = pairs_of(lambda r, c: (r, step_out(c)) if 0 < c < N_COL - 1 else (r ^ 1, c))
 
@@ -103,25 +104,23 @@
     return 1 - odd_row, odd_row, 3 - odd_col, 2 + odd_col
 
 
-def gather_rows(index, base, table, out, rows):
-    unroll = 16
-
+def gather_rows(index, which, table, out, rows):
     def step(j, carry):
-        to = j * (unroll * 8)
-        for u in range(unroll):
-            at = pl.multiple_of(to + u * 8, 8)
-            got = [table[pl.ds(index[base + at + t], 1), :] for t in range(8)]
-            out[pl.ds(at, 8), :] = jnp.concatenate(got, axis=0)
+        to = j * LANES
+        base = j * (4 * LANES) + which * LANES
+        for u in range(0, LANES, 8):
+            got = [table[pl.ds(index[base + u + t], 1), :] for t in range(8)]
+            out[pl.ds(pl.multiple_of(to + u, 8), 8), :] = jnp.concatenate(got, axis=0)
         return carry
 
-    lax.fori_loop(0, rows // 8 // unroll, step, 0)
+    lax.fori_loop(0, rows // LANES, step, 0)
 
 
 def gather_sends(send, table, blocks, extras, outs, sems):
     where = slots()
     copies = []
     for i in (3, 2, 1, 0):
-        gather_rows(send, where[i] * SEND, table, blocks[i], SEND)
+        gather_rows(send, where[i], table, blocks[i], SEND)
         if extras is not None:
             if i >= 2:
                 blocks[i][pl.ds(0, SEND), :] = blocks[i][pl.ds(0, SEND), :] + extras[i][...]
@@ -146,8 +145,13 @@
         table[pl.ds(f * ELEMS + at, CHUNK), :] = traces[:, f * LANES : (f + 1) * LANES]
 
 
-def first_kernel(state, extract, send, table, ek, out_d, out_c, out_b, out_a, full, padded, ba, bb, bc, bd, sems):
-    full[...] = jnp.zeros(full.shape, F32)
+def blank_kernel(blank):
+    blank[...] = jnp.zeros(blank.shape, F32)
+
+
+def first_kernel(
+    state, extract, send, blank, table, ek, out_d, out_c, out_b, out_a, full, padded, ba, bb, bc, bd, sems
+):
     for f in range(4):
         full[pl.ds(f * LANES, NF), pl.ds(0, NQ)] = extract[:, f, :]
     ek[...] = right_parts(full[...], 1)
@@ -223,7 +227,8 @@
 def gather_part(index, table, near, at):
     for f in range(4):
         for u in range(0, SIZE, 8):
-            got = [table[pl.ds(index[f * ELEMS + at + u + t], 1), :] for t in range(8)]
+            base = 4 * at + (u // LANES) * (4 * LANES) + f * LANES + u % LANES
+            got = [table[pl.ds(index[base + t], 1), :] for t in range(8)]
             near[pl.ds(f * SIZE + u, 8), :] = jnp.concatenate(got, axis=0)
 
 
@@ -281,7 +286,7 @@
 
 
 def last_kernel(
-    state, jac, extract, v2k, l2k, nbr, sf_face, sf_dest, sf_row, sf_col, weights, table_in, in_d, in_c, in_b, in_a,
+    state, jac, extract, v2k, l2k, nbr, sf_face, pick, into, sf_row, sf_col, weights, table_in, in_d, in_c, in_b, in_a,
     new_state, table, stay, box_a, box_b,
     padded, near0, near1, new_local, sems, out_sem,
 ):
@@ -299,11 +304,9 @@
     leaving.start()
     ops = jnp.concatenate([extract[20:30, f, :] for f in range(4)], axis=0)
     on_faces = dot3(split(ops), split(new_local[...]))
-    elem = sf_face[...] % ELEMS
     face = sf_face[...] // ELEMS
-    pick = (lax.broadcasted_iota(jnp.int32, (ELEMS, SF), 0) == elem).astype(BF16)
     fh, fl = split(on_faces)
-    chosen = dot(fh, pick) + dot(fl, pick)
+    chosen = dot(fh, pick[...]) + dot(fl, pick[...])
     vz = jnp.zeros((10, SF), F32)
     for f in range(4):
         vz = vz + jnp.where(face == f, chosen[f * 10 : (f + 1) * 10, :], 0.0)
@@ -313,6 +316,17 @@
     values = jnp.concatenate(
         [values, sf_row[...].astype(F32), sf_col[...].astype(F32), jnp.zeros((6, SF), F32)], axis=0
     )
+    vh, vl = split(values)
+    box = dot(vh, into[...], NT) + dot(vl, into[...], NT)
+    stay[...] = box[:, :GROUP]
+    box_a[...] = box[:, GROUP : 2 * GROUP]
+    box_b[...] = box[:, 2 * GROUP :]
+    leaving.wait()
+
+
+def place_faces(sf_face, sf_dest, pick, into):
+    elem = sf_face[...] % ELEMS
+    pick[...] = (lax.broadcasted_iota(jnp.int32, (ELEMS, SF), 0) == elem).astype(BF16)
     row, col, odd_row, odd_col = parities()
     dest = sf_dest[...]
     dr = dest // N_COL - row
@@ -330,16 +344,11 @@
     ranks = dot(owners.astype(BF16), before)
     rank = jnp.sum(ranks * owners, axis=0, keepdims=True).astype(jnp.int32)
     place = group_r * GROUP + group_c * CAP + rank
-    into = (lax.broadcasted_iota(jnp.int32, (3 * GROUP, SF), 0) == place).astype(BF16)
-    vh, vl = split(values)
-    box = dot(vh, into, NT) + dot(vl, into, NT)
-    stay[...] = box[:, :GROUP]
-    box_a[...] = box[:, GROUP : 2 * GROUP]
-    box_b[...] = box[:, 2 * GROUP :]
-    leaving.wait()
-
-
-def stencil_kernel(ocean, wet, depth, after, height, speeds, fields):
+    into[...] = (lax.broadcasted_iota(jnp.int32, (3 * GROUP, SF), 0) == place).astype(BF16)
+
+
+def stencil_kernel(ocean, wet, depth, sf_face, sf_dest, after, height, speeds, pick, into, fields):
+    place_faces(sf_face, sf_dest, pick, into)
     wet_f = wet[...].astype(F32)
     for f in range(3):
         fields[f, pl.ds(0, 8), :] = jnp.zeros((8, TILE), F32)
@@ -402,15 +411,14 @@
         speeds[1, :, here] = speeds[1, :, here] + mask * (0.25 * v)
 
 
-def uplift_of(data):
+def uplift_of(data, first=0, columns=TILE):
     total = data.shape[1]
-    at = lax.broadcasted_iota(jnp.int32, (TILE, total), 0)
-    d_row = at - data[16:17, :].astype(jnp.int32)
-    d_col = at - data[17:18, :].astype(jnp.int32)
+    d_row = lax.broadcasted_iota(jnp.int32, (TILE, total), 0) - data[16:17, :].astype(jnp.int32)
+    d_col = lax.broadcasted_iota(jnp.int32, (columns, total), 0) + (first - data[17:18, :].astype(jnp.int32))
     masks = [d_col == b for b in range(4)]
     added = None
     for a in range(4):
-        spread = jnp.zeros((TILE, total), F32)
+        spread = jnp.zeros((columns, total), F32)
         for b in range(4):
             spread = jnp.where(masks[b], data[4 * a + b : 4 * a + b + 1, :], spread)
         pick = (d_row == a).astype(BF16)
@@ -419,9 +427,20 @@
     return added
 
 
-def finish_own_kernel(
-    mine, wet, depth, height_in, speeds_in, in_d, in_c, in_b, in_a, height, speeds, out,
-    ga, gb, gc, gd, sems, out_sem,
+def side_by_side(blocks, first):
+    half = lax.broadcasted_iota(jnp.int32, (24, LANES), 1) < CAP
+
+    def at_lane(x, lane):
+        if x is None:
+            return jnp.zeros((24, LANES), F32)
+        return x if lane == first else pltpu.roll(x, CAP, 1)
+
+    pairs = [(blocks[i], blocks[i + 1] if i + 1 < len(blocks) else None) for i in range(0, len(blocks), 2)]
+    return jnp.concatenate([jnp.where(half, at_lane(x, 0), at_lane(y, CAP)) for x, y in pairs], axis=1)
+
+
+def finish_edges_kernel(
+    stay, wet, depth, height_in, speeds_in, in_d, in_c, in_b, in_a, height, speeds, ga, gb, gc, gd, sems,
 ):
     arriving = [
         pltpu.make_async_copy(in_a.at[pl.ds(SEND, EDGE), :], ga, sems.at[0]),
@@ -434,29 +453,30 @@
     for copy in arriving:
         copy.wait()
     add_edges(height, speeds, wet, depth, ga, gb, gc, gd)
+    added = uplift_of(side_by_side([stay[:, :LANES]], 0))
+    height[...] = height[...] + added * wet[...].astype(F32)
+
+
+def uplift_own_kernel(got_b, got_a, wet, height_in, speeds, height, out, out_sem):
     leaving = pltpu.make_async_copy(speeds, out.at[pl.ds(1, 2)], out_sem)
     leaving.start()
-    half = lax.broadcasted_iota(jnp.int32, (24, LANES), 1) < CAP
-    first = jnp.where(half, mine[pl.ds(0, 24), :], pltpu.roll(mine[pl.ds(24, 24), :], CAP, 1))
-    second = jnp.where(half, mine[pl.ds(48, 24), :], 0.0)
-    added = uplift_of(jnp.concatenate([first, second], axis=1))
+    added = uplift_of(side_by_side([got_b[:, :LANES], got_a[:, :LANES]], 0))
     height[...] = height[...] + added * wet[...].astype(F32)
     leaving.wait()
 
 
-def uplift_kernel(got_d, got_c, height, wet, whole, out, plane, sems):
+def uplift_far_kernel(got_d, got_c, wet, height, whole, out, plane, sems):
     half = lax.broadcasted_iota(jnp.int32, (24, LANES), 1) < CAP
-    added = uplift_of(jnp.concatenate(
+    data = jnp.concatenate(
         [jnp.where(half, got_d[pl.ds(24 * g, 24), :], got_c[pl.ds(24 * g, 24), :]) for g in range(3)], axis=1
-    ))
-    size = 128
+    )
+    size = TILE // 2
     copies = []
-    for part in range(TILE // size):
-        at = part * size
-        plane[pl.ds(at, size), :] = (
-            height[pl.ds(at, size), :] + added[at : at + size] * wet[pl.ds(at, size), :].astype(F32)
-        )
-        copy = pltpu.make_async_copy(plane.at[pl.ds(at, size), :], out.at[0, pl.ds(at, size), :], sems.at[part])
+    for part in range(2):
+        here = pl.ds(part * size, size)
+        added = uplift_of(data, part * size, size)
+        plane[:, here] = height[:, here] + added * wet[:, here].astype(F32)
+        copy = pltpu.make_async_copy(plane.at[:, here], out.at[0, :, here], sems.at[part])
         copy.start()
         copies.append(copy)
     for copy in copies:
@@ -471,12 +491,16 @@
     return d, c, b, a
 
 
+def stored_order(index):
+    return index.reshape(4, -1, LANES).transpose(1, 0, 2).reshape(-1)
+
+
 def body(
     state, neighbours, send_faces, jacobian, face_extract, volume_op, flux_matrix, lift_op,
     sf_face, sf_dest, sf_row, sf_col, sf_weights, ocean, depth, wet,
 ):
-    nbr = neighbours.reshape(POOL)
-    send = send_faces.reshape(4 * SEND)
+    nbr = stored_order(neighbours)
+    send = stored_order(send_faces)
     jac = jacobian.reshape(1, ELEMS)
     extract = face_extract.transpose(1, 0, 2)
     weights = sf_weights.transpose(1, 0, 2)
@@ -487,11 +511,13 @@
     padded = pltpu.VMEM((KP, ELEMS), F32)
     near = [pltpu.VMEM((4 * SIZE, LANES), F32)] * 2
 
-    table, ek, sd, sc, sb, sa = call(
-        first_kernel, "traces_first", [VMEM, VMEM, SMEM],
-        [table_o, ((4 * LANES, 3 * KP), BF16, VMEM)] + [(short, F32, ANY)] * 4,
-        [pltpu.VMEM((4 * LANES, KP), F32), padded] + [pltpu.VMEM(short, F32)] * 4 + [dma((4,))], flops=10**10,
-    )(state, extract, send)
+    blank_o = ((4 * LANES, KP), F32, VMEM)
+    (blank,) = call(blank_kernel, "blank", [], [blank_o], flops=10**10)()
+    table, ek, sd, sc, sb, sa, _ = call(
+        first_kernel, "traces_first", [VMEM, VMEM, SMEM, VMEM],
+        [table_o, ((4 * LANES, 3 * KP), BF16, VMEM)] + [(short, F32, ANY)] * 4 + [blank_o],
+        [padded] + [pltpu.VMEM(short, F32)] * 4 + [dma((4,))], aliases={3: 6}, flops=10**10,
+    )(state, extract, send, blank)
     recv = exchange(sa, sb, sc, sd)
     v2k, l2k, ea, eb, ec, ed = call(
         prepare_kernel, "prepare", [VMEM] * 6,
@@ -506,38 +532,44 @@
         aliases={11: 1},
     )(state, jac, ek, v2k, l2k, ea, eb, ec, ed, nbr, send, table, *recv)
     recv = exchange(sa, sb, sc, sd)
-    height, speeds = call(
-        stencil_kernel, "stencil", [VMEM] * 4,
-        [((TILE, TILE), F32, VMEM), ((2, TILE, TILE), F32, VMEM)],
+    height, speeds, pick, into = call(
+        stencil_kernel, "stencil", [VMEM] * 6,
+        [
+            ((TILE, TILE), F32, VMEM), ((2, TILE, TILE), F32, VMEM),
+            ((ELEMS, SF), BF16, VMEM), ((3 * GROUP, SF), BF16, VMEM),
+        ],
         [pltpu.VMEM((3, TILE + 16, TILE), F32)], flops=10**9,
-    )(ocean, wet, depth, state[:8, :LANES])
+    )(ocean, wet, depth, sf_face.reshape(1, SF), sf_dest.reshape(1, SF), state[:8, :LANES])
     box_o = ((24, GROUP), F32, VMEM)
     state, _, stay, box_a, box_b = call(
-        last_kernel, "step_last", [VMEM] * 5 + [SMEM] + [VMEM] * 6 + [ANY] * 4,
+        last_kernel, "step_last", [VMEM] * 5 + [SMEM] + [VMEM] * 7 + [ANY] * 4,
         [((NQ, ELEMS), F32, ANY), table_o, box_o, box_o, box_o],
         [padded] + near + [pltpu.VMEM((NQ, ELEMS), F32), dma((4,)), dma(())],
-        aliases={11: 1},
+        aliases={12: 1},
     )(
-        state, jac, extract, v2k, l2k, nbr, sf_face.reshape(1, SF), sf_dest.reshape(1, SF),
+        state, jac, extract, v2k, l2k, nbr, sf_face.reshape(1, SF), pick, into,
         sf_row.reshape(1, SF), sf_col.reshape(1, SF), weights, table, *recv,
     )
-    got_b = lax.ppermute(box_b, BOTH, PAIR_B)
+    got_b = lax.ppermute(box_b, BOTH, PAIR_B_SMALL)
     got_a = lax.ppermute(box_a, BOTH, PAIR_A)
+    plane_o = ((TILE, TILE), F32, VMEM)
+    height, speeds = call(
+        finish_edges_kernel, "finish_edges", [VMEM] * 5 + [ANY] * 4,
+        [plane_o, ((2, TILE, TILE), F32, VMEM)],
+        [pltpu.VMEM((EDGE, LANES), F32)] * 2 + [pltpu.VMEM(short, F32)] * 2 + [dma((4,))],
+        aliases={3: 0, 4: 1}, flops=2 * 10**9,
+    )(stay, wet, depth, height, speeds, *recv)
     mine = jnp.concatenate([stay, got_b, got_a], axis=0)
-    own = mine[:, :LANES]
-    height, _, ocean_out = call(
-        finish_own_kernel, "finish_own", [VMEM] * 5 + [ANY] * 4,
-        [((TILE, TILE), F32, VMEM), ((2, TILE, TILE), F32, VMEM), ((3, TILE, TILE), F32, ANY)],
-        [pltpu.VMEM((EDGE, LANES), F32)] * 2 + [pltpu.VMEM(short, F32)] * 2 + [dma((4,)), dma(())],
-        aliases={3: 0, 4: 1}, flops=10**9,
-    )(own, wet, depth, height, speeds, *recv)
     got_d = lax.ppermute(mine[:, LANES:], BOTH, PAIR_D)
-    got_c = lax.ppermute(own, BOTH, PAIR_C)
+    got_c = lax.ppermute(jnp.pad(mine[:, :LANES], ((0, 8), (0, 0))), BOTH, PAIR_C)
+    height, ocean_out = call(
+        uplift_own_kernel, "uplift_own", [VMEM] * 5, [plane_o, ((3, TILE, TILE), F32, ANY)], [dma(())],
+        aliases={3: 0}, flops=10**9,
+    )(got_b, got_a, wet, height, speeds)
     (ocean_out,) = call(
-        uplift_kernel, "uplift", [VMEM] * 4 + [ANY], [((3, TILE, TILE), F32, ANY)],
-        [pltpu.VMEM((TILE, TILE), F32), dma((4,))],
-        aliases={4: 0}, flops=3 * 10**9,
-    )(got_d, got_c, height, wet, ocean_out)
+        uplift_far_kernel, "uplift_far", [VMEM] * 4 + [ANY], [((3, TILE, TILE), F32, ANY)],
+        [pltpu.VMEM((TILE, TILE), F32), dma((2,))], aliases={4: 0}, flops=3 * 10**9,
+    )(got_d, got_c, wet, height, ocean_out)
     return state, ocean_out
 
 

time: 56.8 us -> 54 us (0.951)
  local copies, waits for them, and re-layouts: 2.91 us -> 1.24 us
  waiting for transfers between devices: 8.24 us -> 7.41 us
    ppermute x2, waiting for transfers between devices: 3.15 us -> 1.12 us  [the longest x1 0.81 us: body(): got_b = lax.ppermute(box_b, BOTH, PAIR_B_SMALL)]
    ppermute x1, waiting for transfers between devices: 0.54 us -> 2.35 us  [body(): got_d = lax.ppermute(mine[:, LANES:], BOTH, PAIR_D)]
    unnamed x38 -> x34, local copies, waits for them, and re-layouts: 2.9 us -> 1.23 us
    ppermute x2, waiting for transfers between devices: 2.71 us -> 2.11 us  [exchange(): d = lax.ppermute(d, BOTH, PAIR_D)]
    pallas_call x5 -> x7, Pallas kernels: 20 us -> 19.8 us  [the longest x1 5.51 us: body(): call(last_kernel, 'step_last', [VMEM] * 5 + [SMEM] + [VMEM] * 7 + [ANY] *...]
  transfers between devices with their start and end apart: 12 -> 12, of which waited for: 7 -> 7; matrix products, arithmetic and copies ran while one was open for 0% -> 0% of each run, Pallas kernels for 17% -> 19%
where the time goes in v4:
time: 54 us; the launch traced here: 53.9 us
  Pallas kernels  29.8 us (55%)
  starting transfers between devices  14.4 us (27%)
  waiting for transfers between devices  7.41 us (14%)
  local copies, waits for them, and re-layouts  1.24 us (2%)
  between operations  1.04 us (2%)
    pallas_call x1, Pallas kernels, body(): call(middle_kernel, 'step_first', [VMEM] * 9 + [SMEM] * 2 + [VMEM] + [ANY...  7.15 us
    ppermute x2, starting transfers between devices, exchange(): d = lax.ppermute(d, BOTH, PAIR_D)  6.76 us
    pallas_call x1, Pallas kernels, body(): call(last_kernel, 'step_last', [VMEM] * 5 + [SMEM] + [VMEM] * 7 + [ANY] *...  5.51 us
    pallas_call x1, Pallas kernels, body(): call(stencil_kernel, 'stencil', [VMEM] * 6, [((TILE, TILE), F32, VMEM), (...  4.51 us
    pallas_call x1, Pallas kernels, body(): call(first_kernel, 'traces_first', [VMEM, VMEM, SMEM, VMEM], [table_o, ((...  3.7 us
    pallas_call x1, Pallas kernels, body(): call(uplift_far_kernel, 'uplift_far', [VMEM] * 4 + [ANY], [((3, TILE, TIL...  3.33 us
    ppermute x2, starting transfers between devices, exchange(): b = lax.ppermute(b, BOTH, PAIR_B)  2.98 us
    pallas_call x1, Pallas kernels, body(): call(prepare_kernel, 'prepare', [VMEM] * 6, [((NQ, 3 * KP), BF16, VMEM),...  2.84 us
  transfers between devices with their start and end apart: 12, of which 7 were waited for; matrix products, arithmetic and copies ran while one was open for 0% of the time, Pallas kernels for 19%

profile of v4, /device:TPU:24, one launch (start us, length us, event | category | flops | bytes accessed | tf_op | source)
XLA Modules:
  0.0 53.9 jit_solution(10854913461856414153)
XLA Ops:
  0.6 0.0 copy-start.3
  0.6 0.0 copy-start.4
  0.6 0.0 copy-start.8
  0.7 1.0 %copy-done.3 = f32[180,1024]{1,0:T(8,128)S(1)} copy-done((f32[180,1024]{1,0:T(8,128)S(1)}, f32[180,1024]{1,0:T(8,128)}, u32[]{:S(2)}) %copy-start.3) | copy-done | bytes 737304
  1.8 0.1 copy-done.4
  1.8 0.0 copy-done.8
  1.8 0.0 copy-start
  1.8 0.0 copy-start.1
  1.9 0.0 copy-start.13
  1.9 0.0 copy-start.14
  1.9 0.0 copy-start.15
  1.9 3.7 %traces_first.1 = (f32[6144,128]{1,0:T(8,128)S(1)}, bf16[512,768]{1,0:T(8,128)(2,1)S(1)}, f32[512,128]{1,0:T(8,128)S(1)}, f32[512,128]{1,0:T(8,128)S(1)}, f32[51...) custom-call(f32[180,1024]{1,0:T(8,128)S(1)} %copy-done.3, ...), custom_call_target="tpu_custom_call", output_to_operand_aliasing={{6}: (3, {})} | custom-call | flops 10000000000 | bytes 2097152 | tf_op jit(solution)/shard_map/traces_first/pallas_call | solution.py:516
  5.6 4.3 %collective-permute-start = (f32[512,128]{1,0:T(8,128)S(1)}, f32[512,128]{1,0:T(8,128)S(1)}, u32[]{:S(2)}, u32[]{:S(2)}) collective-permute-start(f32[512,128]{1,0:T(8,128)S(1)} %get-tuple-element.40), channel_id=1, source_target_pairs={{0,16},{1,2},{2,1},{3,4},{4,3},{5,6},{6,5},{7,8},{8,7},{9,10},{10,... | collective-permute-start | bytes 786440 | tf_op jit(solution)/shard_map/ppermute | solution.py:487
  9.9 0.0 collective-permute-start.1
  9.9 1.9 %collective-permute-start.2 = (f32[512,128]{1,0:T(8,128)S(1)}, f32[512,128]{1,0:T(8,128)S(1)}, u32[]{:S(2)}, u32[]{:S(2)}) collective-permute-start(f32[512,128]{1,0:T(8,128)S(1)} %get-tuple-element.42), channel_id=1, source_target_pairs={{0,112},{1,5},{2,6},{3,115},{4,116},{5,1},{6,2},{7,119},{8,120},{9... | collective-permute-start | bytes 786440 | tf_op jit(solution)/shard_map/ppermute | solution.py:489
  11.8 0.0 copy-start.6
  11.8 0.0 copy-start.7
  11.8 0.0 collective-permute-start.3
  11.8 0.0 copy-done
  11.8 0.0 copy-done.1
  11.8 0.0 copy-done.13
  11.8 0.0 copy-done.14
  11.8 0.0 copy-done.15
  11.9 2.8 %prepare.1 = (bf16[180,768]{1,0:T(8,128)(2,1)S(1)}, bf16[180,1536]{1,0:T(8,128)(2,1)S(1)}, f32[16,128]{1,0:T(8,128)S(1)}, f32[16,128]{1,0:T(8,128)S(1)}, f32[512,128]{1,0:T(8,128)S(1)}, /*index=5*/f32[512,128]{1,0:T(8,128)S(1)}) custom-call(f32[90,4,180]{2,1,0:T(4,128)S(1)} %bitcast.18, f32[180,180]{1,0:T(8,128)S(1)} %copy-done.14, f32[90,90]{1,0:T(8,128)S(1)} %copy-done.15, ...), custom_call_target="tpu_custom_call" | custom-call | flops 5000000000 | bytes 2097152 | tf_op jit(solution)/shard_map/prepare/pallas_call | solution.py:522
  14.7 1.5 %collective-permute-done.in_d = f32[512,128]{1,0:T(8,128)S(1)} collective-permute-done((f32[512,128]{1,0:T(8,128)S(1)}, f32[512,128]{1,0:T(8,128)S(1)}, u32[]{:S(2)}, u32[]{:S(2)}) %collective-permute-start) | collective-permute-done | bytes 262176 | tf_op jit(solution)/shard_map/ppermute | solution.py:487
  16.2 1.5 %collective-permute-done.1.in_c = f32[512,128]{1,0:T(8,128)S(1)} collective-permute-done((f32[512,128]{1,0:T(8,128)S(1)}, f32[512,128]{1,0:T(8,128)S(1)}, u32[]{:S(2)}, u32[]{:S(2)}) %collective-permute-start.1) | collective-permute-done | bytes 262176 | tf_op jit(solution)/shard_map/ppermute | solution.py:488
  17.6 0.0 collective-permute-done.2.in_b
  17.7 0.0 collective-permute-done.3.in_a
  17.7 0.0 copy-done.6
  17.7 0.0 copy-done.7
  17.7 0.0 copy-start.2
  17.7 0.0 copy-start.9
  17.7 0.0 copy-start.12
  17.7 7.1 %step_first.1 = (f32[180,1024]{1,0:T(8,128)S(1)}, f32[6144,128]{1,0:T(8,128)S(1)}, f32[528,128]{1,0:T(8,128)S(1)}, f32[528,128]{1,0:T(8,128)S(1)}, f32[528,128]{1,0:T(8,128)S(1)}, /*index=5*/f32[528,128]{1,0:T(8,128)S(1)}) custom-call(f32[180,1024]{1,0:T(8,128)S(1)} %copy-done.3, f32[1,1024]{1,0:T(1,128)S(1)} %bitcast.23, ...), custom_call_target="tpu_custom_call", output_to_operand_aliasing={{1}: (11, {})} | custom-call | bytes 2097152 | tf_op jit(solution)/shard_map/step_first/pallas_call | solution.py:528
  24.9 0.0 copy-start.5
  24.9 0.0 copy-start.10
  24.9 0.0 copy-start.11
  24.9 2.5 %collective-permute-start.4 = (f32[528,128]{1,0:T(8,128)S(1)}, f32[528,128]{1,0:T(8,128)S(1)}, u32[]{:S(2)}, u32[]{:S(2)}) collective-permute-start(f32[528,128]{1,0:T(8,128)S(1)} %get-tuple-element.48), channel_id=1, source_target_pairs={{0,16},{1,2},{2,1},{3,4},{4,3},{5,6},{6,5},{7,8},{8,7},{9,10},{10,... | collective-permute-start | bytes 811016 | tf_op jit(solution)/shard_map/ppermute | solution.py:487
  27.4 0.0 collective-permute-start.5
  27.4 1.1 %collective-permute-start.6 = (f32[528,128]{1,0:T(8,128)S(1)}, f32[528,128]{1,0:T(8,128)S(1)}, u32[]{:S(2)}, u32[]{:S(2)}) collective-permute-start(f32[528,128]{1,0:T(8,128)S(1)} %get-tuple-element.50), channel_id=1, source_target_pairs={{0,112},{1,5},{2,6},{3,115},{4,116},{5,1},{6,2},{7,119},{8,120},{9... | collective-permute-start | bytes 811016 | tf_op jit(solution)/shard_map/ppermute | solution.py:489
  28.4 0.5 collective-permute-start.7
  29.0 0.0 copy-done.2
  29.0 0.0 copy-done.9
  29.0 0.0 copy-done.12
  29.0 4.5 %stencil.1 = (f32[512,512]{1,0:T(8,128)S(1)}, f32[2,512,512]{2,1,0:T(8,128)S(1)}, bf16[1024,256]{1,0:T(8,128)(2,1)S(1)}, bf16[768,256]{1,0:T(8,128)(2,1)S(1)}) custom-call(f32[3,512,512]{2,1,0:T(8,128)S(1)} %copy-done.1, s32[512,512]{1,0:T(8,128)S(1)} %copy-done, f32[512,512]{1,0:T(8,128)S(1)} %copy-done.2, s32[1,256]{1,0:T(1,128)S(1)} %bitcast.27, ...), custom_call_target="tpu_custom_call" | custom-call | flops 1000000000 | bytes 2097152 | tf_op jit(solution)/shard_map/stencil/pallas_call | solution.py:535
  33.5 0.6 %collective-permute-done.4.in_d = f32[528,128]{1,0:T(8,128)S(1)} collective-permute-done((f32[528,128]{1,0:T(8,128)S(1)}, f32[528,128]{1,0:T(8,128)S(1)}, u32[]{:S(2)}, u32[]{:S(2)}) %collective-permute-start.4) | collective-permute-done | bytes 270368 | tf_op jit(solution)/shard_map/ppermute | solution.py:487
  34.1 0.3 collective-permute-done.5.in_c
  34.4 0.0 collective-permute-done.6.in_b
  34.5 0.0 collective-permute-done.7.in_a
  34.5 0.0 copy-done.5
  34.5 0.0 copy-done.10
  34.5 0.0 copy-done.11
  34.5 5.5 %step_last.1 = (f32[180,1024]{1,0:T(8,128)}, f32[6144,128]{1,0:T(8,128)S(1)}, f32[24,256]{1,0:T(8,128)S(1)}, f32[24,256]{1,0:T(8,128)S(1)}, f32[24,256]{1,0:T(8,128)S(1)}) custom-call(f32[180,1024]{1,0:T(8,128)S(1)} %get-tuple-element.44.state, f32[1,1024]{1,0:T(1,128)S(1)} %bitcast.24, ...), custom_call_target="tpu_custom_call", output_to_operand_aliasing={{1}: (12, {})} | custom-call | bytes 2097152 | tf_op jit(solution)/shard_map/step_last/pallas_call | solution.py:544
  40.0 1.5 %collective-permute-start.8 = (f32[24,256]{1,0:T(8,128)S(1)}, f32[24,256]{1,0:T(8,128)S(1)}, u32[]{:S(2)}, u32[]{:S(2)}) collective-permute-start(f32[24,256]{1,0:T(8,128)S(1)} %get-tuple-element.54), channel_id=1, source_target_pairs={{0,1},{1,0},{2,3},{3,2},{4,5},{5,4},{6,7},{7,6},{8,9},{9,8},{10,11... | collective-permute-start | bytes 73736 | tf_op jit(solution)/shard_map/ppermute | solution.py:553
  41.5 0.2 collective-permute-start.9
  41.6 1.4 %finish_edges.1 = (f32[512,512]{1,0:T(8,128)S(1)}, f32[2,512,512]{2,1,0:T(8,128)S(1)}) custom-call(f32[24,256]{1,0:T(8,128)S(1)} %get-tuple-element.53.stay, s32[512,512]{1,0:T(8,128)S(1)} %copy-done, f32[512,512]{1,0:T(8,128)S(1)} %copy-done.2, f32[512,512]{1,0:T(8,128)S(1)} %get-tuple-element.56.height_in, ...), custom_call_target="tpu_custom_call", output_to_operand_aliasing={{0}: (3, {}), {1}: (4, {})} | custom-call | flops 2000000000 | bytes 2097152 | tf_op jit(solution)/shard_map/finish_edges/pallas_call | solution.py:556
  43.1 0.8 %collective-permute-done.8.got_b = f32[24,256]{1,0:T(8,128)S(1)} collective-permute-done((f32[24,256]{1,0:T(8,128)S(1)}, f32[24,256]{1,0:T(8,128)S(1)}, u32[]{:S(2)}, u32[]{:S(2)}) %collective-permute-start.8) | collective-permute-done | bytes 24608 | tf_op jit(solution)/shard_map/ppermute | solution.py:553
  43.9 0.0 collective-permute-done.9.got_a
  43.9 2.5 %collective-permute-start.10 = (f32[72,128]{1,0:T(8,128)S(1)}, f32[72,128]{1,0:T(8,128)S(1)}, u32[]{:S(2)}, u32[]{:S(2)}) collective-permute-start(f32[72,128]{1,0:T(8,128)S(1)} %get-tuple-element.63), channel_id=1, source_target_pairs={{0,16},{1,2},{2,1},{3,4},{4,3},{5,6},{6,5},{7,8},{8,7},{9,10},{10,... | collective-permute-start | bytes 110600 | tf_op jit(solution)/shard_map/ppermute | solution.py:563
  46.4 0.0 collective-permute-start.11
  46.4 1.3 %uplift_own.1 = (f32[512,512]{1,0:T(8,128)S(1)}, f32[3,512,512]{2,1,0:T(8,128)}) custom-call(f32[24,256]{1,0:T(8,128)S(1)} %collective-permute-done.8.got_b, f32[24,256]{1,0:T(8,128)S(1)} %collective-permute-done.9.got_a, s32[512,512]{1,0:T(8,128)S(1)} %copy-done, f32[512,512]{1,0:T(8,128)S(1)} %get-tuple-element.58.height_in, ...), custom_call_target="tpu_custom_call", output_to_operand_aliasing={{0}: (3, {})} | custom-call | flops 1000000000 | bytes 2097152 | tf_op jit(solution)/shard_map/uplift_own/pallas_call | solution.py:565
  47.7 2.4 %collective-permute-done.10.got_d = f32[72,128]{1,0:T(8,128)S(1)} collective-permute-done((f32[72,128]{1,0:T(8,128)S(1)}, f32[72,128]{1,0:T(8,128)S(1)}, u32[]{:S(2)}, u32[]{:S(2)}) %collective-permute-start.10) | collective-permute-done | bytes 36896 | tf_op jit(solution)/shard_map/ppermute | solution.py:563
  50.1 0.3 collective-permute-done.11.got_c
  50.4 3.3 %uplift_far.1 = f32[3,512,512]{2,1,0:T(8,128)} custom-call(f32[72,128]{1,0:T(8,128)S(1)} %collective-permute-done.10.got_d, f32[80,128]{1,0:T(8,128)S(1)} %collective-permute-done.11.got_c, s32[512,512]{1,0:T(8,128)S(1)} %copy-done, f32[512,512]{1,0:T(8,128)S(1)} %get-tuple-element.60.height, ...), custom_call_target="tpu_custom_call", output_to_operand_aliasing={{}: (4, {})} | custom-call | flops 3000000000 | bytes 2097152 | tf_op jit(solution)/shard_map/uplift_far/pallas_call | solution.py:569
  (7 shorter events, 0.1 us)
Async XLA Ops:
  0.6 1.1 %copy-start.3 = (f32[180,1024]{1,0:T(8,128)S(1)}, f32[180,1024]{1,0:T(8,128)}, u32[]{:S(2)}) copy-start(f32[180,1024]{1,0:T(8,128)} %state.3) | copy-start | bytes 2211844
  0.6 1.2 %copy-start.4 = (f32[4,90,180]{2,0,1:T(4,128)S(1)}, f32[4,90,180]{2,0,1:T(4,128)}, u32[]{:S(2)}) copy-start(f32[4,90,180]{2,0,1:T(4,128)} %param.20) | copy-start | bytes 777604
  0.6 1.2 %copy-start.8 = (s32[4,512]{1,0:T(4,128)S(1)}, s32[4,512]{1,0:T(4,128)}, u32[]{:S(2)}) copy-start(s32[4,512]{1,0:T(4,128)} %param.18) | copy-start | bytes 24580
  1.8 10.0 %copy-start = (s32[512,512]{1,0:T(8,128)S(1)}, s32[512,512]{1,0:T(8,128)}, u32[]{:S(2)}) copy-start(s32[512,512]{1,0:T(8,128)} %wet.9) | copy-start | bytes 3145732
  1.8 10.0 %copy-start.1 = (f32[3,512,512]{2,1,0:T(8,128)S(1)}, f32[3,512,512]{2,1,0:T(8,128)}, u32[]{:S(2)}) copy-start(f32[3,512,512]{2,1,0:T(8,128)} %ocean.3) | copy-start | bytes 9437188
  1.9 10.0 %copy-start.13 = (f32[180,4,90]{2,1,0:T(4,128)S(1)}, f32[180,4,90]{2,1,0:T(4,128)}, u32[]{:S(2)}) copy-start(f32[180,4,90]{2,1,0:T(4,128)} %lift.1) | copy-start | bytes 777604
  1.9 10.0 %copy-start.14 = (f32[180,180]{1,0:T(8,128)S(1)}, f32[180,180]{1,0:T(8,128)}, u32[]{:S(2)}) copy-start(f32[180,180]{1,0:T(8,128)} %volume.1) | copy-start | bytes 388804
  1.9 10.0 %copy-start.15 = (f32[90,90]{1,0:T(8,128)S(1)}, f32[90,90]{1,0:T(8,128)}, u32[]{:S(2)}) copy-start(f32[90,90]{1,0:T(8,128)} %flux.1) | copy-start | bytes 97204
  5.6 10.6 %collective-permute-start = (f32[512,128]{1,0:T(8,128)S(1)}, f32[512,128]{1,0:T(8,128)S(1)}, u32[]{:S(2)}, u32[]{:S(2)}) collective-permute-start(f32[512,128]{1,0:T(8,128)S(1)} %get-tuple-element.40), channel_id=1, source_target_pairs={{0,16},{1,2},{2,1},{3,4},{4,3},{5,6},{6,5},{7,8},{8,7},{9,10},{10,... | collective-permute-start | bytes 786440 | tf_op jit(solution)/shard_map/ppermute | solution.py:487
  9.9 7.8 %collective-permute-start.1 = (f32[512,128]{1,0:T(8,128)S(1)}, f32[512,128]{1,0:T(8,128)S(1)}, u32[]{:S(2)}, u32[]{:S(2)}) collective-permute-start(f32[512,128]{1,0:T(8,128)S(1)} %get-tuple-element.41), channel_id=1, source_target_pairs={{0,1},{1,0},{2,3},{3,2},{4,5},{5,4},{6,7},{7,6},{8,9},{9,8},{10,11... | collective-permute-start | bytes 786440 | tf_op jit(solution)/shard_map/ppermute | solution.py:488
  9.9 7.8 %collective-permute-start.2 = (f32[512,128]{1,0:T(8,128)S(1)}, f32[512,128]{1,0:T(8,128)S(1)}, u32[]{:S(2)}, u32[]{:S(2)}) collective-permute-start(f32[512,128]{1,0:T(8,128)S(1)} %get-tuple-element.42), channel_id=1, source_target_pairs={{0,112},{1,5},{2,6},{3,115},{4,116},{5,1},{6,2},{7,119},{8,120},{9... | collective-permute-start | bytes 786440 | tf_op jit(solution)/shard_map/ppermute | solution.py:489
  11.8 5.9 %copy-start.6 = (s32[4,1024]{1,0:T(4,128)S(1)}, s32[4,1024]{1,0:T(4,128)}, u32[]{:S(2)}) copy-start(s32[4,1024]{1,0:T(4,128)} %param.17) | copy-start | bytes 49156
  11.8 5.9 %copy-start.7 = (f32[1024]{0:T(1024)S(1)}, f32[1024]{0:T(1024)}, u32[]{:S(2)}) copy-start(f32[1024]{0:T(1024)} %param.19) | copy-start | bytes 12292
  11.8 5.8 %collective-permute-start.3 = (f32[512,128]{1,0:T(8,128)S(1)}, f32[512,128]{1,0:T(8,128)S(1)}, u32[]{:S(2)}, u32[]{:S(2)}) collective-permute-start(f32[512,128]{1,0:T(8,128)S(1)} %get-tuple-element.43), channel_id=1, source_target_pairs={{0,16},{1,17},{2,18},{3,19},{4,20},{5,21},{6,22},{7,23},{8,24},{9,... | collective-permute-start | bytes 786440 | tf_op jit(solution)/shard_map/ppermute | solution.py:490
  17.7 11.3 %copy-start.2 = (f32[512,512]{1,0:T(8,128)S(1)}, f32[512,512]{1,0:T(8,128)}, u32[]{:S(2)}) copy-start(f32[512,512]{1,0:T(8,128)} %depth.3) | copy-start | bytes 3145732
  17.7 11.3 %copy-start.9 = (s32[256]{0:T(256)S(1)}, s32[256]{0:T(256)}, u32[]{:S(2)}) copy-start(s32[256]{0:T(256)} %param.24) | copy-start | bytes 3076
  17.7 11.3 %copy-start.12 = (s32[256,1]{0,1:T(1,128)S(1)}, s32[256,1]{0,1:T(1,128)}, u32[]{:S(2)}) copy-start(s32[256,1]{0,1:T(1,128)} %param.25) | copy-start | bytes 3076
  24.9 9.6 %copy-start.5 = (f32[16,10,256]{2,0,1:T(8,128)S(1)}, f32[16,10,256]{2,0,1:T(8,128)}, u32[]{:S(2)}) copy-start(f32[16,10,256]{2,0,1:T(8,128)} %param.28) | copy-start | bytes 491524
  24.9 9.6 %copy-start.10 = (s32[256]{0:T(256)S(1)}, s32[256]{0:T(256)}, u32[]{:S(2)}) copy-start(s32[256]{0:T(256)} %param.26) | copy-start | bytes 3076
  24.9 9.6 %copy-start.11 = (s32[256]{0:T(256)S(1)}, s32[256]{0:T(256)}, u32[]{:S(2)}) copy-start(s32[256]{0:T(256)} %param.27) | copy-start | bytes 3076
  24.9 9.2 %collective-permute-start.4 = (f32[528,128]{1,0:T(8,128)S(1)}, f32[528,128]{1,0:T(8,128)S(1)}, u32[]{:S(2)}, u32[]{:S(2)}) collective-permute-start(f32[528,128]{1,0:T(8,128)S(1)} %get-tuple-element.48), channel_id=1, source_target_pairs={{0,16},{1,2},{2,1},{3,4},{4,3},{5,6},{6,5},{7,8},{8,7},{9,10},{10,... | collective-permute-start | bytes 811016 | tf_op jit(solution)/shard_map/ppermute | solution.py:487
  27.4 7.1 %collective-permute-start.5 = (f32[528,128]{1,0:T(8,128)S(1)}, f32[528,128]{1,0:T(8,128)S(1)}, u32[]{:S(2)}, u32[]{:S(2)}) collective-permute-start(f32[528,128]{1,0:T(8,128)S(1)} %get-tuple-element.49), channel_id=1, source_target_pairs={{0,1},{1,0},{2,3},{3,2},{4,5},{5,4},{6,7},{7,6},{8,9},{9,8},{10,11... | collective-permute-start | bytes 811016 | tf_op jit(solution)/shard_map/ppermute | solution.py:488
  27.4 7.1 %collective-permute-start.6 = (f32[528,128]{1,0:T(8,128)S(1)}, f32[528,128]{1,0:T(8,128)S(1)}, u32[]{:S(2)}, u32[]{:S(2)}) collective-permute-start(f32[528,128]{1,0:T(8,128)S(1)} %get-tuple-element.50), channel_id=1, source_target_pairs={{0,112},{1,5},{2,6},{3,115},{4,116},{5,1},{6,2},{7,119},{8,120},{9... | collective-permute-start | bytes 811016 | tf_op jit(solution)/shard_map/ppermute | solution.py:489
  28.4 6.0 %collective-permute-start.7 = (f32[528,128]{1,0:T(8,128)S(1)}, f32[528,128]{1,0:T(8,128)S(1)}, u32[]{:S(2)}, u32[]{:S(2)}) collective-permute-start(f32[528,128]{1,0:T(8,128)S(1)} %get-tuple-element.51), channel_id=1, source_target_pairs={{0,16},{1,17},{2,18},{3,19},{4,20},{5,21},{6,22},{7,23},{8,24},{9,... | collective-permute-start | bytes 811016 | tf_op jit(solution)/shard_map/ppermute | solution.py:490
  40.0 3.9 %collective-permute-start.8 = (f32[24,256]{1,0:T(8,128)S(1)}, f32[24,256]{1,0:T(8,128)S(1)}, u32[]{:S(2)}, u32[]{:S(2)}) collective-permute-start(f32[24,256]{1,0:T(8,128)S(1)} %get-tuple-element.54), channel_id=1, source_target_pairs={{0,1},{1,0},{2,3},{3,2},{4,5},{5,4},{6,7},{7,6},{8,9},{9,8},{10,11... | collective-permute-start | bytes 73736 | tf_op jit(solution)/shard_map/ppermute | solution.py:553
  41.5 2.5 %collective-permute-start.9 = (f32[24,256]{1,0:T(8,128)S(1)}, f32[24,256]{1,0:T(8,128)S(1)}, u32[]{:S(2)}, u32[]{:S(2)}) collective-permute-start(f32[24,256]{1,0:T(8,128)S(1)} %get-tuple-element.55), channel_id=1, source_target_pairs={{0,16},{1,17},{2,18},{3,19},{4,20},{5,21},{6,22},{7,23},{8,24},{9,... | collective-permute-start | bytes 73736 | tf_op jit(solution)/shard_map/ppermute | solution.py:554
  43.9 6.1 %collective-permute-start.10 = (f32[72,128]{1,0:T(8,128)S(1)}, f32[72,128]{1,0:T(8,128)S(1)}, u32[]{:S(2)}, u32[]{:S(2)}) collective-permute-start(f32[72,128]{1,0:T(8,128)S(1)} %get-tuple-element.63), channel_id=1, source_target_pairs={{0,16},{1,2},{2,1},{3,4},{4,3},{5,6},{6,5},{7,8},{8,7},{9,10},{10,... | collective-permute-start | bytes 110600 | tf_op jit(solution)/shard_map/ppermute | solution.py:563
  46.4 4.0 %collective-permute-start.11 = (f32[80,128]{1,0:T(8,128)S(1)}, f32[80,128]{1,0:T(8,128)S(1)}, u32[]{:S(2)}, u32[]{:S(2)}) collective-permute-start(f32[80,128]{1,0:T(8,128)S(1)} %pad.4), channel_id=1, source_target_pairs={{0,1},{1,0},{2,3},{3,2},{4,5},{5,4},{6,7},{7,6},{8,9},{9,8},{10,11... | collective-permute-start | bytes 122888 | tf_op jit(solution)/shard_map/ppermute | solution.py:564

commit v5 on v4

--- a/solution.py
+++ b/solution.py
@@ -163,7 +163,10 @@
         copy.wait()
 
 
-def prepare_kernel(extract, volume, flux, lift, ocean, wet, v2k, l2k, ea, eb, ec, ed, v2, l2):
+def prepare_kernel(
+    extract, volume, flux, lift, ocean, wet, sf_face, sf_dest, v2k, l2k, ea, eb, ec, ed, pick, into, v2, l2
+):
+    place_faces(sf_face, sf_dest, pick, into)
     total = volume[...]
     fl = split(flux[...])
     l2[...] = jnp.zeros(l2.shape, F32)
@@ -347,14 +350,13 @@
     into[...] = (lax.broadcasted_iota(jnp.int32, (3 * GROUP, SF), 0) == place).astype(BF16)
 
 
-def stencil_kernel(ocean, wet, depth, sf_face, sf_dest, after, height, speeds, pick, into, fields):
-    place_faces(sf_face, sf_dest, pick, into)
+def stencil_kernel(ocean, wet, depth, after, height, speeds, fields):
     wet_f = wet[...].astype(F32)
     for f in range(3):
         fields[f, pl.ds(0, 8), :] = jnp.zeros((8, TILE), F32)
         fields[f, pl.ds(TILE + 8, 8), :] = jnp.zeros((8, TILE), F32)
         fields[f, pl.ds(8, TILE), :] = ocean[f] * wet_f
-    rows = 32
+    rows = 64
     lane = lax.broadcasted_iota(jnp.int32, (rows, TILE), 1)
 
     def step(i, carry):
@@ -519,12 +521,13 @@
         [padded] + [pltpu.VMEM(short, F32)] * 4 + [dma((4,))], aliases={3: 6}, flops=10**10,
     )(state, extract, send, blank)
     recv = exchange(sa, sb, sc, sd)
-    v2k, l2k, ea, eb, ec, ed = call(
-        prepare_kernel, "prepare", [VMEM] * 6,
+    v2k, l2k, ea, eb, ec, ed, pick, into = call(
+        prepare_kernel, "prepare", [VMEM] * 8,
         [((NQ, 3 * KP), BF16, VMEM), ((NQ, 12 * LANES), BF16, VMEM)]
-        + [((EDGE, LANES), F32, VMEM)] * 2 + [(short, F32, VMEM)] * 2,
+        + [((EDGE, LANES), F32, VMEM)] * 2 + [(short, F32, VMEM)] * 2
+        + [((ELEMS, SF), BF16, VMEM), ((3 * GROUP, SF), BF16, VMEM)],
         [pltpu.VMEM((NQ, KP), F32), pltpu.VMEM((NQ, 4 * LANES), F32)], flops=5 * 10**9,
-    )(extract, volume_op, flux_matrix, lift_op, ocean, wet)
+    )(extract, volume_op, flux_matrix, lift_op, ocean, wet, sf_face.reshape(1, SF), sf_dest.reshape(1, SF))
     state, table, sd, sc, sb, sa = call(
         middle_kernel, "step_first", [VMEM] * 9 + [SMEM] * 2 + [VMEM] + [ANY] * 4,
         [((NQ, ELEMS), F32, VMEM), table_o] + [(tall, F32, ANY)] * 4,
@@ -532,14 +535,13 @@
         aliases={11: 1},
     )(state, jac, ek, v2k, l2k, ea, eb, ec, ed, nbr, send, table, *recv)
     recv = exchange(sa, sb, sc, sd)
-    height, speeds, pick, into = call(
-        stencil_kernel, "stencil", [VMEM] * 6,
+    height, speeds = call(
+        stencil_kernel, "stencil", [VMEM] * 4,
         [
             ((TILE, TILE), F32, VMEM), ((2, TILE, TILE), F32, VMEM),
-            ((ELEMS, SF), BF16, VMEM), ((3 * GROUP, SF), BF16, VMEM),
         ],
         [pltpu.VMEM((3, TILE + 16, TILE), F32)], flops=10**9,
-    )(ocean, wet, depth, sf_face.reshape(1, SF), sf_dest.reshape(1, SF), state[:8, :LANES])
+    )(ocean, wet, depth, state[:8, :LANES])
     box_o = ((24, GROUP), F32, VMEM)
     state, _, stay, box_a, box_b = call(
         last_kernel, "step_last", [VMEM] * 5 + [SMEM] + [VMEM] * 7 + [ANY] * 4,

time: 54 us -> 54.1 us (level)
  transfers between devices with their start and end apart: 12 -> 12, of which waited for: 7 -> 7; matrix products, arithmetic and copies ran while one was open for 0% -> 0% of each run, Pallas kernels for 19% -> 18%
where the time goes in v5:
time: 54.1 us; the launch traced here: 53.9 us
  Pallas kernels  29.4 us (54%)
  starting transfers between devices  14.4 us (27%)
  waiting for transfers between devices  7.84 us (14%)
  local copies, waits for them, and re-layouts  1.25 us (2%)
  between operations  1.06 us (2%)
    pallas_call x1, Pallas kernels, body(): call(middle_kernel, 'step_first', [VMEM] * 9 + [SMEM] * 2 + [VMEM] + [ANY...  7.17 us
    ppermute x2, starting transfers between devices, exchange(): d = lax.ppermute(d, BOTH, PAIR_D)  6.78 us
    pallas_call x1, Pallas kernels, body(): call(last_kernel, 'step_last', [VMEM] * 5 + [SMEM] + [VMEM] * 7 + [ANY] *...  5.5 us
    pallas_call x1, Pallas kernels, body(): call(first_kernel, 'traces_first', [VMEM, VMEM, SMEM, VMEM], [table_o, ((...  3.7 us
    pallas_call x1, Pallas kernels, body(): call(stencil_kernel, 'stencil', [VMEM] * 4, [((TILE, TILE), F32, VMEM), (...  3.56 us
    pallas_call x1, Pallas kernels, body(): call(uplift_far_kernel, 'uplift_far', [VMEM] * 4 + [ANY], [((3, TILE, TIL...  3.35 us
    pallas_call x1, Pallas kernels, body(): call(prepare_kernel, 'prepare', [VMEM] * 8, [((NQ, 3 * KP), BF16, VMEM),...  3.31 us
    ppermute x2, starting transfers between devices, exchange(): b = lax.ppermute(b, BOTH, PAIR_B)  2.93 us
  transfers between devices with their start and end apart: 12, of which 7 were waited for; matrix products, arithmetic and copies ran while one was open for 0% of the time, Pallas kernels for 18%

profile of v5, /device:TPU:24, one launch (start us, length us, event | category | flops | bytes accessed | tf_op | source)
XLA Modules:
  0.0 53.9 jit_solution(3663307102769793716)
XLA Ops:
  0.6 0.0 copy-start.3
  0.6 0.0 copy-start.4
  0.6 0.0 copy-start.8
  0.7 1.0 %copy-done.3 = f32[180,1024]{1,0:T(8,128)S(1)} copy-done((f32[180,1024]{1,0:T(8,128)S(1)}, f32[180,1024]{1,0:T(8,128)}, u32[]{:S(2)}) %copy-start.3) | copy-done | bytes 737304
  1.8 0.1 copy-done.4
  1.8 0.0 copy-done.8
  1.8 0.0 copy-start
  1.8 0.0 copy-start.1
  1.9 0.0 copy-start.9
  1.9 0.0 copy-start.12
  1.9 0.0 copy-start.13
  1.9 0.0 copy-start.14
  1.9 0.0 copy-start.15
  1.9 3.7 %traces_first.1 = (f32[6144,128]{1,0:T(8,128)S(1)}, bf16[512,768]{1,0:T(8,128)(2,1)S(1)}, f32[512,128]{1,0:T(8,128)S(1)}, f32[512,128]{1,0:T(8,128)S(1)}, f32[51...) custom-call(f32[180,1024]{1,0:T(8,128)S(1)} %copy-done.3, ...), custom_call_target="tpu_custom_call", output_to_operand_aliasing={{6}: (3, {})} | custom-call | flops 10000000000 | bytes 2097152 | tf_op jit(solution)/shard_map/traces_first/pallas_call | solution.py:518
  5.6 4.3 %collective-permute-start = (f32[512,128]{1,0:T(8,128)S(1)}, f32[512,128]{1,0:T(8,128)S(1)}, u32[]{:S(2)}, u32[]{:S(2)}) collective-permute-start(f32[512,128]{1,0:T(8,128)S(1)} %get-tuple-element.40), channel_id=1, source_target_pairs={{0,16},{1,2},{2,1},{3,4},{4,3},{5,6},{6,5},{7,8},{8,7},{9,10},{10,... | collective-permute-start | bytes 786440 | tf_op jit(solution)/shard_map/ppermute | solution.py:489
  9.9 0.0 collective-permute-start.1
  9.9 1.9 %collective-permute-start.2 = (f32[512,128]{1,0:T(8,128)S(1)}, f32[512,128]{1,0:T(8,128)S(1)}, u32[]{:S(2)}, u32[]{:S(2)}) collective-permute-start(f32[512,128]{1,0:T(8,128)S(1)} %get-tuple-element.42), channel_id=1, source_target_pairs={{0,112},{1,5},{2,6},{3,115},{4,116},{5,1},{6,2},{7,119},{8,120},{9... | collective-permute-start | bytes 786440 | tf_op jit(solution)/shard_map/ppermute | solution.py:491
  11.8 0.0 collective-permute-start.3
  11.8 0.0 copy-done
  11.8 0.0 copy-done.1
  11.8 0.0 copy-done.9
  11.9 0.0 copy-done.12
  11.9 0.0 copy-done.13
  11.9 0.0 copy-done.14
  11.9 0.0 copy-done.15
  11.9 0.0 copy-start.6
  11.9 0.0 copy-start.7
  11.9 3.3 %prepare.1 = (bf16[180,768]{1,0:T(8,128)(2,1)S(1)}, bf16[180,1536]{1,0:T(8,128)(2,1)S(1)}, f32[16,128]{1,0:T(8,128)S(1)}, f32[16,128]{1,0:T(8,128)S(1)}, f32[512...) custom-call(f32[90,4,180]{2,1,0:T(4,128)S(1)} %bitcast.18, ...), custom_call_target="tpu_custom_call" | custom-call | flops 5000000000 | bytes 2097152 | tf_op jit(solution)/shard_map/prepare/pallas_call | solution.py:524
  15.2 1.0 %collective-permute-done.in_d = f32[512,128]{1,0:T(8,128)S(1)} collective-permute-done((f32[512,128]{1,0:T(8,128)S(1)}, f32[512,128]{1,0:T(8,128)S(1)}, u32[]{:S(2)}, u32[]{:S(2)}) %collective-permute-start) | collective-permute-done | bytes 262176 | tf_op jit(solution)/shard_map/ppermute | solution.py:489
  16.2 1.5 %collective-permute-done.1.in_c = f32[512,128]{1,0:T(8,128)S(1)} collective-permute-done((f32[512,128]{1,0:T(8,128)S(1)}, f32[512,128]{1,0:T(8,128)S(1)}, u32[]{:S(2)}, u32[]{:S(2)}) %collective-permute-start.1) | collective-permute-done | bytes 262176 | tf_op jit(solution)/shard_map/ppermute | solution.py:490
  17.7 0.0 collective-permute-done.2.in_b
  17.7 0.0 collective-permute-done.3.in_a
  17.7 0.0 copy-done.6
  17.7 0.0 copy-done.7
  17.7 0.0 copy-start.2
  17.7 7.2 %step_first.1 = (f32[180,1024]{1,0:T(8,128)S(1)}, f32[6144,128]{1,0:T(8,128)S(1)}, f32[528,128]{1,0:T(8,128)S(1)}, f32[528,128]{1,0:T(8,128)S(1)}, f32[528,128]{1,0:T(8,128)S(1)}, /*index=5*/f32[528,128]{1,0:T(8,128)S(1)}) custom-call(f32[180,1024]{1,0:T(8,128)S(1)} %copy-done.3, f32[1,1024]{1,0:T(1,128)S(1)} %bitcast.23, ...), custom_call_target="tpu_custom_call", output_to_operand_aliasing={{1}: (11, {})} | custom-call | bytes 2097152 | tf_op jit(solution)/shard_map/step_first/pallas_call | solution.py:531
  24.9 0.0 copy-start.5
  24.9 0.0 copy-start.10
  24.9 0.0 copy-start.11
  24.9 2.5 %collective-permute-start.4 = (f32[528,128]{1,0:T(8,128)S(1)}, f32[528,128]{1,0:T(8,128)S(1)}, u32[]{:S(2)}, u32[]{:S(2)}) collective-permute-start(f32[528,128]{1,0:T(8,128)S(1)} %get-tuple-element.48), channel_id=1, source_target_pairs={{0,16},{1,2},{2,1},{3,4},{4,3},{5,6},{6,5},{7,8},{8,7},{9,10},{10,... | collective-permute-start | bytes 811016 | tf_op jit(solution)/shard_map/ppermute | solution.py:489
  27.4 0.0 collective-permute-start.5
  27.4 1.0 %collective-permute-start.6 = (f32[528,128]{1,0:T(8,128)S(1)}, f32[528,128]{1,0:T(8,128)S(1)}, u32[]{:S(2)}, u32[]{:S(2)}) collective-permute-start(f32[528,128]{1,0:T(8,128)S(1)} %get-tuple-element.50), channel_id=1, source_target_pairs={{0,112},{1,5},{2,6},{3,115},{4,116},{5,1},{6,2},{7,119},{8,120},{9... | collective-permute-start | bytes 811016 | tf_op jit(solution)/shard_map/ppermute | solution.py:491
  28.4 0.6 %collective-permute-start.7 = (f32[528,128]{1,0:T(8,128)S(1)}, f32[528,128]{1,0:T(8,128)S(1)}, u32[]{:S(2)}, u32[]{:S(2)}) collective-permute-start(f32[528,128]{1,0:T(8,128)S(1)} %get-tuple-element.51), channel_id=1, source_target_pairs={{0,16},{1,17},{2,18},{3,19},{4,20},{5,21},{6,22},{7,23},{8,24},{9,... | collective-permute-start | bytes 811016 | tf_op jit(solution)/shard_map/ppermute | solution.py:492
  29.0 0.0 copy-done.2
  29.0 3.6 %stencil.1 = (f32[512,512]{1,0:T(8,128)S(1)}, f32[2,512,512]{2,1,0:T(8,128)S(1)}) custom-call(f32[3,512,512]{2,1,0:T(8,128)S(1)} %copy-done.1, s32[512,512]{1,0:T(8,128)S(1)} %copy-done, f32[512,512]{1,0:T(8,128)S(1)} %copy-done.2, f32[8,128]{1,0:T(8,128)S(1)} %slice.11.after), custom_call_target="tpu_custom_call" | custom-call | flops 1000000000 | bytes 2097152 | tf_op jit(solution)/shard_map/stencil/pallas_call | solution.py:538
  32.6 1.6 %collective-permute-done.4.in_d = f32[528,128]{1,0:T(8,128)S(1)} collective-permute-done((f32[528,128]{1,0:T(8,128)S(1)}, f32[528,128]{1,0:T(8,128)S(1)}, u32[]{:S(2)}, u32[]{:S(2)}) %collective-permute-start.4) | collective-permute-done | bytes 270368 | tf_op jit(solution)/shard_map/ppermute | solution.py:489
  34.2 0.3 collective-permute-done.5.in_c
  34.5 0.0 collective-permute-done.6.in_b
  34.5 0.0 collective-permute-done.7.in_a
  34.5 0.0 copy-done.5
  34.5 0.0 copy-done.10
  34.5 0.0 copy-done.11
  34.5 5.5 %step_last.1 = (f32[180,1024]{1,0:T(8,128)}, f32[6144,128]{1,0:T(8,128)S(1)}, f32[24,256]{1,0:T(8,128)S(1)}, f32[24,256]{1,0:T(8,128)S(1)}, f32[24,256]{1,0:T(8,128)S(1)}) custom-call(f32[180,1024]{1,0:T(8,128)S(1)} %get-tuple-element.44.state, f32[1,1024]{1,0:T(1,128)S(1)} %bitcast.24, ...), custom_call_target="tpu_custom_call", output_to_operand_aliasing={{1}: (12, {})} | custom-call | bytes 2097152 | tf_op jit(solution)/shard_map/step_last/pallas_call | solution.py:546
  40.0 1.5 %collective-permute-start.8 = (f32[24,256]{1,0:T(8,128)S(1)}, f32[24,256]{1,0:T(8,128)S(1)}, u32[]{:S(2)}, u32[]{:S(2)}) collective-permute-start(f32[24,256]{1,0:T(8,128)S(1)} %get-tuple-element.54), channel_id=1, source_target_pairs={{0,1},{1,0},{2,3},{3,2},{4,5},{5,4},{6,7},{7,6},{8,9},{9,8},{10,11... | collective-permute-start | bytes 73736 | tf_op jit(solution)/shard_map/ppermute | solution.py:555
  41.5 0.2 collective-permute-start.9
  41.7 1.5 %finish_edges.1 = (f32[512,512]{1,0:T(8,128)S(1)}, f32[2,512,512]{2,1,0:T(8,128)S(1)}) custom-call(f32[24,256]{1,0:T(8,128)S(1)} %get-tuple-element.53.stay, s32[512,512]{1,0:T(8,128)S(1)} %copy-done, f32[512,512]{1,0:T(8,128)S(1)} %copy-done.2, f32[512,512]{1,0:T(8,128)S(1)} %get-tuple-element.56.height_in, ...), custom_call_target="tpu_custom_call", output_to_operand_aliasing={{0}: (3, {}), {1}: (4, {})} | custom-call | flops 2000000000 | bytes 2097152 | tf_op jit(solution)/shard_map/finish_edges/pallas_call | solution.py:558
  43.2 0.8 %collective-permute-done.8.got_b = f32[24,256]{1,0:T(8,128)S(1)} collective-permute-done((f32[24,256]{1,0:T(8,128)S(1)}, f32[24,256]{1,0:T(8,128)S(1)}, u32[]{:S(2)}, u32[]{:S(2)}) %collective-permute-start.8) | collective-permute-done | bytes 24608 | tf_op jit(solution)/shard_map/ppermute | solution.py:555
  44.0 0.0 collective-permute-done.9.got_a
  44.0 2.4 %collective-permute-start.10 = (f32[72,128]{1,0:T(8,128)S(1)}, f32[72,128]{1,0:T(8,128)S(1)}, u32[]{:S(2)}, u32[]{:S(2)}) collective-permute-start(f32[72,128]{1,0:T(8,128)S(1)} %get-tuple-element.63), channel_id=1, source_target_pairs={{0,16},{1,2},{2,1},{3,4},{4,3},{5,6},{6,5},{7,8},{8,7},{9,10},{10,... | collective-permute-start | bytes 110600 | tf_op jit(solution)/shard_map/ppermute | solution.py:565
  46.4 0.0 collective-permute-start.11
  46.4 1.3 %uplift_own.1 = (f32[512,512]{1,0:T(8,128)S(1)}, f32[3,512,512]{2,1,0:T(8,128)}) custom-call(f32[24,256]{1,0:T(8,128)S(1)} %collective-permute-done.8.got_b, f32[24,256]{1,0:T(8,128)S(1)} %collective-permute-done.9.got_a, s32[512,512]{1,0:T(8,128)S(1)} %copy-done, f32[512,512]{1,0:T(8,128)S(1)} %get-tuple-element.58.height_in, ...), custom_call_target="tpu_custom_call", output_to_operand_aliasing={{0}: (3, {})} | custom-call | flops 1000000000 | bytes 2097152 | tf_op jit(solution)/shard_map/uplift_own/pallas_call | solution.py:567
  47.8 2.4 %collective-permute-done.10.got_d = f32[72,128]{1,0:T(8,128)S(1)} collective-permute-done((f32[72,128]{1,0:T(8,128)S(1)}, f32[72,128]{1,0:T(8,128)S(1)}, u32[]{:S(2)}, u32[]{:S(2)}) %collective-permute-start.10) | collective-permute-done | bytes 36896 | tf_op jit(solution)/shard_map/ppermute | solution.py:565
  50.1 0.3 collective-permute-done.11.got_c
  50.4 3.3 %uplift_far.1 = f32[3,512,512]{2,1,0:T(8,128)} custom-call(f32[72,128]{1,0:T(8,128)S(1)} %collective-permute-done.10.got_d, f32[80,128]{1,0:T(8,128)S(1)} %collective-permute-done.11.got_c, s32[512,512]{1,0:T(8,128)S(1)} %copy-done, f32[512,512]{1,0:T(8,128)S(1)} %get-tuple-element.60.height, ...), custom_call_target="tpu_custom_call", output_to_operand_aliasing={{}: (4, {})} | custom-call | flops 3000000000 | bytes 2097152 | tf_op jit(solution)/shard_map/uplift_far/pallas_call | solution.py:571
  (7 shorter events, 0.1 us)
Async XLA Ops:
  0.6 1.1 %copy-start.3 = (f32[180,1024]{1,0:T(8,128)S(1)}, f32[180,1024]{1,0:T(8,128)}, u32[]{:S(2)}) copy-start(f32[180,1024]{1,0:T(8,128)} %state.3) | copy-start | bytes 2211844
  0.6 1.2 %copy-start.4 = (f32[4,90,180]{2,0,1:T(4,128)S(1)}, f32[4,90,180]{2,0,1:T(4,128)}, u32[]{:S(2)}) copy-start(f32[4,90,180]{2,0,1:T(4,128)} %param.20) | copy-start | bytes 777604
  0.6 1.2 %copy-start.8 = (s32[4,512]{1,0:T(4,128)S(1)}, s32[4,512]{1,0:T(4,128)}, u32[]{:S(2)}) copy-start(s32[4,512]{1,0:T(4,128)} %param.18) | copy-start | bytes 24580
  1.8 10.0 %copy-start = (s32[512,512]{1,0:T(8,128)S(1)}, s32[512,512]{1,0:T(8,128)}, u32[]{:S(2)}) copy-start(s32[512,512]{1,0:T(8,128)} %wet.9) | copy-start | bytes 3145732
  1.8 10.0 %copy-start.1 = (f32[3,512,512]{2,1,0:T(8,128)S(1)}, f32[3,512,512]{2,1,0:T(8,128)}, u32[]{:S(2)}) copy-start(f32[3,512,512]{2,1,0:T(8,128)} %ocean.3) | copy-start | bytes 9437188
  1.9 10.0 %copy-start.9 = (s32[256]{0:T(256)S(1)}, s32[256]{0:T(256)}, u32[]{:S(2)}) copy-start(s32[256]{0:T(256)} %param.24) | copy-start | bytes 3076
  1.9 10.0 %copy-start.12 = (f32[180,4,90]{2,1,0:T(4,128)S(1)}, f32[180,4,90]{2,1,0:T(4,128)}, u32[]{:S(2)}) copy-start(f32[180,4,90]{2,1,0:T(4,128)} %lift.1) | copy-start | bytes 777604
  1.9 10.0 %copy-start.13 = (f32[180,180]{1,0:T(8,128)S(1)}, f32[180,180]{1,0:T(8,128)}, u32[]{:S(2)}) copy-start(f32[180,180]{1,0:T(8,128)} %volume.1) | copy-start | bytes 388804
  1.9 10.0 %copy-start.14 = (f32[90,90]{1,0:T(8,128)S(1)}, f32[90,90]{1,0:T(8,128)}, u32[]{:S(2)}) copy-start(f32[90,90]{1,0:T(8,128)} %flux.1) | copy-start | bytes 97204
  1.9 10.0 %copy-start.15 = (s32[256,1]{0,1:T(1,128)S(1)}, s32[256,1]{0,1:T(1,128)}, u32[]{:S(2)}) copy-start(s32[256,1]{0,1:T(1,128)} %param.25) | copy-start | bytes 3076
  5.6 10.6 %collective-permute-start = (f32[512,128]{1,0:T(8,128)S(1)}, f32[512,128]{1,0:T(8,128)S(1)}, u32[]{:S(2)}, u32[]{:S(2)}) collective-permute-start(f32[512,128]{1,0:T(8,128)S(1)} %get-tuple-element.40), channel_id=1, source_target_pairs={{0,16},{1,2},{2,1},{3,4},{4,3},{5,6},{6,5},{7,8},{8,7},{9,10},{10,... | collective-permute-start | bytes 786440 | tf_op jit(solution)/shard_map/ppermute | solution.py:489
  9.9 7.8 %collective-permute-start.1 = (f32[512,128]{1,0:T(8,128)S(1)}, f32[512,128]{1,0:T(8,128)S(1)}, u32[]{:S(2)}, u32[]{:S(2)}) collective-permute-start(f32[512,128]{1,0:T(8,128)S(1)} %get-tuple-element.41), channel_id=1, source_target_pairs={{0,1},{1,0},{2,3},{3,2},{4,5},{5,4},{6,7},{7,6},{8,9},{9,8},{10,11... | collective-permute-start | bytes 786440 | tf_op jit(solution)/shard_map/ppermute | solution.py:490
  9.9 7.8 %collective-permute-start.2 = (f32[512,128]{1,0:T(8,128)S(1)}, f32[512,128]{1,0:T(8,128)S(1)}, u32[]{:S(2)}, u32[]{:S(2)}) collective-permute-start(f32[512,128]{1,0:T(8,128)S(1)} %get-tuple-element.42), channel_id=1, source_target_pairs={{0,112},{1,5},{2,6},{3,115},{4,116},{5,1},{6,2},{7,119},{8,120},{9... | collective-permute-start | bytes 786440 | tf_op jit(solution)/shard_map/ppermute | solution.py:491
  11.8 5.9 %collective-permute-start.3 = (f32[512,128]{1,0:T(8,128)S(1)}, f32[512,128]{1,0:T(8,128)S(1)}, u32[]{:S(2)}, u32[]{:S(2)}) collective-permute-start(f32[512,128]{1,0:T(8,128)S(1)} %get-tuple-element.43), channel_id=1, source_target_pairs={{0,16},{1,17},{2,18},{3,19},{4,20},{5,21},{6,22},{7,23},{8,24},{9,... | collective-permute-start | bytes 786440 | tf_op jit(solution)/shard_map/ppermute | solution.py:492
  11.9 5.8 %copy-start.6 = (s32[4,1024]{1,0:T(4,128)S(1)}, s32[4,1024]{1,0:T(4,128)}, u32[]{:S(2)}) copy-start(s32[4,1024]{1,0:T(4,128)} %param.17) | copy-start | bytes 49156
  11.9 5.8 %copy-start.7 = (f32[1024]{0:T(1024)S(1)}, f32[1024]{0:T(1024)}, u32[]{:S(2)}) copy-start(f32[1024]{0:T(1024)} %param.19) | copy-start | bytes 12292
  17.7 11.3 %copy-start.2 = (f32[512,512]{1,0:T(8,128)S(1)}, f32[512,512]{1,0:T(8,128)}, u32[]{:S(2)}) copy-start(f32[512,512]{1,0:T(8,128)} %depth.3) | copy-start | bytes 3145732
  24.9 9.6 %copy-start.5 = (f32[16,10,256]{2,0,1:T(8,128)S(1)}, f32[16,10,256]{2,0,1:T(8,128)}, u32[]{:S(2)}) copy-start(f32[16,10,256]{2,0,1:T(8,128)} %param.28) | copy-start | bytes 491524
  24.9 9.6 %copy-start.10 = (s32[256]{0:T(256)S(1)}, s32[256]{0:T(256)}, u32[]{:S(2)}) copy-start(s32[256]{0:T(256)} %param.26) | copy-start | bytes 3076
  24.9 9.6 %copy-start.11 = (s32[256]{0:T(256)S(1)}, s32[256]{0:T(256)}, u32[]{:S(2)}) copy-start(s32[256]{0:T(256)} %param.27) | copy-start | bytes 3076
  24.9 9.2 %collective-permute-start.4 = (f32[528,128]{1,0:T(8,128)S(1)}, f32[528,128]{1,0:T(8,128)S(1)}, u32[]{:S(2)}, u32[]{:S(2)}) collective-permute-start(f32[528,128]{1,0:T(8,128)S(1)} %get-tuple-element.48), channel_id=1, source_target_pairs={{0,16},{1,2},{2,1},{3,4},{4,3},{5,6},{6,5},{7,8},{8,7},{9,10},{10,... | collective-permute-start | bytes 811016 | tf_op jit(solution)/shard_map/ppermute | solution.py:489
  27.4 7.1 %collective-permute-start.5 = (f32[528,128]{1,0:T(8,128)S(1)}, f32[528,128]{1,0:T(8,128)S(1)}, u32[]{:S(2)}, u32[]{:S(2)}) collective-permute-start(f32[528,128]{1,0:T(8,128)S(1)} %get-tuple-element.49), channel_id=1, source_target_pairs={{0,1},{1,0},{2,3},{3,2},{4,5},{5,4},{6,7},{7,6},{8,9},{9,8},{10,11... | collective-permute-start | bytes 811016 | tf_op jit(solution)/shard_map/ppermute | solution.py:490
  27.4 7.1 %collective-permute-start.6 = (f32[528,128]{1,0:T(8,128)S(1)}, f32[528,128]{1,0:T(8,128)S(1)}, u32[]{:S(2)}, u32[]{:S(2)}) collective-permute-start(f32[528,128]{1,0:T(8,128)S(1)} %get-tuple-element.50), channel_id=1, source_target_pairs={{0,112},{1,5},{2,6},{3,115},{4,116},{5,1},{6,2},{7,119},{8,120},{9... | collective-permute-start | bytes 811016 | tf_op jit(solution)/shard_map/ppermute | solution.py:491
  28.4 6.1 %collective-permute-start.7 = (f32[528,128]{1,0:T(8,128)S(1)}, f32[528,128]{1,0:T(8,128)S(1)}, u32[]{:S(2)}, u32[]{:S(2)}) collective-permute-start(f32[528,128]{1,0:T(8,128)S(1)} %get-tuple-element.51), channel_id=1, source_target_pairs={{0,16},{1,17},{2,18},{3,19},{4,20},{5,21},{6,22},{7,23},{8,24},{9,... | collective-permute-start | bytes 811016 | tf_op jit(solution)/shard_map/ppermute | solution.py:492
  40.0 3.9 %collective-permute-start.8 = (f32[24,256]{1,0:T(8,128)S(1)}, f32[24,256]{1,0:T(8,128)S(1)}, u32[]{:S(2)}, u32[]{:S(2)}) collective-permute-start(f32[24,256]{1,0:T(8,128)S(1)} %get-tuple-element.54), channel_id=1, source_target_pairs={{0,1},{1,0},{2,3},{3,2},{4,5},{5,4},{6,7},{7,6},{8,9},{9,8},{10,11... | collective-permute-start | bytes 73736 | tf_op jit(solution)/shard_map/ppermute | solution.py:555
  41.5 2.4 %collective-permute-start.9 = (f32[24,256]{1,0:T(8,128)S(1)}, f32[24,256]{1,0:T(8,128)S(1)}, u32[]{:S(2)}, u32[]{:S(2)}) collective-permute-start(f32[24,256]{1,0:T(8,128)S(1)} %get-tuple-element.55), channel_id=1, source_target_pairs={{0,16},{1,17},{2,18},{3,19},{4,20},{5,21},{6,22},{7,23},{8,24},{9,... | collective-permute-start | bytes 73736 | tf_op jit(solution)/shard_map/ppermute | solution.py:556
  44.0 6.1 %collective-permute-start.10 = (f32[72,128]{1,0:T(8,128)S(1)}, f32[72,128]{1,0:T(8,128)S(1)}, u32[]{:S(2)}, u32[]{:S(2)}) collective-permute-start(f32[72,128]{1,0:T(8,128)S(1)} %get-tuple-element.63), channel_id=1, source_target_pairs={{0,16},{1,2},{2,1},{3,4},{4,3},{5,6},{6,5},{7,8},{8,7},{9,10},{10,... | collective-permute-start | bytes 110600 | tf_op jit(solution)/shard_map/ppermute | solution.py:565
  46.4 4.0 %collective-permute-start.11 = (f32[80,128]{1,0:T(8,128)S(1)}, f32[80,128]{1,0:T(8,128)S(1)}, u32[]{:S(2)}, u32[]{:S(2)}) collective-permute-start(f32[80,128]{1,0:T(8,128)S(1)} %pad.4), channel_id=1, source_target_pairs={{0,1},{1,0},{2,3},{3,2},{4,5},{5,4},{6,7},{7,6},{8,9},{9,8},{10,11... | collective-permute-start | bytes 122888 | tf_op jit(solution)/shard_map/ppermute | solution.py:566
